TPU v7x, 128 devices: a whole 4x4x4 slice. The times are simulated.
128 devices in a mesh: ctx: 16 (over x, y), exp: 8 (over z, core).
Axes of the slice: x: 4, y: 4, z: 4, core: 2. Of those that a mesh axis runs over, the one named last changes fastest.
Arguments:
- mixer_in: bfloat16 [2048, 8192], P('ctx', 'exp'), may hold values from -6 to 6
- gate_in: bfloat16 [2048, 8192], P('ctx', 'exp'), may hold values from -6 to 6
- conv_weight: float32 [4, 8192], P(None, 'exp'), may hold values from -3 to 3
- conv_bias: float32 [8192], P('exp'), may hold values from -3 to 3
- x_proj: bfloat16 [8192, 544], P('exp'), may hold values from -0.03125 to 0.03125
- dt_proj: bfloat16 [512, 8192], P(None, 'exp'), may hold values from -0.25 to 0.25
- dt_bias: float32 [8192], P('exp'), may hold values from -1.5 to 0.5
- decay_rate: float32 [16, 8192], P(None, 'exp'), may hold values from 9.765625e-05 to 0.1
- skip: float32 [8192], P('exp'), may hold values from 0.5 to 1.5
- out_proj: bfloat16 [8192, 4096], P('exp', 'ctx'), may hold values from -0.015625 to 0.015625
- residual: bfloat16 [2048, 4096], P(('ctx', 'exp')), may hold values from -6 to 6
- gain: float32 [4096], replicated, may hold values from 0.5 to 1.5
- router: bfloat16 [4096, 8], replicated, may hold values from -0.09375 to 0.09375
- w_gate: bfloat16 [8, 4096, 12288], P('exp', None, 'ctx'), may hold values from -0.09375 to 0.09375
- w_up: bfloat16 [8, 4096, 12288], P('exp', None, 'ctx'), may hold values from -0.09375 to 0.09375
- w_down: bfloat16 [8, 12288, 4096], P('exp', 'ctx'), may hold values from -0.0546875 to 0.0546875
- expert_ids: int32 [2048, 2], P(('ctx', 'exp')), may hold values from 0 to 7, all different within a row; in each aligned block of 16 rows (0 to 15, 16 to 31, ...) at most 5 rows name the same one
Outputs:
- block_out: bfloat16 [2048, 4096], P(('ctx', 'exp'))
Inputs may be any that keep to these rules, and one draw needn't show every extreme that they name: `expert_ids`: the two ids of a token differ. In each aligned block of 16 tokens no expert is named more than 5 times.
All inputs are finite; a program needn't handle non-finite values.
Results may differ from a plain program's by a relative error of at most 0.007.
Values may be sent and summed in bfloat16 or wider, within the bound.
A program may use at most 128 MiB of HBM per device.

v0:
```python
import jax
import jax.numpy as jnp
from jax import lax
from jax.sharding import PartitionSpec as P


def from_behind(value, axis, steps):
    count = lax.axis_size(axis)
    first, last = (max(0, -steps), min(count, count - steps))
    return lax.ppermute(value, axis, [(source, source + steps) for source in range(first, last)])


def entering_2(part, axis, combine, identity):
    place = lax.axis_index(axis)
    gathered = jax.tree.map(lambda a: lax.all_gather(a, axis), part)
    state = jax.tree.map(lambda a, e: jnp.zeros_like(a) + jnp.asarray(e, a.dtype), part, identity)

    def one(lap, state):
        return combine(
            state, jax.tree.map(lambda a: lax.dynamic_index_in_dim(a, lap, 0, False), gathered)
        )

    return lax.fori_loop(0, place, one, state)


def link_pairs(earlier, later):
    return (earlier[0] * later[0], later[0] * earlier[1] + later[1])


def mixer_conv(padded, conv_weight, conv_bias, length):
    conv_sum = conv_bias[None, :] + conv_weight[0][None, :] * padded[0:length]
    for offset in range(1, conv_weight.shape[0]):
        conv_sum = conv_sum + conv_weight[offset][None, :] * padded[offset : offset + length]
    return jax.nn.silu(conv_sum).astype(jnp.bfloat16)


def shards(
    mixer_in,
    gate_in,
    conv_weight,
    conv_bias,
    x_proj,
    dt_proj,
    dt_bias,
    decay_rate,
    skip,
    out_proj,
    residual,
    gain,
    router,
    w_gate,
    w_up,
    w_down,
    expert_ids,
):
    length, channels = mixer_in.shape
    kernel_width = conv_weight.shape[0]
    rim_rows = from_behind(mixer_in[length - (kernel_width - 1) :], "ctx", 1)
    padded = jnp.concatenate([rim_rows, mixer_in], axis=0).astype(jnp.float32)
    conv_out = mixer_conv(padded, conv_weight, conv_bias, length)
    projected = lax.psum(jnp.dot(conv_out, x_proj, preferred_element_type=jnp.float32), "exp")
    rank_width = dt_proj.shape[0]
    state_count = (projected.shape[1] - rank_width) // 2
    step_low = projected[:, :rank_width].astype(jnp.bfloat16)
    b_mat = projected[:, rank_width : rank_width + state_count]
    c_mat = projected[:, rank_width + state_count :]
    step_size = jax.nn.softplus(
        jnp.dot(step_low, dt_proj, preferred_element_type=jnp.float32) + dt_bias[None, :]
    )
    x_value = conv_out.astype(jnp.float32)
    drive = step_size * x_value
    total_step = jnp.sum(step_size, axis=0)
    block_width = 256
    block_count = channels // block_width
    group_len = 32
    group_count = length // group_len
    b_groups = b_mat.reshape(group_count, group_len, state_count)
    c_groups = c_mat.reshape(group_count, group_len, state_count)

    def to_blocks(values):
        return values.reshape(values.shape[0], block_count, block_width).transpose(1, 0, 2)

    def local_scan(pieces):
        step_b, drive_b, rate_b = pieces
        steps_g = step_b.reshape(group_count, group_len, block_width)
        running = jnp.cumsum(steps_g, axis=1)
        exponent = rate_b[None, None] * running[:, :, None, :]
        inputs = b_groups[:, :, :, None] * drive_b.reshape(group_count, group_len, 1, block_width)
        decay_in = jnp.exp(-exponent)
        inner = decay_in * jnp.cumsum(jnp.exp(exponent) * inputs, axis=1)
        group_decay = decay_in[:, -1]
        group_final = inner[:, -1]

        def carry_step(state, parts):
            decay_part, final_part = parts
            return (decay_part * state + final_part, state)

        last_state, entering = lax.scan(
            carry_step,
            jnp.zeros((state_count, block_width), jnp.float32),
            (group_decay, group_final),
        )
        states = inner + decay_in * entering[:, None]
        local_out = jnp.sum(c_groups[:, :, :, None] * states, axis=2).reshape(length, block_width)
        return (local_out, last_state)

    local_blocks, final_blocks = lax.map(
        local_scan, (to_blocks(step_size), to_blocks(drive), to_blocks(decay_rate))
    )
    b_total = final_blocks.transpose(1, 0, 2).reshape(state_count, channels)
    a_total = jnp.exp(-decay_rate * total_step[None, :])
    carry_in = entering_2(
        (a_total, b_total), "ctx", link_pairs, (jnp.ones_like(a_total), jnp.zeros_like(b_total))
    )[1]
    cumulative = jnp.cumsum(step_size, axis=0)

    def carried(pieces):
        cum_b, rate_b, carry_b = pieces
        weight = jnp.exp(-rate_b[None] * cum_b[:, None, :]) * carry_b[None]
        return jnp.sum(c_mat[:, :, None] * weight, axis=1)

    carry_blocks = lax.map(
        carried, (to_blocks(cumulative), to_blocks(decay_rate), to_blocks(carry_in))
    )
    scan_out = (local_blocks + carry_blocks).transpose(1, 0, 2).reshape(length, channels) + skip[
        None, :
    ] * x_value
    gated = (scan_out * jax.nn.silu(gate_in.astype(jnp.float32))).astype(jnp.bfloat16)
    tok_rows = residual.shape[0]
    exp_count = lax.axis_size("exp")
    full_out = lax.all_gather(out_proj, "ctx", axis=1, tiled=True)
    mamba_out = lax.psum_scatter(
        jnp.dot(gated, full_out, preferred_element_type=jnp.float32),
        "exp",
        scatter_dimension=0,
        tiled=True,
    )
    stream = residual.astype(jnp.float32) + mamba_out
    normed = (
        stream * lax.rsqrt(jnp.mean(stream * stream, axis=1, keepdims=True) + 1e-06) * gain[None, :]
    ).astype(jnp.bfloat16)
    logits = jnp.dot(normed, router, preferred_element_type=jnp.float32)
    picked = jnp.take_along_axis(logits, expert_ids, axis=1)
    first_gate = jax.nn.sigmoid(picked[:, 0] - picked[:, 1])
    gate_weights = jnp.stack([first_gate, 1.0 - first_gate], axis=1)
    top_count = expert_ids.shape[1]
    capacity = 5 * top_count * tok_rows // (4 * exp_count)
    flat_ids = expert_ids.reshape(-1)
    expert_hits = (flat_ids[:, None] == jnp.arange(exp_count, dtype=jnp.int32)[None, :]).astype(
        jnp.int32
    )
    earlier = jnp.cumsum(expert_hits, axis=0) - expert_hits
    slot_index = jnp.sum(earlier * expert_hits, axis=1)
    target = flat_ids * capacity + slot_index
    placing = (
        jnp.arange(exp_count * capacity, dtype=jnp.int32)[:, None] == target[None, :]
    ).astype(jnp.bfloat16)
    copies = jnp.repeat(normed, top_count, axis=0)
    outgoing = (
        jnp.dot(placing, copies, preferred_element_type=jnp.float32)
        .astype(jnp.bfloat16)
        .reshape(exp_count, capacity, -1)
    )
    arrived = lax.all_to_all(outgoing, "exp", split_axis=0, concat_axis=0, tiled=True)
    item_count = arrived.shape[1]
    own_rows = exp_count * item_count
    flat_rows = arrived.reshape(own_rows, -1)
    gathered = lax.all_gather(flat_rows, "ctx", axis=0, tiled=True)
    gate_val = jnp.dot(gathered, w_gate[0], preferred_element_type=jnp.float32)
    up_val = jnp.dot(gathered, w_up[0], preferred_element_type=jnp.float32)
    hidden = (jax.nn.silu(gate_val) * up_val).astype(jnp.bfloat16)
    summed_rows = lax.psum_scatter(
        jnp.dot(hidden, w_down[0], preferred_element_type=jnp.float32).astype(jnp.bfloat16),
        "ctx",
        scatter_dimension=0,
        tiled=True,
    )
    answer = summed_rows.reshape(exp_count, item_count, -1)
    returned = lax.all_to_all(answer, "exp", split_axis=0, concat_axis=0, tiled=True)
    back_rows = returned.reshape(exp_count * capacity, -1)
    fetched = (
        jnp.take(back_rows, target, axis=0).reshape(tok_rows, top_count, -1).astype(jnp.float32)
    )
    expert_mix = jnp.sum(gate_weights[:, :, None] * fetched, axis=1)
    return (stream + expert_mix).astype(jnp.bfloat16)


def solution(mesh):
    in_specs = (
        P("ctx", "exp"),
        P("ctx", "exp"),
        P(None, "exp"),
        P("exp"),
        P("exp", None),
        P(None, "exp"),
        P("exp"),
        P(None, "exp"),
        P("exp"),
        P("exp", "ctx"),
        P(("ctx", "exp"), None),
        P(),
        P(),
        P("exp", None, "ctx"),
        P("exp", None, "ctx"),
        P("exp", "ctx", None),
        P(("ctx", "exp"), None),
    )
    out_specs = P(("ctx", "exp"), None)
    return jax.shard_map(shards, mesh=mesh, in_specs=in_specs, out_specs=out_specs, check_vma=False)
```

profile of v0, /device:TPU:1, one launch (start us, length us, event | category | flops | bytes accessed | tf_op | source)
XLA Modules:
  0.0 530.1 jit_solution(5454164598774543847)
XLA Ops:
  7.4 4.0 collective-permute-start
  16.4 61.2 %all-reduce.3.cloned.1.call-done = f32[128,544]{0,1:T(8,128)} async-done(((f32[128,544]{0,1:T(8,128)}), f32[128,544]{0,1:T(8,128)}) %all-reduce.3.cloned.1.call-update) | async-done | bytes 278544 | tf_op jit(solution)/shard_map/psum | solution.py:61
  79.8 1.6 fusion.37
  84.1 36.1 %while.48 = (s32[]{:T(128)}, f32[4,128,256]{2,1,0:T(8,128)}, f32[4,16,256]{2,1,0:T(8,128)}, f32[128,16]{1,0:T(8,128)}, f32[4,16,256]{2,1,0:T(8,128)}, /*index=5*...) while((s32[]{:T(128)}, f32[4,128,256]{2,1,0:T(8,128)}, ...), condition=%wide.region_7.8_spmd, body=%wide.region_1.7_spmd.sunk | while | flops 24592388 | bytes 8554277 | solution.py:107
  85.9 1.5 fusion.58
  87.8 2.5 while.51
  90.3 1.6 multiply_reduce_fusion.6
  95.0 1.5 fusion.58
  96.8 2.5 while.51
  99.3 1.6 multiply_reduce_fusion.6
  104.0 1.5 fusion.58
  105.9 2.5 while.51
  108.3 1.6 multiply_reduce_fusion.6
  113.1 1.5 fusion.58
  114.9 2.5 while.51
  117.4 1.6 multiply_reduce_fusion.6
  121.9 1.5 multiply_exponential_fusion.1
  125.5 38.6 %all-gather.6.cloned.1.call-done = f32[16,16,1024]{2,1,0:T(8,128)} async-done(((f32[1,16,1024]{2,1,0:T(8,128)}), f32[16,16,1024]{2,1,0:T(8,128)}) %all-gather.6.cloned.1.call-update) | async-done | bytes 1048592 | tf_op jit(solution)/shard_map/all_gather | solution.py:15
  164.0 44.2 %all-gather.12.cloned.1.call-done = f32[256,1024]{1,0:T(8,128)} async-done(((f32[16,1024]{1,0:T(8,128)}), f32[256,1024]{1,0:T(8,128)}) %all-gather.12.cloned.1.call-update) | async-done | bytes 1048592 | tf_op jit(solution)/shard_map/all_gather | solution.py:15
  208.4 6.5 %while.50 = (s32[]{:T(128)}, f32[4,128,256]{2,1,0:T(8,128)S(1)}, f32[128,16]{1,0:T(8,128)S(1)}, f32[4,16,256]{2,1,0:T(8,128)}, f32[4,128,256]{2,0,1:T(4,128)S(1)}, /*index=5*/f32[4,16,256]{2,0,1:T(4,128)S(1)}, s32[]{:T(128)}) while((s32[]{:T(128)}, f32[4,128,256]{2,1,0:T(8,128)S(1)}, f32[128,16]{1,0:T(8,128)S(1)}, ...), condition=%wide.region_14.15_spmd, body=%wide.region_12.14_spmd.sunk | while | flops 2068482 | bytes 1187933 | solution.py:122
  215.1 73.5 %all-gather.8.cloned.1.call-done = bf16[1024,4096]{1,0:T(8,128)(2,1)} async-done(((bf16[1024,256]{1,0:T(8,128)(2,1)}), bf16[1024,4096]{1,0:T(8,128)(2,1)}) %all-gather.8.cloned.1.call-update) | async-done | bytes 8388624 | tf_op jit(solution)/shard_map/all_gather | solution.py:131
  288.6 6.1 %fusion.29 = f32[128,4096]{1,0:T(8,128)} fusion(bf16[1024,4096]{1,0:T(8,128)(2,1)} %all-gather.8.cloned.1.call-done, f32[128,1024]{1,0:T(8,128)S(1)} %bitcast.136, bf16[128,1024]{1,0:T(8,128)(2,1)S(1)} %copy-done.3, bf16[128,1024]{1,0:T(8,128)(2,1)S(1)} %copy-done.15, f32[1024]{0:T(1024)S(1)} %copy-done.16), kind=kOutput, calls=%fused_computation.68 | convolution fusion | flops 1075052544 | bytes 11538432 | tf_op jit(solution)/shard_map/dot_general | solution.py:133
  295.8 30.0 %reduce-scatter.5.cloned.1.call-done = f32[16,4096]{1,0:T(8,128)} async-done(((f32[128,4096]{1,0:T(8,128)}), f32[16,4096]{1,0:T(8,128)}) %reduce-scatter.5.cloned.1.call-update) | async-done | bytes 262160 | tf_op jit(solution)/shard_map/reduce_scatter | solution.py:132
  328.7 15.6 %all_to_all.10 = bf16[8,5,4096]{2,1,0:T(8,128)(2,1)S(1)} all-to-all(bf16[8,5,4096]{2,1,0:T(8,128)(2,1)S(1)} %reshape.137), channel_id=1, replica_groups=mesh['ctx'=16,'exp'=8] {'exp'}, dimensions={0} | all-to-all | bytes 655360 | tf_op jit(solution)/shard_map/all_to_all | solution.py:164
  345.4 55.8 %all-gather.10.cloned.1.call-done = bf16[640,4096]{1,0:T(8,128)(2,1)} async-done(((bf16[40,4096]{1,0:T(8,128)(2,1)}), bf16[640,4096]{1,0:T(8,128)(2,1)}) %all-gather.10.cloned.1.call-update) | async-done | bytes 5242896 | tf_op jit(solution)/shard_map/all_gather | solution.py:168
  401.2 8.1 %fusion.15 = f32[640,768]{1,0:T(8,128)S(1)} fusion(bf16[640,4096]{1,0:T(8,128)(2,1)} %all-gather.10.cloned.1.call-done, bf16[1,4096,768]{2,1,0:T(8,128)(2,1)} %param.38), kind=kOutput, calls=%fused_computation.37 | convolution fusion | flops 4026531840 | bytes 13500416 | tf_op jit(solution)/shard_map/dot_general | solution.py:169
  409.4 7.2 %multiply_convert_fusion = bf16[640,768]{1,0:T(8,128)(2,1)S(1)} fusion(f32[640,768]{1,0:T(8,128)S(1)} %fusion.15, bf16[640,4096]{1,0:T(8,128)(2,1)S(1)} %copy-done.14, bf16[1,4096,768]{2,1,0:T(8,128)(2,1)} %param.39), kind=kOutput, calls=%fused_computation.40 | convolution fusion | flops 4029480960 | bytes 14483456 | tf_op jit(solution)/shard_map/dot_general | solution.py:170
  416.6 8.8 %convolution_convert_fusion = bf16[640,4096]{1,0:T(8,128)(2,1)} fusion(bf16[640,768]{1,0:T(8,128)(2,1)S(1)} %multiply_convert_fusion, bf16[1,768,4096]{2,1,0:T(8,128)(2,1)} %param.40), kind=kOutput, calls=%fused_computation.33 | convolution fusion | flops 4029153280 | bytes 12517376 | tf_op jit(solution)/shard_map/dot_general | solution.py:173
  427.2 76.0 %reduce-scatter.7.cloned.1.call-done = bf16[40,4096]{1,0:T(8,128)(2,1)} async-done(((bf16[640,4096]{1,0:T(8,128)(2,1)}), bf16[40,4096]{1,0:T(8,128)(2,1)}) %reduce-scatter.7.cloned.1.call-update) | async-done | bytes 327696
  503.2 1.9 reshape.139
  505.1 6.1 %all-to-all-start.1 = ((bf16[8,5,4096]{2,1,0:T(8,128)(2,1)}), bf16[8,5,4096]{2,1,0:T(8,128)(2,1)S(1)}, u32[]{:S(2)}, u32[]{:S(2)}) async-start(bf16[8,5,4096]{2,1,0:T(8,128)(2,1)} %reshape.139), calls=%async_computation.2 | async-start | bytes 1048576 | tf_op jit(solution)/shard_map/all_to_all | solution.py:179
  511.3 9.4 %all-to-all-done.1 = bf16[8,5,4096]{2,1,0:T(8,128)(2,1)S(1)} async-done(((bf16[8,5,4096]{2,1,0:T(8,128)(2,1)}), bf16[8,5,4096]{2,1,0:T(8,128)(2,1)S(1)}, u32[]{:S(2)}, u32[]{:S(2)}) %all-to-all-start.1) | async-done | bytes 327712 | tf_op jit(solution)/shard_map/all_to_all | solution.py:179
  (207 shorter events, 53.8 us)
Async XLA Ops:
  6.5 7.9 %copy-start = (bf16[1024,544]{0,1:T(8,128)(2,1)S(1)}, bf16[1024,544]{0,1:T(8,128)(2,1)}, u32[]{:S(2)}) copy-start(bf16[1024,544]{0,1:T(8,128)(2,1)} %param.29) | copy-start | bytes 3342340
  6.5 71.1 %all-reduce.3.cloned.1.call-start = ((), (), s32[]{:S(2)}) async-start(), calls=%async_computation.4 | async-start | bytes 557056 | tf_op jit(solution)/shard_map/psum | solution.py:61
  7.4 4.9 collective-permute-start
  13.3 2.4 copy-start.9
  13.3 66.5 %copy-start.8 = (bf16[512,1024]{1,0:T(8,128)(2,1)S(1)}, bf16[512,1024]{1,0:T(8,128)(2,1)}, u32[]{:S(2)}) copy-start(bf16[512,1024]{1,0:T(8,128)(2,1)} %param.30) | copy-start | bytes 3145732
  13.3 66.5 %copy-start.13 = (f32[1024]{0:T(1024)S(1)}, f32[1024]{0:T(1024)}, u32[]{:S(2)}) copy-start(f32[1024]{0:T(1024)} %param.31) | copy-start | bytes 12292
  14.5 66.9 %copy-start.2 = (bf16[128,1024]{1,0:T(8,128)(2,1)}, bf16[128,1024]{1,0:T(8,128)(2,1)S(1)}, u32[]{:S(2)}) copy-start(bf16[128,1024]{1,0:T(8,128)(2,1)S(1)} %multiply_convert_fusion.1) | copy-start | bytes 786436
  15.7 148.3 %all-gather.6.cloned.1.call-start = ((), (), s32[]{:S(2)}) async-start(), calls=%async_computation.5 | async-start | bytes 1114112 | tf_op jit(solution)/shard_map/all_gather | solution.py:15
  81.4 0.8 copy-start.1
  121.8 86.5 %all-gather.12.cloned.1.call-start = ((), (), s32[]{:S(2)}) async-start(), calls=%async_computation.9 | async-start | bytes 1114112 | tf_op jit(solution)/shard_map/all_gather | solution.py:15
  123.4 165.2 %all-gather.8.cloned.1.call-start = ((), (), s32[]{:S(2)}) async-start(), calls=%async_computation.6 | async-start | bytes 8912896 | tf_op jit(solution)/shard_map/all_gather | solution.py:131
  124.0 201.9 %reduce-scatter.5.cloned.1.call-start = ((), (), s32[]{:S(2)}) async-start(), calls=%async_computation.7 | async-start | bytes 2359296 | tf_op jit(solution)/shard_map/reduce_scatter | solution.py:132
  124.0 84.4 %copy-start.4 = (f32[128,16]{1,0:T(8,128)S(1)}, f32[128,16]{1,0:T(8,128)}, u32[]{:S(2)}) copy-start(f32[128,16]{1,0:T(8,128)} %get-tuple-element.595) | copy-start | bytes 24580
  208.4 6.6 %copy-start.6 = (f32[4,128,256]{2,1,0:T(8,128)S(1)}, f32[4,128,256]{2,1,0:T(8,128)}, u32[]{:S(2)}) copy-start(f32[4,128,256]{2,1,0:T(8,128)} %get-tuple-element.152) | copy-start | bytes 1572868
  214.9 73.6 %copy-start.3 = (bf16[128,1024]{1,0:T(8,128)(2,1)S(1)}, bf16[128,1024]{1,0:T(8,128)(2,1)}, u32[]{:S(2)}) copy-start(bf16[128,1024]{1,0:T(8,128)(2,1)} %copy-done.2) | copy-start | bytes 786436
  214.9 73.6 %copy-start.15 = (bf16[128,1024]{1,0:T(8,128)(2,1)S(1)}, bf16[128,1024]{1,0:T(8,128)(2,1)}, u32[]{:S(2)}) copy-start(bf16[128,1024]{1,0:T(8,128)(2,1)} %param.26) | copy-start | bytes 786436
  214.9 73.6 %copy-start.16 = (f32[1024]{0:T(1024)S(1)}, f32[1024]{0:T(1024)}, u32[]{:S(2)}) copy-start(f32[1024]{0:T(1024)} %param.33) | copy-start | bytes 12292
  294.7 0.7 copy-start.11
  294.7 31.2 %copy-start.7 = (bf16[16,4096]{1,0:T(8,128)(2,1)S(1)}, bf16[16,4096]{1,0:T(8,128)(2,1)}, u32[]{:S(2)}) copy-start(bf16[16,4096]{1,0:T(8,128)(2,1)} %param.35) | copy-start | bytes 393220
  294.7 32.3 %copy-start.12 = (f32[4096]{0:T(1024)S(1)}, f32[4096]{0:T(1024)}, u32[]{:S(2)}) copy-start(f32[4096]{0:T(1024)} %param.36) | copy-start | bytes 49156
  294.7 106.6 %all-gather.10.cloned.1.call-start = ((), (), s32[]{:S(2)}) async-start(), calls=%async_computation.8 | async-start | bytes 5570560 | tf_op jit(solution)/shard_map/all_gather | solution.py:168
  345.2 157.9 %reduce-scatter.7.cloned.1.call-start = ((), (), s32[]{:S(2)}) async-start(), calls=%async_computation.10 | async-start | bytes 5570560
  401.2 8.1 %copy-start.14 = (bf16[640,4096]{1,0:T(8,128)(2,1)S(1)}, bf16[640,4096]{1,0:T(8,128)(2,1)}, u32[]{:S(2)}) copy-start(bf16[640,4096]{1,0:T(8,128)(2,1)} %all-gather.10.cloned.1.call-done) | copy-start | bytes 15728644
  425.3 0.8 copy-start.10
  505.1 15.6 %all-to-all-start.1 = ((bf16[8,5,4096]{2,1,0:T(8,128)(2,1)}), bf16[8,5,4096]{2,1,0:T(8,128)(2,1)S(1)}, u32[]{:S(2)}, u32[]{:S(2)}) async-start(bf16[8,5,4096]{2,1,0:T(8,128)(2,1)} %reshape.139), calls=%async_computation.2 | async-start | bytes 1048576 | tf_op jit(solution)/shard_map/all_to_all | solution.py:179
  511.3 11.2 %copy-start.5 = (f32[16,4096]{1,0:T(8,128)S(1)}, f32[16,4096]{1,0:T(8,128)}, u32[]{:S(2)}) copy-start(f32[16,4096]{1,0:T(8,128)} %reduce-scatter.5.cloned.1.call-done) | copy-start | bytes 786436
Sparse Core Ops, SparseCore 0:
  15.8 61.7 all-reduce.2
  121.9 42.0 all-gather.5
  166.4 41.8 all-gather.11
  210.5 78.0 all-gather.7
  294.8 31.0 reduce-scatter.4
  345.3 55.8 all-gather.9
  425.5 77.6 reduce-scatter.6
where the time goes:
time: 532 us; the launch traced here: 530 us
  waiting for transfers between devices  389 us (73%)
  other arithmetic  37.5 us (7%)
  matrix products  33.3 us (6%)
  local copies, waits for them, and re-layouts  29.5 us (6%)
  blocking collectives  15.6 us (3%)
  between operations  13.9 us (3%)
  starting transfers between devices  10.6 us (2%)
    all_gather x2, waiting for transfers between devices, entering_2(): gathered = jax.tree.map(lambda a: lax.all_gather(a, axis), part)  82.8 us
    unnamed x8, waiting for transfers between devices  76.6 us
    all_gather x1, waiting for transfers between devices, shards(): full_out = lax.all_gather(out_proj, 'ctx', axis=1, tiled=True)  73.5 us
    psum x1, waiting for transfers between devices, shards(): lax.psum(jnp.dot(conv_out, x_proj, preferred_element_type=jnp.float32), '...  61.2 us
    all_gather x1, waiting for transfers between devices, shards(): gathered = lax.all_gather(flat_rows, 'ctx', axis=0, tiled=True)  55.8 us
    reduce_scatter x1, waiting for transfers between devices, shards(): lax.psum_scatter(jnp.dot(gated, full_out, preferred_element_type=jnp.floa...  30 us
    all_to_all x1, blocking collectives, shards(): lax.all_to_all(outgoing, 'exp', split_axis=0, concat_axis=0, tiled=True)  15.6 us
  transfers between devices with their start and end apart: 9, of which 8 were waited for; matrix products, arithmetic and copies ran while one was open for 2% of the time, Pallas kernels for 0%

commit v1 on v0

--- a/solution.py
+++ b/solution.py
@@ -1,7 +1,16 @@
+import functools
+
 import jax
 import jax.numpy as jnp
+import numpy as np
 from jax import lax
+from jax.experimental import pallas as pl
+from jax.experimental.pallas import tpu as pltpu
 from jax.sharding import PartitionSpec as P
+
+F32 = jnp.float32
+BF16 = jnp.bfloat16
+VMEM_LIMIT = 60 * 1024 * 1024
 
 
 def from_behind(value, axis, steps):
@@ -32,6 +41,400 @@
     for offset in range(1, conv_weight.shape[0]):
         conv_sum = conv_sum + conv_weight[offset][None, :] * padded[offset : offset + length]
     return jax.nn.silu(conv_sum).astype(jnp.bfloat16)
+
+
+def remote(src, dst, send_sem, recv_sem, device):
+    return pltpu.make_async_remote_copy(
+        src_ref=src,
+        dst_ref=dst,
+        send_sem=send_sem,
+        recv_sem=recv_sem,
+        device_id=device,
+        device_id_type=pl.DeviceIdType.MESH,
+    )
+
+
+def greet(devices):
+    barrier = pltpu.get_barrier_semaphore()
+    for device in devices:
+        pl.semaphore_signal(barrier, inc=1, device_id=device, device_id_type=pl.DeviceIdType.MESH)
+    pl.semaphore_wait(barrier, len(devices))
+
+
+def wrap(index, count):
+    return lax.rem(index + count, count)
+
+
+def dot(a, b):
+    return jnp.dot(a, b, preferred_element_type=F32)
+
+
+class Half:
+    def __init__(self, half, mx, my):
+        self.half = half
+        self.mx, self.my = mx, my
+        self.p, self.q = (mx, my) if half == 0 else (my, mx)
+
+    def one(self, step):
+        p = wrap(self.p + step, 4)
+        return {"ctx": p * 4 + self.my if self.half == 0 else self.mx * 4 + p}
+
+    def two(self, step):
+        q = wrap(self.q + step, 4)
+        return {"ctx": self.mx * 4 + q if self.half == 0 else q * 4 + self.my}
+
+    def unit(self, u, v):
+        return (u, v) if self.half == 0 else (v, u)
+
+    def group(self, v):
+        return (slice(None), v) if self.half == 0 else (v, slice(None))
+
+
+def moe_kernel(
+    normed,
+    stream,
+    gates,
+    spread_a,
+    spread_b,
+    pick_a,
+    pick_b,
+    fetch,
+    w_gate,
+    w_up,
+    w_down,
+    out,
+    go,
+    rcv,
+    rback,
+    xa,
+    xb,
+    wgu,
+    wd,
+    lhs,
+    acc,
+    hid,
+    oa,
+    ob,
+    far,
+    near,
+    tot,
+    far2,
+    near2,
+    w_sem,
+    d_send,
+    d_recv,
+    g_send,
+    g_recv,
+    s_send,
+    s_recv,
+    r_send,
+    r_recv,
+):
+    ctx, exp = lax.axis_index("ctx"), lax.axis_index("exp")
+    mx, my = ctx // 4, ctx % 4
+    halves = (Half(0, mx, my), Half(1, mx, my))
+    xs, os = (xa, xb), (oa, ob)
+    lo, hi = pl.ds(0, 1024), pl.ds(1024, 1024)
+    every = slice(None)
+
+    loads = [
+        pltpu.make_async_copy(w_gate.at[0], wgu.at[:, pl.ds(0, 768)], w_sem.at[0]),
+        pltpu.make_async_copy(w_up.at[0], wgu.at[:, pl.ds(768, 768)], w_sem.at[1]),
+        pltpu.make_async_copy(w_down.at[0], wd, w_sem.at[2]),
+    ]
+    for load in loads:
+        load.start()
+    greet(
+        [h.one(s) for h in halves for s in (1, -1)]
+        + [{"exp": lax.rem(exp + d, 8)} for d in range(1, 8)]
+    )
+
+    rows = normed[...]
+    packed = dot(spread_a[...], rows[:, :2048]) + dot(spread_b[...], rows[:, 2048:])
+    go[...] = packed.astype(BF16).reshape(8, 16, 2048)
+    sends = []
+    for d in range(1, 8):
+        peer = lax.rem(exp + d, 8)
+        c = remote(go.at[peer], rcv.at[exp], d_send.at[d], d_recv.at[d], {"exp": peer})
+        c.start()
+        sends.append(c)
+    rcv[pl.ds(exp, 1)] = go[pl.ds(exp, 1)]
+    acc[...] = jnp.zeros_like(acc)
+    for c in sends:
+        c.wait_recv()
+    flat = rcv[...].reshape(128, 2048)
+    xa[pl.ds(mx, 1), pl.ds(my, 1)] = dot(pick_a[...], flat).astype(BF16)[None, None]
+    xb[pl.ds(mx, 1), pl.ds(my, 1)] = dot(pick_b[...], flat).astype(BF16)[None, None]
+    for c in sends:
+        c.wait_send()
+
+    sent = []
+
+    def push(h, x, at, cols, g, k, device):
+        place = x.at[at + (every, cols)] if cols is not None else x.at[at]
+        c = remote(place, place, g_send.at[h, g, k], g_recv.at[h, g, k], device)
+        c.start()
+        sent.append(c)
+        return c
+
+    first, second = [], [[None] * 4, [None] * 4]
+
+    def second_start(i, g, u):
+        h, x = halves[i], xs[i]
+        at = h.unit(u, h.q)
+        second[i][g] = [
+            push(i, x, at, None, g + 1, 0, h.two(1)),
+            push(i, x, at, None, g + 1, 1, h.two(-1)),
+        ]
+
+    def second_pass(i, g, u):
+        h, x = halves[i], xs[i]
+        second[i][g][0].wait_recv()
+        a = push(i, x, h.unit(u, wrap(h.q - 1, 4)), lo, g + 1, 2, h.two(1))
+        second[i][g][1].wait_recv()
+        b = push(i, x, h.unit(u, wrap(h.q + 1, 4)), hi, g + 1, 3, h.two(-1))
+        second[i][g] += [a, b]
+
+    for i, (h, x) in enumerate(zip(halves, xs)):
+        at = h.unit(h.p, h.q)
+        first.append(
+            [push(i, x, at, None, 0, 0, h.one(1)), push(i, x, at, None, 0, 1, h.one(-1))]
+        )
+    for i, h in enumerate(halves):
+        second_start(i, 0, h.p)
+    for i, (h, x) in enumerate(zip(halves, xs)):
+        left, right = wrap(h.p - 1, 4), wrap(h.p + 1, 4)
+        first[i][0].wait_recv()
+        first[i].append(push(i, x, h.unit(left, h.q), lo, 0, 2, h.one(1)))
+        first[i][1].wait_recv()
+        first[i].append(push(i, x, h.unit(right, h.q), hi, 0, 3, h.one(-1)))
+        second_start(i, 1, left)
+        second_start(i, 2, right)
+    for i, h in enumerate(halves):
+        first[i][2].wait_recv()
+        first[i][3].wait_recv()
+        second_start(i, 3, wrap(h.p + 2, 4))
+
+    def gate_up(i, v):
+        h = halves[i]
+        at = h.group(v)
+        lhs[...] = xs[i][at].reshape(160, 2048)
+
+        @pl.loop(0, 6)
+        def _(j):
+            cols = pl.ds(pl.multiple_of(j * 256, 256), 256)
+            part = dot(lhs[...], wgu[pl.ds(i * 2048, 2048), cols])
+            place = at + (every, cols)
+            acc[place] = acc[place] + part.reshape(4, 40, 256)
+
+    loads[0].wait()
+    loads[1].wait()
+    for i, h in enumerate(halves):
+        gate_up(i, h.q)
+    for g in range(4):
+        for i, h in enumerate(halves):
+            u = (h.p, wrap(h.p - 1, 4), wrap(h.p + 1, 4), wrap(h.p + 2, 4))[g]
+            second_pass(i, g, u)
+    for i, h in enumerate(halves):
+        gate_up(i, wrap(h.q - 1, 4))
+        gate_up(i, wrap(h.q + 1, 4))
+    for i, h in enumerate(halves):
+        for g in range(4):
+            second[i][g][2].wait_recv()
+            second[i][g][3].wait_recv()
+        gate_up(i, wrap(h.q + 2, 4))
+
+    @pl.loop(0, 16)
+    def _(n):
+        at = (n // 4, n % 4)
+        gate = acc[at + (every, pl.ds(0, 768))]
+        up = acc[at + (every, pl.ds(768, 768))]
+        hid[at] = (gate * jax.nn.sigmoid(gate) * up).astype(BF16)
+
+    loads[2].wait()
+
+    def down(i, v):
+        at = halves[i].group(v)
+        lhs[:, pl.ds(0, 768)] = hid[at].reshape(160, 768)
+
+        @pl.loop(0, 8)
+        def _(j):
+            start = pl.multiple_of(j * 256, 256)
+            part = dot(lhs[:, pl.ds(0, 768)], wd[:, pl.ds(i * 2048 + start, 256)])
+            os[i][at + (every, pl.ds(start, 256))] = part.reshape(4, 40, 256).astype(BF16)
+
+    def send(src, dst, i, stage, k, device):
+        c = remote(src, dst, s_send.at[i, stage, k], s_recv.at[i, stage, k], device)
+        c.start()
+        sent.append(c)
+        return c
+
+    def ring_far(i, stage, chunk, ahead, behind, step):
+        return [
+            send(chunk(2, lo), ahead, i, stage, 0, step(1)),
+            send(chunk(2, hi), behind, i, stage, 1, step(-1)),
+        ]
+
+    def add_into(ref, at, other, other_at):
+        ref[at] = (ref[at].astype(F32) + other[other_at].astype(F32)).astype(BF16)
+
+    stage_one = [None, None]
+    for i, h in enumerate(halves):
+        down(i, wrap(h.q + 2, 4))
+        o, at = os[i], h.group(wrap(h.q + 2, 4))
+        stage_one[i] = [
+            send(o.at[at + (every, lo)], far.at[i, 0], i, 0, 0, h.two(1)),
+            send(o.at[at + (every, hi)], far.at[i, 1], i, 0, 1, h.two(-1)),
+        ]
+    for i, h in enumerate(halves):
+        o = os[i]
+        down(i, wrap(h.q + 1, 4))
+        at = h.group(wrap(h.q + 1, 4))
+        stage_one[i].append(
+            send(o.at[at + (every, hi)], near.at[i, 0, :, :, hi], i, 0, 2, h.two(1))
+        )
+        down(i, wrap(h.q - 1, 4))
+        at = h.group(wrap(h.q - 1, 4))
+        stage_one[i].append(
+            send(o.at[at + (every, lo)], near.at[i, 1, :, :, lo], i, 0, 3, h.two(-1))
+        )
+    for i, h in enumerate(halves):
+        down(i, h.q)
+    for i, h in enumerate(halves):
+        o = os[i]
+        stage_one[i][0].wait_recv()
+        at = h.group(wrap(h.q + 1, 4)) + (every, lo)
+        add_into(o, at, far, (i, 0))
+        stage_one[i].append(send(o.at[at], near.at[i, 0, :, :, lo], i, 0, 4, h.two(1)))
+        stage_one[i][1].wait_recv()
+        at = h.group(wrap(h.q - 1, 4)) + (every, hi)
+        add_into(o, at, far, (i, 1))
+        stage_one[i].append(send(o.at[at], near.at[i, 1, :, :, hi], i, 0, 5, h.two(-1)))
+
+    stage_two = [None, None]
+    for i, h in enumerate(halves):
+        for c in stage_one[i][2:]:
+            c.wait_recv()
+
+        def total(u):
+            mine = os[i][h.unit(u, h.q)].astype(F32)
+            tot[i, u] = (mine + near[i, 0, u].astype(F32) + near[i, 1, u].astype(F32)).astype(BF16)
+
+        opposite, ahead, behind = wrap(h.p + 2, 4), wrap(h.p + 1, 4), wrap(h.p - 1, 4)
+        total(opposite)
+        stage_two[i] = [
+            send(tot.at[i, opposite, :, lo], far2.at[i, 0], i, 1, 0, h.one(1)),
+            send(tot.at[i, opposite, :, hi], far2.at[i, 1], i, 1, 1, h.one(-1)),
+        ]
+        total(ahead)
+        total(behind)
+        stage_two[i].append(send(tot.at[i, ahead, :, hi], near2.at[i, 0, :, hi], i, 1, 2, h.one(1)))
+        stage_two[i].append(
+            send(tot.at[i, behind, :, lo], near2.at[i, 1, :, lo], i, 1, 3, h.one(-1))
+        )
+        total(h.p)
+    for i, h in enumerate(halves):
+        ahead, behind = wrap(h.p + 1, 4), wrap(h.p - 1, 4)
+        stage_two[i][0].wait_recv()
+        add_into(tot, (i, ahead, every, lo), far2, (i, 0))
+        stage_two[i].append(send(tot.at[i, ahead, :, lo], near2.at[i, 0, :, lo], i, 1, 4, h.one(1)))
+        stage_two[i][1].wait_recv()
+        add_into(tot, (i, behind, every, hi), far2, (i, 1))
+        stage_two[i].append(
+            send(tot.at[i, behind, :, hi], near2.at[i, 1, :, hi], i, 1, 5, h.one(-1))
+        )
+    ends = []
+    for i, h in enumerate(halves):
+        for c in stage_two[i][2:]:
+            c.wait_recv()
+        final = (
+            tot[i, h.p].astype(F32) + near2[i, 0].astype(F32) + near2[i, 1].astype(F32)
+        ).astype(BF16)
+        ends.append(final)
+
+    across = (((0,), (0,)), ((), ()))
+    back = lax.dot_general(pick_a[...], ends[0], across, preferred_element_type=F32)
+    back = back + lax.dot_general(pick_b[...], ends[1], across, preferred_element_type=F32)
+    go[...] = back.astype(BF16).reshape(8, 16, 2048)
+    sends = []
+    for d in range(1, 8):
+        peer = lax.rem(exp + d, 8)
+        c = remote(go.at[peer], rback.at[exp], r_send.at[d], r_recv.at[d], {"exp": peer})
+        c.start()
+        sends.append(c)
+    rback[pl.ds(exp, 1)] = go[pl.ds(exp, 1)]
+    for c in sends:
+        c.wait_recv()
+    flat = rback[...].reshape(128, 2048)
+    g = gates[...]
+    for i in range(2):
+        cols = pl.ds(i * 2048, 2048)
+        mix = g[:, 0:1] * dot(fetch[i, 0], flat) + g[:, 1:2] * dot(fetch[i, 1], flat)
+        out[:, cols] = (stream[:, cols] + mix).astype(BF16)
+    for c in sends + sent:
+        c.wait_send()
+
+
+def expert_layer(normed, stream, gates, expert_ids, w_gate, w_up, w_down):
+    flat_ids = expert_ids.reshape(-1)
+    hits = (flat_ids[:, None] == jnp.arange(8, dtype=jnp.int32)[None, :]).astype(jnp.int32)
+    earlier = jnp.cumsum(hits, axis=0) - hits
+    slot = jnp.sum(earlier * hits, axis=1)
+    target = (flat_ids * 16 + slot).reshape(16, 2)
+    places = jnp.arange(128, dtype=jnp.int32)
+    first = target[:, 0][:, None] == places[None, :]
+    both = first | (target[:, 1][:, None] == places[None, :])
+    spread_a = both.T.astype(BF16)
+    spread_b = jnp.roll(spread_a, 8, axis=0)
+    fetch_a = jnp.stack([first, both & ~first]).astype(BF16)
+    fetch = jnp.stack([fetch_a, jnp.roll(fetch_a, 8, axis=2)])
+    pick = np.zeros((2, 40, 128), np.float32)
+    for j in range(8):
+        for s in range(5):
+            pick[0, j * 5 + s, j * 16 + s] = 1.0
+            pick[1, j * 5 + s, j * 16 + 8 + s] = 1.0
+    pick_a, pick_b = jnp.asarray(pick[0], BF16), jnp.asarray(pick[1], BF16)
+    vmem = pl.BlockSpec(memory_space=pltpu.VMEM)
+    anywhere = pl.BlockSpec(memory_space=pl.ANY)
+    dma = pltpu.SemaphoreType.DMA
+    return pl.pallas_call(
+        moe_kernel,
+        out_shape=jax.ShapeDtypeStruct((16, 4096), BF16),
+        in_specs=[vmem] * 8 + [anywhere] * 3,
+        out_specs=vmem,
+        scratch_shapes=[
+            pltpu.VMEM((8, 16, 2048), BF16),
+            pltpu.VMEM((8, 16, 2048), BF16),
+            pltpu.VMEM((8, 16, 2048), BF16),
+            pltpu.VMEM((4, 4, 40, 2048), BF16),
+            pltpu.VMEM((4, 4, 40, 2048), BF16),
+            pltpu.VMEM((4096, 1536), BF16),
+            pltpu.VMEM((768, 4096), BF16),
+            pltpu.VMEM((160, 2048), BF16),
+            pltpu.VMEM((4, 4, 40, 1536), F32),
+            pltpu.VMEM((4, 4, 40, 768), BF16),
+            pltpu.VMEM((4, 4, 40, 2048), BF16),
+            pltpu.VMEM((4, 4, 40, 2048), BF16),
+            pltpu.VMEM((2, 2, 4, 40, 1024), BF16),
+            pltpu.VMEM((2, 2, 4, 40, 2048), BF16),
+            pltpu.VMEM((2, 4, 40, 2048), BF16),
+            pltpu.VMEM((2, 2, 40, 1024), BF16),
+            pltpu.VMEM((2, 2, 40, 2048), BF16),
+            dma((3,)),
+            dma((8,)),
+            dma((8,)),
+            dma((2, 5, 4)),
+            dma((2, 5, 4)),
+            dma((2, 2, 6)),
+            dma((2, 2, 6)),
+            dma((8,)),
+            dma((8,)),
+        ],
+        compiler_params=pltpu.CompilerParams(
+            collective_id=1, has_side_effects=True, vmem_limit_bytes=VMEM_LIMIT
+        ),
+        cost_estimate=pl.CostEstimate(flops=12_000_000_000, bytes_accessed=19_000_000, transcendentals=0),
+    )(normed, stream, gates, spread_a, spread_b, pick_a, pick_b, fetch, w_gate, w_up, w_down)
 
 
 def shards(
@@ -143,46 +546,7 @@
     picked = jnp.take_along_axis(logits, expert_ids, axis=1)
     first_gate = jax.nn.sigmoid(picked[:, 0] - picked[:, 1])
     gate_weights = jnp.stack([first_gate, 1.0 - first_gate], axis=1)
-    top_count = expert_ids.shape[1]
-    capacity = 5 * top_count * tok_rows // (4 * exp_count)
-    flat_ids = expert_ids.reshape(-1)
-    expert_hits = (flat_ids[:, None] == jnp.arange(exp_count, dtype=jnp.int32)[None, :]).astype(
-        jnp.int32
-    )
-    earlier = jnp.cumsum(expert_hits, axis=0) - expert_hits
-    slot_index = jnp.sum(earlier * expert_hits, axis=1)
-    target = flat_ids * capacity + slot_index
-    placing = (
-        jnp.arange(exp_count * capacity, dtype=jnp.int32)[:, None] == target[None, :]
-    ).astype(jnp.bfloat16)
-    copies = jnp.repeat(normed, top_count, axis=0)
-    outgoing = (
-        jnp.dot(placing, copies, preferred_element_type=jnp.float32)
-        .astype(jnp.bfloat16)
-        .reshape(exp_count, capacity, -1)
-    )
-    arrived = lax.all_to_all(outgoing, "exp", split_axis=0, concat_axis=0, tiled=True)
-    item_count = arrived.shape[1]
-    own_rows = exp_count * item_count
-    flat_rows = arrived.reshape(own_rows, -1)
-    gathered = lax.all_gather(flat_rows, "ctx", axis=0, tiled=True)
-    gate_val = jnp.dot(gathered, w_gate[0], preferred_element_type=jnp.float32)
-    up_val = jnp.dot(gathered, w_up[0], preferred_element_type=jnp.float32)
-    hidden = (jax.nn.silu(gate_val) * up_val).astype(jnp.bfloat16)
-    summed_rows = lax.psum_scatter(
-        jnp.dot(hidden, w_down[0], preferred_element_type=jnp.float32).astype(jnp.bfloat16),
-        "ctx",
-        scatter_dimension=0,
-        tiled=True,
-    )
-    answer = summed_rows.reshape(exp_count, item_count, -1)
-    returned = lax.all_to_all(answer, "exp", split_axis=0, concat_axis=0, tiled=True)
-    back_rows = returned.reshape(exp_count * capacity, -1)
-    fetched = (
-        jnp.take(back_rows, target, axis=0).reshape(tok_rows, top_count, -1).astype(jnp.float32)
-    )
-    expert_mix = jnp.sum(gate_weights[:, :, None] * fetched, axis=1)
-    return (stream + expert_mix).astype(jnp.bfloat16)
+    return expert_layer(normed, stream, gate_weights, expert_ids, w_gate, w_up, w_down)
 
 
 def solution(mesh):

time: 532 us -> 438 us (0.82)
  waiting for transfers between devices: 389 us -> 246 us
  Pallas kernels: 0 us -> 99 us
  matrix products: 33.3 us -> 8.99 us
  blocking collectives: 15.6 us -> 0 us
  starting transfers between devices: 10.6 us -> 4.18 us
    pallas_call x0 -> x1, Pallas kernels: none -> 99 us  [expert_layer(): pl.pallas_call(moe_kernel, out_shape=jax.ShapeDtypeStruct((16, 4096), BF1...]
    unnamed x8 -> x5, waiting for transfers between devices: 76.6 us -> 0.59 us
    all_gather x1 -> x0, waiting for transfers between devices: 55.8 us -> none  [shards(): gathered = lax.all_gather(flat_rows, 'ctx', axis=0, tiled=True)]
    dot_general x4 -> x0, matrix products: 24.3 us -> none  [the longest x1 8.79 us: shards(): jnp.dot(hidden, w_down[0], preferred_element_type=jnp.float32)]
    all_to_all x1 -> x0, blocking collectives: 15.6 us -> none  [shards(): lax.all_to_all(outgoing, 'exp', split_axis=0, concat_axis=0, tiled=True)]
    all_to_all x1 -> x0, waiting for transfers between devices: 9.37 us -> none  [shards(): lax.all_to_all(answer, 'exp', split_axis=0, concat_axis=0, tiled=True)]
    all_to_all x1 -> x0, starting transfers between devices: 6.14 us -> none  [shards(): lax.all_to_all(answer, 'exp', split_axis=0, concat_axis=0, tiled=True)]
  transfers between devices with their start and end apart: 9 -> 6, of which waited for: 8 -> 5; matrix products, arithmetic and copies ran while one was open for 2% -> 3% of each run, Pallas kernels for 0% -> 0%
where the time goes in v1:
time: 438 us; the launch traced here: 436 us
  waiting for transfers between devices  246 us (56%)
  Pallas kernels  99 us (23%)
  other arithmetic  37.2 us (8%)
  local copies, waits for them, and re-layouts  26.7 us (6%)
  between operations  13.5 us (3%)
  matrix products  8.99 us (2%)
    pallas_call x1, Pallas kernels, expert_layer(): pl.pallas_call(moe_kernel, out_shape=jax.ShapeDtypeStruct((16, 4096), BF1...  99 us
    all_gather x2, waiting for transfers between devices, entering_2(): gathered = jax.tree.map(lambda a: lax.all_gather(a, axis), part)  82.8 us
    all_gather x1, waiting for transfers between devices, shards(): full_out = lax.all_gather(out_proj, 'ctx', axis=1, tiled=True)  73.5 us
    psum x1, waiting for transfers between devices, shards(): lax.psum(jnp.dot(conv_out, x_proj, preferred_element_type=jnp.float32), '...  61.2 us
    reduce_scatter x1, waiting for transfers between devices, shards(): lax.psum_scatter(jnp.dot(gated, full_out, preferred_element_type=jnp.floa...  27.8 us
    dynamic_update_slice x16, other arithmetic, shards(): lax.map(local_scan, (to_blocks(step_size), to_blocks(drive), to_blocks(de...  9.64 us
  transfers between devices with their start and end apart: 6, of which 5 were waited for; matrix products, arithmetic and copies ran while one was open for 3% of the time, Pallas kernels for 0%

profile of v1, /device:TPU:1, one launch (start us, length us, event | category | flops | bytes accessed | tf_op | source)
XLA Modules:
  0.0 435.9 jit_solution(2482200950870394874)
XLA Ops:
  7.4 4.0 collective-permute-start
  12.3 1.0 maximum_convert_fusion
  13.3 1.1 multiply_convert_fusion
  14.5 1.2 fusion.43
  16.4 61.2 %all-reduce.2.cloned.1.call-done = f32[128,544]{0,1:T(8,128)} async-done(((f32[128,544]{0,1:T(8,128)}), f32[128,544]{0,1:T(8,128)}) %all-reduce.2.cloned.1.call-update) | async-done | bytes 278544 | tf_op jit(solution)/shard_map/psum | solution.py:464
  79.8 1.6 fusion.39
  82.2 1.1 bitcast_bitcast_fusion
  84.1 36.1 %while.48 = (s32[]{:T(128)}, f32[4,128,256]{2,1,0:T(8,128)}, f32[4,16,256]{2,1,0:T(8,128)}, f32[128,16]{1,0:T(8,128)}, f32[4,16,256]{2,1,0:T(8,128)}, /*index=5*...) while((s32[]{:T(128)}, f32[4,128,256]{2,1,0:T(8,128)}, ...), condition=%wide.region_7.8_spmd, body=%wide.region_1.7_spmd.sunk | while | flops 24592388 | bytes 8554277 | solution.py:510
  84.1 1.0 constant_dynamic-slice_fusion.7
  85.9 1.5 fusion.56
  87.8 2.5 while.51
  90.2 1.6 multiply_reduce_fusion.5
  95.0 1.5 fusion.56
  96.8 2.5 while.51
  99.3 1.6 multiply_reduce_fusion.5
  104.0 1.5 fusion.56
  105.8 2.5 while.51
  108.3 1.6 multiply_reduce_fusion.5
  113.0 1.5 fusion.56
  114.9 2.5 while.51
  117.3 1.6 multiply_reduce_fusion.5
  121.9 1.5 multiply_exponential_fusion.1
  124.0 1.3 reshape.261
  125.5 38.6 %all-gather.5.cloned.1.call-done = f32[16,16,1024]{2,1,0:T(8,128)} async-done(((f32[1,16,1024]{2,1,0:T(8,128)}), f32[16,16,1024]{2,1,0:T(8,128)}) %all-gather.5.cloned.1.call-update) | async-done | bytes 1048592 | tf_op jit(solution)/shard_map/all_gather | solution.py:24
  164.0 44.2 %all-gather.9.cloned.1.call-done = f32[256,1024]{1,0:T(8,128)} async-done(((f32[16,1024]{1,0:T(8,128)}), f32[256,1024]{1,0:T(8,128)}) %all-gather.9.cloned.1.call-update) | async-done | bytes 1048592 | tf_op jit(solution)/shard_map/all_gather | solution.py:24
  208.4 6.5 %while.50 = (s32[]{:T(128)}, f32[4,128,256]{2,1,0:T(8,128)S(1)}, f32[128,16]{1,0:T(8,128)S(1)}, f32[4,16,256]{2,1,0:T(8,128)}, f32[4,128,256]{2,0,1:T(4,128)S(1)}, /*index=5*/f32[4,16,256]{2,0,1:T(4,128)S(1)}, s32[]{:T(128)}) while((s32[]{:T(128)}, f32[4,128,256]{2,1,0:T(8,128)S(1)}, f32[128,16]{1,0:T(8,128)S(1)}, ...), condition=%wide.region_14.15_spmd, body=%wide.region_12.14_spmd.sunk | while | flops 2068482 | bytes 1187933 | solution.py:525
  215.1 73.5 %all-gather.7.cloned.1.call-done = bf16[1024,4096]{1,0:T(8,128)(2,1)} async-done(((bf16[1024,256]{1,0:T(8,128)(2,1)}), bf16[1024,4096]{1,0:T(8,128)(2,1)}) %all-gather.7.cloned.1.call-update) | async-done | bytes 8388624 | tf_op jit(solution)/shard_map/all_gather | solution.py:534
  288.6 6.1 %fusion.22 = f32[128,4096]{1,0:T(8,128)} fusion(bf16[1024,4096]{1,0:T(8,128)(2,1)} %all-gather.7.cloned.1.call-done, f32[128,1024]{1,0:T(8,128)S(1)} %bitcast.125, bf16[128,1024]{1,0:T(8,128)(2,1)S(1)} %copy-done.3, bf16[128,1024]{1,0:T(8,128)(2,1)S(1)} %copy-done.16, f32[1024]{0:T(1024)S(1)} %copy-done.17), kind=kOutput, calls=%fused_computation.57 | convolution fusion | flops 1075052544 | bytes 11538432 | tf_op jit(solution)/shard_map/dot_general | solution.py:536
  298.0 27.8 %reduce-scatter.2.cloned.1.call-done = f32[16,4096]{1,0:T(8,128)} async-done(((f32[128,4096]{1,0:T(8,128)}), f32[16,4096]{1,0:T(8,128)}) %reduce-scatter.2.cloned.1.call-update) | async-done | bytes 262160 | tf_op jit(solution)/shard_map/reduce_scatter | solution.py:535
  325.9 1.1 multiply_reduce_fusion.2
  328.9 99.0 %shard_map.181 = bf16[16,4096]{1,0:T(8,128)(2,1)} custom-call(bf16[16,4096]{1,0:T(8,128)(2,1)} %copy-done.8, f32[16,4096]{1,0:T(8,128)} %copy-done.6, f32[16,2]{1,0:T(8,128)} %pad_maximum_fusion.2.gates, bf16[128,16]{1,0:T(8,128)(2,1)} %copy-done.10, bf16[128,16]{1,0:T(8,128)(2,1)} %pad_maximum_fusion.spread_b, bf16[40,128]{1,0:T(8,128)(2,1)} %constant.111.clone.pick_a, ...), custom_call_target="tpu_custom_call" | custom-call | flops 12000000000 | bytes 19000000 | tf_op jit(solution)/shard_map/pallas_call | solution.py:400
  427.8 1.6 copy.184
  (195 shorter events, 42.6 us)
Async XLA Ops:
  6.5 7.9 %copy-start = (bf16[1024,544]{0,1:T(8,128)(2,1)S(1)}, bf16[1024,544]{0,1:T(8,128)(2,1)}, u32[]{:S(2)}) copy-start(bf16[1024,544]{0,1:T(8,128)(2,1)} %param.31) | copy-start | bytes 3342340
  6.5 71.1 %all-reduce.2.cloned.1.call-start = ((), (), s32[]{:S(2)}) async-start(), calls=%async_computation.1 | async-start | bytes 557056 | tf_op jit(solution)/shard_map/psum | solution.py:464
  7.4 4.9 %collective-permute-start = (bf16[3,1024]{1,0:T(4,128)(2,1)S(1)}, bf16[3,1024]{1,0:T(4,128)(2,1)S(1)}, u32[]{:S(2)}, u32[]{:S(2)}) collective-permute-start(bf16[3,1024]{1,0:T(4,128)(2,1)S(1)} %slice.72), channel_id=1, source_target_pairs={{0,8},{8,16},{16,24},{24,32},{32,40},{40,48},{48,56},{56,64},{64,7... | collective-permute-start | bytes 18440 | tf_op jit(solution)/shard_map/ppermute | solution.py:19
  13.3 2.4 copy-start.9
  13.3 66.5 %copy-start.7 = (bf16[512,1024]{1,0:T(8,128)(2,1)S(1)}, bf16[512,1024]{1,0:T(8,128)(2,1)}, u32[]{:S(2)}) copy-start(bf16[512,1024]{1,0:T(8,128)(2,1)} %param.32) | copy-start | bytes 3145732
  13.3 66.5 %copy-start.14 = (f32[1024]{0:T(1024)S(1)}, f32[1024]{0:T(1024)}, u32[]{:S(2)}) copy-start(f32[1024]{0:T(1024)} %param.33) | copy-start | bytes 12292
  14.5 66.9 %copy-start.2 = (bf16[128,1024]{1,0:T(8,128)(2,1)}, bf16[128,1024]{1,0:T(8,128)(2,1)S(1)}, u32[]{:S(2)}) copy-start(bf16[128,1024]{1,0:T(8,128)(2,1)S(1)} %multiply_convert_fusion) | copy-start | bytes 786436
  15.7 148.3 %all-gather.5.cloned.1.call-start = ((), (), s32[]{:S(2)}) async-start(), calls=%async_computation.2 | async-start | bytes 1114112 | tf_op jit(solution)/shard_map/all_gather | solution.py:24
  81.4 0.8 copy-start.1
  121.8 86.5 %all-gather.9.cloned.1.call-start = ((), (), s32[]{:S(2)}) async-start(), calls=%async_computation.5 | async-start | bytes 1114112 | tf_op jit(solution)/shard_map/all_gather | solution.py:24
  123.4 165.2 %all-gather.7.cloned.1.call-start = ((), (), s32[]{:S(2)}) async-start(), calls=%async_computation.3 | async-start | bytes 8912896 | tf_op jit(solution)/shard_map/all_gather | solution.py:534
  124.0 201.9 %reduce-scatter.2.cloned.1.call-start = ((), (), s32[]{:S(2)}) async-start(), calls=%async_computation.4 | async-start | bytes 2359296 | tf_op jit(solution)/shard_map/reduce_scatter | solution.py:535
  124.0 84.4 %copy-start.4 = (f32[128,16]{1,0:T(8,128)S(1)}, f32[128,16]{1,0:T(8,128)}, u32[]{:S(2)}) copy-start(f32[128,16]{1,0:T(8,128)} %get-tuple-element.601) | copy-start | bytes 24580
  208.4 6.6 %copy-start.5 = (f32[4,128,256]{2,1,0:T(8,128)S(1)}, f32[4,128,256]{2,1,0:T(8,128)}, u32[]{:S(2)}) copy-start(f32[4,128,256]{2,1,0:T(8,128)} %get-tuple-element.152) | copy-start | bytes 1572868
  214.9 73.6 %copy-start.3 = (bf16[128,1024]{1,0:T(8,128)(2,1)S(1)}, bf16[128,1024]{1,0:T(8,128)(2,1)}, u32[]{:S(2)}) copy-start(bf16[128,1024]{1,0:T(8,128)(2,1)} %copy-done.2) | copy-start | bytes 786436
  214.9 73.6 %copy-start.16 = (bf16[128,1024]{1,0:T(8,128)(2,1)S(1)}, bf16[128,1024]{1,0:T(8,128)(2,1)}, u32[]{:S(2)}) copy-start(bf16[128,1024]{1,0:T(8,128)(2,1)} %param.28) | copy-start | bytes 786436
  214.9 73.6 %copy-start.17 = (f32[1024]{0:T(1024)S(1)}, f32[1024]{0:T(1024)}, u32[]{:S(2)}) copy-start(f32[1024]{0:T(1024)} %param.35) | copy-start | bytes 12292
  294.7 0.7 copy-start.15
  294.7 31.2 %copy-start.11 = (bf16[16,4096]{1,0:T(8,128)(2,1)S(1)}, bf16[16,4096]{1,0:T(8,128)(2,1)}, u32[]{:S(2)}) copy-start(bf16[16,4096]{1,0:T(8,128)(2,1)} %param.37) | copy-start | bytes 393220
  294.7 32.3 %copy-start.13 = (f32[4096]{0:T(1024)S(1)}, f32[4096]{0:T(1024)}, u32[]{:S(2)}) copy-start(f32[4096]{0:T(1024)} %param.38) | copy-start | bytes 49156
  294.7 32.5 %copy-start.12 = (bf16[4096,8]{0,1:T(8,128)(2,1)S(1)}, bf16[4096,8]{0,1:T(8,128)(2,1)}, u32[]{:S(2)}) copy-start(bf16[4096,8]{0,1:T(8,128)(2,1)} %param.39) | copy-start | bytes 196612
  296.1 31.9 %copy-start.10 = (bf16[128,16]{1,0:T(8,128)(2,1)}, bf16[128,16]{1,0:T(8,128)(2,1)S(1)}, u32[]{:S(2)}) copy-start(bf16[128,16]{1,0:T(8,128)(2,1)S(1)} %fusion.27.spread_a) | copy-start | bytes 12292
  327.0 1.0 copy-start.6
  327.1 0.9 copy-start.8
Sparse Core Ops, SparseCore 0:
  15.8 61.7 all-reduce.1
  121.9 42.0 all-gather.4
  166.4 41.8 all-gather.8
  210.5 78.0 all-gather.6
  294.8 31.0 reduce-scatter.1

commit v2 on v1

--- a/solution.py
+++ b/solution.py
@@ -1,5 +1,3 @@
-import functools
-
 import jax
 import jax.numpy as jnp
 import numpy as np
@@ -11,36 +9,6 @@
 F32 = jnp.float32
 BF16 = jnp.bfloat16
 VMEM_LIMIT = 60 * 1024 * 1024
-
-
-def from_behind(value, axis, steps):
-    count = lax.axis_size(axis)
-    first, last = (max(0, -steps), min(count, count - steps))
-    return lax.ppermute(value, axis, [(source, source + steps) for source in range(first, last)])
-
-
-def entering_2(part, axis, combine, identity):
-    place = lax.axis_index(axis)
-    gathered = jax.tree.map(lambda a: lax.all_gather(a, axis), part)
-    state = jax.tree.map(lambda a, e: jnp.zeros_like(a) + jnp.asarray(e, a.dtype), part, identity)
-
-    def one(lap, state):
-        return combine(
-            state, jax.tree.map(lambda a: lax.dynamic_index_in_dim(a, lap, 0, False), gathered)
-        )
-
-    return lax.fori_loop(0, place, one, state)
-
-
-def link_pairs(earlier, later):
-    return (earlier[0] * later[0], later[0] * earlier[1] + later[1])
-
-
-def mixer_conv(padded, conv_weight, conv_bias, length):
-    conv_sum = conv_bias[None, :] + conv_weight[0][None, :] * padded[0:length]
-    for offset in range(1, conv_weight.shape[0]):
-        conv_sum = conv_sum + conv_weight[offset][None, :] * padded[offset : offset + length]
-    return jax.nn.silu(conv_sum).astype(jnp.bfloat16)
 
 
 def remote(src, dst, send_sem, recv_sem, device):
@@ -437,6 +405,405 @@
     )(normed, stream, gates, spread_a, spread_b, pick_a, pick_b, fetch, w_gate, w_up, w_down)
 
 
+LOG2E = 1.4426950408889634
+
+
+def mixer_kernel(
+    mixer_in,
+    gate_in,
+    conv_weight,
+    conv_bias,
+    x_proj,
+    dt_proj,
+    dt_bias,
+    decay_rate,
+    skip,
+    out_proj,
+    residual,
+    gain,
+    router,
+    expert_ids,
+    stream_out,
+    normed_out,
+    gates_out,
+    rim,
+    padded,
+    conv_out,
+    part,
+    parts,
+    proj,
+    bc_v,
+    bc_s,
+    step_t,
+    drive_t,
+    cum_t,
+    y_t,
+    rate_t,
+    enter_t,
+    fin_own,
+    fin_y,
+    sum_y,
+    fin_x,
+    sum_x,
+    opg,
+    ga,
+    zs,
+    rz,
+    ms,
+    mo,
+    h_sem,
+    a_send,
+    a_recv,
+    b_send,
+    b_recv,
+    o_send,
+    o_recv,
+    c_send,
+    c_recv,
+    g_send,
+    g_recv,
+    z_send,
+    z_recv,
+    m_send,
+    m_recv,
+    l_sem,
+):
+    ctx, exp = lax.axis_index("ctx"), lax.axis_index("exp")
+    mx, my = ctx // 4, ctx % 4
+    every = slice(None)
+
+    def along_x(d):
+        return {"ctx": wrap(mx + d, 4) * 4 + my}
+
+    def along_y(d):
+        return {"ctx": mx * 4 + wrap(my + d, 4)}
+
+    def peer(d):
+        return {"exp": lax.rem(exp + d, 8)}
+
+    behind, ahead = {"ctx": lax.rem(ctx + 15, 16)}, {"ctx": lax.rem(ctx + 1, 16)}
+    greet(
+        [behind, ahead]
+        + [along_x(d) for d in (1, 2, -1)]
+        + [along_y(d) for d in (1, 2, -1)]
+        + [peer(d) for d in range(1, 8)]
+    )
+    sent = []
+
+    def send(src, dst, ss, rs, device):
+        c = remote(src, dst, ss, rs, device)
+        c.start()
+        sent.append(c)
+        return c
+
+    halo = send(mixer_in.at[pl.ds(112, 16)], rim, h_sem.at[0], h_sem.at[1], ahead)
+    columns = [
+        send(out_proj, opg.at[my], o_send.at[0], o_recv.at[0], along_y(1)),
+        send(out_proj, opg.at[my], o_send.at[1], o_recv.at[1], along_y(-1)),
+    ]
+    opg[pl.ds(my, 1)] = out_proj[...][None]
+    padded[pl.ds(8, 128), :] = mixer_in[...].astype(F32)
+    for g in range(8):
+        rate_t[pl.ds(g, 16, stride=8), :] = decay_rate[:, g * 128 : (g + 1) * 128] * (-LOG2E)
+    halo.wait_recv()
+    keep = jnp.where(ctx > 0, 1.0, 0.0).astype(F32)
+    padded[pl.ds(0, 8), :] = rim[pl.ds(0, 16), :].astype(F32)[8:] * keep
+    for g in range(8):
+        cols = pl.ds(g * 128, 128)
+        total = conv_bias[:, cols] + conv_weight[0:1, cols] * padded[pl.ds(5, 128), cols]
+        for k in range(1, 4):
+            total = total + conv_weight[k : k + 1, cols] * padded[pl.ds(5 + k, 128), cols]
+        conv_out[:, cols] = (total * jax.nn.sigmoid(total)).astype(BF16)
+
+    part[...] = dot(conv_out[...], x_proj[...]).reshape(8, 16, 544)
+    scatter = [
+        send(part.at[lax.rem(exp + d, 8)], parts.at[exp], a_send.at[d], a_recv.at[d], peer(d))
+        for d in range(1, 8)
+    ]
+    parts[pl.ds(exp, 1)] = part[pl.ds(exp, 1)]
+    for c in scatter:
+        c.wait_recv()
+    total = parts[0]
+    for j in range(1, 8):
+        total = total + parts[j]
+    proj[pl.ds(exp, 1)] = total[None]
+    gather = [
+        send(proj.at[exp], proj.at[exp], b_send.at[d], b_recv.at[d], peer(d)) for d in range(1, 8)
+    ]
+    top, low = pl.ds(0, 512), pl.ds(512, 512)
+    left, right = wrap(my - 1, 4), wrap(my + 1, 4)
+    columns[0].wait_recv()
+    columns.append(
+        send(opg.at[left, top], opg.at[left, top], o_send.at[2], o_recv.at[2], along_y(1))
+    )
+    columns[1].wait_recv()
+    columns.append(
+        send(opg.at[right, low], opg.at[right, low], o_send.at[3], o_recv.at[3], along_y(-1))
+    )
+    for c in gather:
+        c.wait_recv()
+    bc_v[:, pl.ds(0, 32)] = proj[:, :, pl.ds(512, 32)].reshape(128, 32)
+    scalars = pltpu.make_async_copy(bc_v, bc_s, l_sem.at[0])
+    scalars.start()
+    step_low = proj[:, :, pl.ds(0, 512)].reshape(128, 512).astype(BF16)
+    for j in range(4):
+        cols = pl.ds(j * 256, 256)
+        raw = dot(step_low, dt_proj[:, cols]) + dt_bias[:, cols]
+        step = jnp.maximum(raw, 0.0) + jnp.log1p(jnp.exp(-jnp.abs(raw)))
+        drive = step * conv_out[:, cols].astype(F32)
+        for i in range(2):
+            rows = pl.ds(j * 2 + i, 128, stride=8)
+            step_t[rows, :] = step[:, i * 128 : (i + 1) * 128]
+            drive_t[rows, :] = drive[:, i * 128 : (i + 1) * 128]
+    scalars.wait()
+
+    rates = [rate_t[pl.ds(n * 8, 8), :] for n in range(16)]
+    zero = jnp.zeros((8, 128), F32)
+
+    def scan_step(t, carry):
+        states, running = carry
+        rows = pl.ds(pl.multiple_of(t * 8, 8), 8)
+        s, d = step_t[rows, :], drive_t[rows, :]
+        outs = [zero, zero]
+        after = []
+        for n in range(16):
+            h = jnp.exp2(rates[n] * s) * states[n] + bc_s[t, n] * d
+            outs[n % 2] = outs[n % 2] + bc_s[t, 16 + n] * h
+            after.append(h)
+        running = running + s
+        y_t[rows, :] = outs[0] + outs[1]
+        cum_t[rows, :] = running
+        return (tuple(after), running)
+
+    states, running = lax.fori_loop(0, 128, scan_step, ((zero,) * 16, zero), unroll=2)
+
+    def exchange(finals, total, fin, sums, place, base, step):
+        for n in range(16):
+            fin_own[base // 6, pl.ds(n * 8, 8), :] = finals[n].astype(BF16)
+        sums[pl.ds(place, 1)] = total[None]
+        fin[pl.ds(place, 1)] = fin_own[base // 6][None]
+        moves = []
+        for k, d in enumerate((1, -1, 2)):
+            s, r = base + 2 * k, base + 2 * k + 1
+            moves.append(
+                send(fin_own.at[base // 6], fin.at[place], c_send.at[s], c_recv.at[s], step(d))
+            )
+            moves.append(send(sums.at[place], sums.at[place], c_send.at[r], c_recv.at[r], step(d)))
+        for c in moves:
+            c.wait_recv()
+
+    exchange(states, running, fin_y, sum_y, my, 0, along_y)
+    before, row_total = zero, zero
+    for v in range(4):
+        before = before + jnp.where(v < my, 1.0, 0.0).astype(F32) * sum_y[v]
+        row_total = row_total + sum_y[v]
+    row_final = []
+    for n in range(16):
+        entering, whole = zero, zero
+        for v in range(4):
+            own = fin_y[v, pl.ds(n * 8, 8), :].astype(F32)
+            decay = jnp.exp2(rates[n] * sum_y[v])
+            entering = jnp.where(v < my, decay * entering + own, entering)
+            whole = decay * whole + own
+        enter_t[pl.ds(n * 8, 8), :] = entering
+        row_final.append(whole)
+    exchange(row_final, row_total, fin_x, sum_x, mx, 6, along_x)
+    for n in range(16):
+        entering = zero
+        for u in range(4):
+            own = fin_x[u, pl.ds(n * 8, 8), :].astype(F32)
+            decay = jnp.exp2(rates[n] * sum_x[u])
+            entering = jnp.where(u < mx, decay * entering + own, entering)
+        rows = pl.ds(n * 8, 8)
+        enter_t[rows, :] = enter_t[rows, :] + jnp.exp2(rates[n] * before) * entering
+
+    def add_entering(t, carry):
+        rows = pl.ds(pl.multiple_of(t * 8, 8), 8)
+        c = cum_t[rows, :]
+        outs = [y_t[rows, :], zero]
+        for n in range(16):
+            outs[n % 2] = outs[n % 2] + bc_s[t, 16 + n] * (jnp.exp2(rates[n] * c) * entered[n])
+        y_t[rows, :] = outs[0] + outs[1]
+        return carry
+
+    entered = [enter_t[pl.ds(n * 8, 8), :] for n in range(16)]
+    moves = []
+    for half in range(2):
+        lax.fori_loop(half * 64, half * 64 + 64, add_entering, 0, unroll=2)
+        rows = pl.ds(half * 64, 64)
+        for g in range(8):
+            cols = pl.ds(g * 128, 128)
+            y = y_t[pl.ds(half * 512 + g, 64, stride=8), :]
+            y = y + skip[:, cols] * conv_out[rows, cols].astype(F32)
+            z = gate_in[rows, cols].astype(F32)
+            ga[pl.ds(mx, 1), rows, cols] = (y * (z * jax.nn.sigmoid(z))).astype(BF16)[None]
+        place = ga.at[mx, rows]
+        for k, d in enumerate((1, -1)):
+            s = half * 2 + k
+            moves.append(send(place, place, g_send.at[s], g_recv.at[s], along_x(d)))
+
+    def project(u):
+        for v in range(4):
+            cols = pl.ds(v * 256, 256)
+            out = dot(ga[u], opg[v])
+            zs[pl.ds(u, 1), :, :, cols] = out.astype(BF16).reshape(1, 8, 16, 256)
+        rz[pl.ds(u, 1), pl.ds(exp, 1)] = zs[pl.ds(u, 1), pl.ds(exp, 1)]
+
+    def scatter_group(k, u):
+        return [
+            send(zs.at[u, lax.rem(exp + d, 8)], rz.at[u, exp], z_send.at[k, d], z_recv.at[k, d], peer(d))
+            for d in range(1, 8)
+        ]
+
+    for c in columns[2:]:
+        c.wait_recv()
+    left, right, far = wrap(mx - 1, 4), wrap(mx + 1, 4), wrap(mx + 2, 4)
+    top, low = pl.ds(0, 64), pl.ds(64, 64)
+    project(mx)
+    groups = [scatter_group(0, mx)]
+    moves[0].wait_recv()
+    moves.append(send(ga.at[left, top], ga.at[left, top], g_send.at[4], g_recv.at[4], along_x(1)))
+    moves[1].wait_recv()
+    moves[3].wait_recv()
+    moves.append(send(ga.at[right, low], ga.at[right, low], g_send.at[5], g_recv.at[5], along_x(-1)))
+    moves[2].wait_recv()
+    for k, u in ((1, left), (2, right)):
+        project(u)
+        groups.append(scatter_group(k, u))
+    moves[4].wait_recv()
+    moves[5].wait_recv()
+    project(far)
+    groups.append(scatter_group(3, far))
+    backs = []
+    for k, (u, d) in enumerate(((mx, 0), (left, -1), (right, 1), (far, 2))):
+        for c in groups[k]:
+            c.wait_recv()
+        total = rz[u, 0].astype(F32)
+        for j in range(1, 8):
+            total = total + rz[u, j].astype(F32)
+        if d == 0:
+            mo[pl.ds(mx, 1)] = total[None]
+        else:
+            ms[k - 1] = total
+            backs.append(send(ms.at[k - 1], mo.at[mx], m_send.at[k], m_recv.at[k], along_x(d)))
+    for c in backs:
+        c.wait_recv()
+
+    squares = jnp.zeros((16, 1), F32)
+    for u in range(4):
+        cols = pl.ds(u * 1024, 1024)
+        rows = residual[:, cols].astype(F32) + mo[u]
+        stream_out[:, cols] = rows
+        squares = squares + jnp.sum(rows * rows, axis=1, keepdims=True)
+    scale = lax.rsqrt(squares * (1.0 / 4096.0) + 1e-06)
+    logits = jnp.zeros((16, 8), F32)
+    for u in range(4):
+        cols = pl.ds(u * 1024, 1024)
+        rows = (stream_out[:, cols] * scale * gain[:, cols]).astype(BF16)
+        normed_out[:, cols] = rows
+        logits = logits + dot(rows, router[cols, :])
+    ids = expert_ids[...]
+    lanes = lax.broadcasted_iota(jnp.int32, (16, 8), 1)
+    signs = jnp.where(ids[:, 0:1] == lanes, 1.0, 0.0) - jnp.where(ids[:, 1:2] == lanes, 1.0, 0.0)
+    first = jax.nn.sigmoid(jnp.sum(logits * signs, axis=1, keepdims=True))
+    gates_out[:, 0:1] = first
+    gates_out[:, 1:2] = 1.0 - first
+    for c in sent:
+        c.wait_send()
+
+
+def mixer_layer(
+    mixer_in,
+    gate_in,
+    conv_weight,
+    conv_bias,
+    x_proj,
+    dt_proj,
+    dt_bias,
+    decay_rate,
+    skip,
+    out_proj,
+    residual,
+    gain,
+    router,
+    expert_ids,
+):
+    vmem = pl.BlockSpec(memory_space=pltpu.VMEM)
+    dma = pltpu.SemaphoreType.DMA
+    return pl.pallas_call(
+        mixer_kernel,
+        out_shape=[
+            jax.ShapeDtypeStruct((16, 4096), F32),
+            jax.ShapeDtypeStruct((16, 4096), BF16),
+            jax.ShapeDtypeStruct((16, 2), F32),
+        ],
+        in_specs=[vmem] * 14,
+        out_specs=[vmem] * 3,
+        scratch_shapes=[
+            pltpu.VMEM((16, 1024), BF16),
+            pltpu.VMEM((136, 1024), F32),
+            pltpu.VMEM((128, 1024), BF16),
+            pltpu.VMEM((8, 16, 544), F32),
+            pltpu.VMEM((8, 16, 544), F32),
+            pltpu.VMEM((8, 16, 544), F32),
+            pltpu.VMEM((128, 128), F32),
+            pltpu.SMEM((128, 128), F32),
+            pltpu.VMEM((1024, 128), F32),
+            pltpu.VMEM((1024, 128), F32),
+            pltpu.VMEM((1024, 128), F32),
+            pltpu.VMEM((1024, 128), F32),
+            pltpu.VMEM((128, 128), F32),
+            pltpu.VMEM((128, 128), F32),
+            pltpu.VMEM((2, 128, 128), BF16),
+            pltpu.VMEM((4, 128, 128), BF16),
+            pltpu.VMEM((4, 8, 128), F32),
+            pltpu.VMEM((4, 128, 128), BF16),
+            pltpu.VMEM((4, 8, 128), F32),
+            pltpu.VMEM((4, 1024, 256), BF16),
+            pltpu.VMEM((4, 128, 1024), BF16),
+            pltpu.VMEM((4, 8, 16, 1024), BF16),
+            pltpu.VMEM((4, 8, 16, 1024), BF16),
+            pltpu.VMEM((3, 16, 1024), F32),
+            pltpu.VMEM((4, 16, 1024), F32),
+            dma((2,)),
+            dma((8,)),
+            dma((8,)),
+            dma((8,)),
+            dma((8,)),
+            dma((4,)),
+            dma((4,)),
+            dma((12,)),
+            dma((12,)),
+            dma((6,)),
+            dma((6,)),
+            dma((4, 8)),
+            dma((4, 8)),
+            dma((4,)),
+            dma((4,)),
+            dma((1,)),
+        ],
+        compiler_params=pltpu.CompilerParams(
+            collective_id=0, has_side_effects=True, vmem_limit_bytes=VMEM_LIMIT
+        ),
+        cost_estimate=pl.CostEstimate(flops=1_500_000_000, bytes_accessed=5_000_000, transcendentals=0),
+    )(
+        mixer_in,
+        gate_in,
+        conv_weight,
+        conv_bias[None],
+        x_proj,
+        dt_proj,
+        dt_bias[None],
+        decay_rate,
+        skip[None],
+        out_proj,
+        residual,
+        gain[None],
+        router,
+        expert_ids,
+    )
+
+
 def shards(
     mixer_in,
     gate_in,
@@ -456,97 +823,23 @@
     w_down,
     expert_ids,
 ):
-    length, channels = mixer_in.shape
-    kernel_width = conv_weight.shape[0]
-    rim_rows = from_behind(mixer_in[length - (kernel_width - 1) :], "ctx", 1)
-    padded = jnp.concatenate([rim_rows, mixer_in], axis=0).astype(jnp.float32)
-    conv_out = mixer_conv(padded, conv_weight, conv_bias, length)
-    projected = lax.psum(jnp.dot(conv_out, x_proj, preferred_element_type=jnp.float32), "exp")
-    rank_width = dt_proj.shape[0]
-    state_count = (projected.shape[1] - rank_width) // 2
-    step_low = projected[:, :rank_width].astype(jnp.bfloat16)
-    b_mat = projected[:, rank_width : rank_width + state_count]
-    c_mat = projected[:, rank_width + state_count :]
-    step_size = jax.nn.softplus(
-        jnp.dot(step_low, dt_proj, preferred_element_type=jnp.float32) + dt_bias[None, :]
+    stream, normed, gates = mixer_layer(
+        mixer_in,
+        gate_in,
+        conv_weight,
+        conv_bias,
+        x_proj,
+        dt_proj,
+        dt_bias,
+        decay_rate,
+        skip,
+        out_proj,
+        residual,
+        gain,
+        router,
+        expert_ids,
     )
-    x_value = conv_out.astype(jnp.float32)
-    drive = step_size * x_value
-    total_step = jnp.sum(step_size, axis=0)
-    block_width = 256
-    block_count = channels // block_width
-    group_len = 32
-    group_count = length // group_len
-    b_groups = b_mat.reshape(group_count, group_len, state_count)
-    c_groups = c_mat.reshape(group_count, group_len, state_count)
-
-    def to_blocks(values):
-        return values.reshape(values.shape[0], block_count, block_width).transpose(1, 0, 2)
-
-    def local_scan(pieces):
-        step_b, drive_b, rate_b = pieces
-        steps_g = step_b.reshape(group_count, group_len, block_width)
-        running = jnp.cumsum(steps_g, axis=1)
-        exponent = rate_b[None, None] * running[:, :, None, :]
-        inputs = b_groups[:, :, :, None] * drive_b.reshape(group_count, group_len, 1, block_width)
-        decay_in = jnp.exp(-exponent)
-        inner = decay_in * jnp.cumsum(jnp.exp(exponent) * inputs, axis=1)
-        group_decay = decay_in[:, -1]
-        group_final = inner[:, -1]
-
-        def carry_step(state, parts):
-            decay_part, final_part = parts
-            return (decay_part * state + final_part, state)
-
-        last_state, entering = lax.scan(
-            carry_step,
-            jnp.zeros((state_count, block_width), jnp.float32),
-            (group_decay, group_final),
-        )
-        states = inner + decay_in * entering[:, None]
-        local_out = jnp.sum(c_groups[:, :, :, None] * states, axis=2).reshape(length, block_width)
-        return (local_out, last_state)
-
-    local_blocks, final_blocks = lax.map(
-        local_scan, (to_blocks(step_size), to_blocks(drive), to_blocks(decay_rate))
-    )
-    b_total = final_blocks.transpose(1, 0, 2).reshape(state_count, channels)
-    a_total = jnp.exp(-decay_rate * total_step[None, :])
-    carry_in = entering_2(
-        (a_total, b_total), "ctx", link_pairs, (jnp.ones_like(a_total), jnp.zeros_like(b_total))
-    )[1]
-    cumulative = jnp.cumsum(step_size, axis=0)
-
-    def carried(pieces):
-        cum_b, rate_b, carry_b = pieces
-        weight = jnp.exp(-rate_b[None] * cum_b[:, None, :]) * carry_b[None]
-        return jnp.sum(c_mat[:, :, None] * weight, axis=1)
-
-    carry_blocks = lax.map(
-        carried, (to_blocks(cumulative), to_blocks(decay_rate), to_blocks(carry_in))
-    )
-    scan_out = (local_blocks + carry_blocks).transpose(1, 0, 2).reshape(length, channels) + skip[
-        None, :
-    ] * x_value
-    gated = (scan_out * jax.nn.silu(gate_in.astype(jnp.float32))).astype(jnp.bfloat16)
-    tok_rows = residual.shape[0]
-    exp_count = lax.axis_size("exp")
-    full_out = lax.all_gather(out_proj, "ctx", axis=1, tiled=True)
-    mamba_out = lax.psum_scatter(
-        jnp.dot(gated, full_out, preferred_element_type=jnp.float32),
-        "exp",
-        scatter_dimension=0,
-        tiled=True,
-    )
-    stream = residual.astype(jnp.float32) + mamba_out
-    normed = (
-        stream * lax.rsqrt(jnp.mean(stream * stream, axis=1, keepdims=True) + 1e-06) * gain[None, :]
-    ).astype(jnp.bfloat16)
-    logits = jnp.dot(normed, router, preferred_element_type=jnp.float32)
-    picked = jnp.take_along_axis(logits, expert_ids, axis=1)
-    first_gate = jax.nn.sigmoid(picked[:, 0] - picked[:, 1])
-    gate_weights = jnp.stack([first_gate, 1.0 - first_gate], axis=1)
-    return expert_layer(normed, stream, gate_weights, expert_ids, w_gate, w_up, w_down)
+    return expert_layer(normed, stream, gates, expert_ids, w_gate, w_up, w_down)
 
 
 def solution(mesh):

time: 438 us -> 172 us (0.39)
  waiting for transfers between devices: 246 us -> 0 us
  Pallas kernels: 99 us -> 161 us
  other arithmetic: 37.2 us -> 1.71 us
  local copies, waits for them, and re-layouts: 26.7 us -> 8.58 us
  between operations: 13.5 us -> 0.08 us
  matrix products: 8.99 us -> 0 us
    all_gather x3 -> x0, waiting for transfers between devices: 156 us -> none  [the longest x2 82.8 us: entering_2(): gathered = jax.tree.map(lambda a: lax.all_gather(a, axis), part)]
    pallas_call x0 -> x1, Pallas kernels: none -> 63.4 us  [mixer_layer(): pl.pallas_call(mixer_kernel, out_shape=[jax.ShapeDtypeStruct((16, 4096),...]
    psum x1 -> x0, waiting for transfers between devices: 61.2 us -> none  [shards(): lax.psum(jnp.dot(conv_out, x_proj, preferred_element_type=jnp.float32), '...]
    reduce_scatter x1 -> x0, waiting for transfers between devices: 27.8 us -> none  [shards(): lax.psum_scatter(jnp.dot(gated, full_out, preferred_element_type=jnp.floa...]
    reduce_sum x9 -> x0, other arithmetic: 10.3 us -> none  [the longest x4 6.44 us: local_scan(): jnp.sum(c_groups[:, :, :, None] * states, axis=2)]
    dynamic_update_slice x16 -> x0, other arithmetic: 9.64 us -> none  [shards(): lax.map(local_scan, (to_blocks(step_size), to_blocks(drive), to_blocks(de...]
    dot_general x4 -> x0, matrix products: 8.99 us -> none  [the longest x1 6.1 us: shards(): jnp.dot(gated, full_out, preferred_element_type=jnp.float32)]
    another operation x15 -> x0, other arithmetic: 7.4 us -> none  [the longest x4 6.07 us: local_scan(): inner = decay_in * jnp.cumsum(jnp.exp(exponent) * inputs, axis=1)]
  transfers between devices with their start and end apart: 6 -> 0, of which waited for: 5 -> 0; matrix products, arithmetic and copies ran while one was open for 3% -> 0% of each run, Pallas kernels for 0% -> 0%
where the time goes in v2:
time: 172 us; the launch traced here: 171 us
  Pallas kernels  161 us (94%)
  local copies, waits for them, and re-layouts  8.58 us (5%)
    pallas_call x1, Pallas kernels, expert_layer(): pl.pallas_call(moe_kernel, out_shape=jax.ShapeDtypeStruct((16, 4096), BF1...  97.7 us
    pallas_call x1, Pallas kernels, mixer_layer(): pl.pallas_call(mixer_kernel, out_shape=[jax.ShapeDtypeStruct((16, 4096),...  63.4 us
    unnamed x8, local copies, waits for them, and re-layouts  7.53 us

profile of v2, /device:TPU:1, one launch (start us, length us, event | category | flops | bytes accessed | tf_op | source)
XLA Modules:
  0.0 171.4 jit_solution(6675378434604865092)
XLA Ops:
  0.0 0.0 copy-start.1
  0.0 2.4 %copy.47.x_proj = bf16[1024,544]{1,0:T(8,128)(2,1)} copy(bf16[1024,544]{0,1:T(8,128)(2,1)} %param.23) | data formatting | bytes 2228224 | tf_op args[4]
  2.4 2.2 %copy.48.router = bf16[4096,8]{1,0:T(8,128)(2,1)} copy(bf16[4096,8]{0,1:T(8,128)(2,1)} %param.31) | data formatting | bytes 131072 | tf_op args[12]
  4.6 1.4 copy.49.expert_ids
  6.0 63.4 %shard_map.181 = (f32[16,4096]{1,0:T(8,128)}, bf16[16,4096]{1,0:T(8,128)(2,1)}, f32[16,2]{1,0:T(8,128)}) custom-call(bf16[128,1024]{1,0:T(8,128)(2,1)} %mixer_in.1, bf16[128,1024]{1,0:T(8,128)(2,1)} %gate_in.1, f32[4,1024]{1,0:T(4,128)} %conv_weight.1, f32[1,1024]{1,0:T(1,128)} %bitcast.17, bf16[1024,544]{1,0:T(8,128)(2,1)} %copy.47.x_proj, ...), custom_call_target="tpu_custom_call" | custom-call | flops 1500000000 | bytes 5000000 | tf_op jit(solution)/shard_map/pallas_call | solution.py:733
  69.4 0.8 eq.95
  70.1 0.1 fusion.2
  70.2 0.1 reduce_window_sum.11
  70.3 0.2 select_reduce_fusion
  70.5 0.1 reduce_sum.12
  70.5 0.1 copy.51
  70.6 0.0 copy-done.1
  70.7 0.0 copy-start
  70.7 0.6 pad_maximum_fusion.spread_b
  71.3 0.1 fusion.6
  71.4 0.1 slice.30
  71.5 0.1 maximum_bitcast_fusion
  71.6 0.6 pad_maximum_fusion.1.fetch
  72.2 0.0 copy-done
  72.2 97.7 %shard_map.182 = bf16[16,4096]{1,0:T(8,128)(2,1)} custom-call(bf16[16,4096]{1,0:T(8,128)(2,1)} %get-tuple-element.8.normed, f32[16,4096]{1,0:T(8,128)} %get-tuple-element.9.stream, f32[16,2]{1,0:T(8,128)} %get-tuple-element.10.gates, bf16[128,16]{1,0:T(8,128)(2,1)} %copy-done, bf16[128,16]{1,0:T(8,128)(2,1)} %pad_maximum_fusion.spread_b, ...), custom_call_target="tpu_custom_call" | custom-call | flops 12000000000 | bytes 19000000 | tf_op jit(solution)/shard_map/pallas_call | solution.py:368
  169.8 1.6 copy.53
  (7 shorter events, 0.1 us)
Async XLA Ops:
  0.0 70.6 %copy-start.1 = (s32[16,2]{0,1:T(2,128)S(1)}, s32[16,2]{0,1:T(2,128)}, u32[]{:S(2)}) copy-start(s32[16,2]{0,1:T(2,128)} %param.35) | copy-start | bytes 388
  70.7 1.5 copy-start

commit v3 on v1

v3 whole, which is shorter than its diff:
```python
import jax
import jax.numpy as jnp
import numpy as np
from jax import lax
from jax.experimental import pallas as pl
from jax.experimental.pallas import tpu as pltpu
from jax.sharding import PartitionSpec as P

F32 = jnp.float32
BF16 = jnp.bfloat16
VMEM_LIMIT = 60 * 1024 * 1024


def remote(src, dst, send_sem, recv_sem, device):
    return pltpu.make_async_remote_copy(
        src_ref=src,
        dst_ref=dst,
        send_sem=send_sem,
        recv_sem=recv_sem,
        device_id=device,
        device_id_type=pl.DeviceIdType.MESH,
    )


def greet(devices):
    barrier = pltpu.get_barrier_semaphore()
    for device in devices:
        pl.semaphore_signal(barrier, inc=1, device_id=device, device_id_type=pl.DeviceIdType.MESH)
    pl.semaphore_wait(barrier, len(devices))


def wrap(index, count):
    return lax.rem(index + count, count)


def dot(a, b):
    return jnp.dot(a, b, preferred_element_type=F32)


def dot_t(a, b):
    return lax.dot_general(a, b, (((1,), (1,)), ((), ())), preferred_element_type=F32)


class Half:
    def __init__(self, half, mx, my):
        self.half = half
        self.mx, self.my = mx, my
        self.p, self.q = (mx, my) if half == 0 else (my, mx)

    def one(self, step):
        p = wrap(self.p + step, 4)
        return {"ctx": p * 4 + self.my if self.half == 0 else self.mx * 4 + p}

    def two(self, step):
        q = wrap(self.q + step, 4)
        return {"ctx": self.mx * 4 + q if self.half == 0 else q * 4 + self.my}

    def unit(self, u, v):
        return (u, v) if self.half == 0 else (v, u)

    def group(self, v):
        return (slice(None), v) if self.half == 0 else (v, slice(None))


LOG2E = 1.4426950408889634

INPUTS = (
    "mixer_in",
    "gate_in",
    "conv_weight",
    "conv_bias",
    "x_proj",
    "dt_proj",
    "dt_bias",
    "decay_rate",
    "skip",
    "out_proj",
    "residual",
    "gain",
    "router",
    "expert_ids",
    "w_gate",
    "w_up",
    "w_down",
    "pick_a",
    "pick_b",
)

SCRATCH = {
    "stream": pltpu.VMEM((16, 4096), F32),
    "normed": pltpu.VMEM((16, 4096), BF16),
    "spread": pltpu.VMEM((2, 128, 16), BF16),
    "fetch": pltpu.VMEM((2, 2, 128, 16), BF16),
    "rim": pltpu.VMEM((16, 1024), BF16),
    "padded": pltpu.VMEM((136, 1024), F32),
    "conv_out": pltpu.VMEM((128, 1024), BF16),
    "part": pltpu.VMEM((8, 16, 544), F32),
    "parts": pltpu.VMEM((8, 16, 544), F32),
    "low_rank": pltpu.VMEM((8, 16, 512), BF16),
    "maps": pltpu.VMEM((8, 16, 128), F32),
    "bc_s": pltpu.SMEM((8, 16, 128), F32),
    "step_t": pltpu.VMEM((1024, 128), F32),
    "drive_t": pltpu.VMEM((1024, 128), F32),
    "cum_t": pltpu.VMEM((1024, 128), F32),
    "y_t": pltpu.VMEM((1024, 128), F32),
    "rate_t": pltpu.VMEM((128, 128), F32),
    "enter_t": pltpu.VMEM((128, 128), F32),
    "fin_own": pltpu.VMEM((2, 128, 128), BF16),
    "fin_y": pltpu.VMEM((4, 128, 128), BF16),
    "sum_y": pltpu.VMEM((4, 8, 128), F32),
    "fin_x": pltpu.VMEM((4, 128, 128), BF16),
    "sum_x": pltpu.VMEM((4, 8, 128), F32),
    "opg": pltpu.VMEM((4, 1024, 256), BF16),
    "ga": pltpu.VMEM((4, 128, 1024), BF16),
    "zs": pltpu.VMEM((4, 8, 16, 1024), BF16),
    "rz": pltpu.VMEM((4, 8, 16, 1024), BF16),
    "ms": pltpu.VMEM((3, 16, 1024), F32),
    "mo": pltpu.VMEM((4, 16, 1024), F32),
    "h_sem": pltpu.SemaphoreType.DMA((2,)),
    "a_send": pltpu.SemaphoreType.DMA((8,)),
    "a_recv": pltpu.SemaphoreType.DMA((8,)),
    "b_send": pltpu.SemaphoreType.DMA((16,)),
    "b_recv": pltpu.SemaphoreType.DMA((16,)),
    "o_send": pltpu.SemaphoreType.DMA((4,)),
    "o_recv": pltpu.SemaphoreType.DMA((4,)),
    "c_send": pltpu.SemaphoreType.DMA((12,)),
    "c_recv": pltpu.SemaphoreType.DMA((12,)),
    "g_send": pltpu.SemaphoreType.DMA((6,)),
    "g_recv": pltpu.SemaphoreType.DMA((6,)),
    "z_send": pltpu.SemaphoreType.DMA((4, 8)),
    "z_recv": pltpu.SemaphoreType.DMA((4, 8)),
    "m_send": pltpu.SemaphoreType.DMA((4,)),
    "m_recv": pltpu.SemaphoreType.DMA((4,)),
    "l_sem": pltpu.SemaphoreType.DMA((1,)),
    "go": pltpu.VMEM((8, 16, 2048), BF16),
    "rcv": pltpu.VMEM((8, 16, 2048), BF16),
    "rback": pltpu.VMEM((8, 16, 2048), BF16),
    "xa": pltpu.VMEM((4, 4, 40, 2048), BF16),
    "xb": pltpu.VMEM((4, 4, 40, 2048), BF16),
    "wgu": pltpu.VMEM((4096, 1536), BF16),
    "wd": pltpu.VMEM((768, 4096), BF16),
    "lhs": pltpu.VMEM((160, 2048), BF16),
    "acc": pltpu.VMEM((4, 4, 40, 1536), F32),
    "hid": pltpu.VMEM((4, 4, 40, 768), BF16),
    "oa": pltpu.VMEM((4, 4, 40, 2048), BF16),
    "ob": pltpu.VMEM((4, 4, 40, 2048), BF16),
    "far": pltpu.VMEM((2, 2, 4, 40, 1024), BF16),
    "near": pltpu.VMEM((2, 2, 4, 40, 2048), BF16),
    "tot": pltpu.VMEM((2, 4, 40, 2048), BF16),
    "far2": pltpu.VMEM((2, 2, 40, 1024), BF16),
    "near2": pltpu.VMEM((2, 2, 40, 2048), BF16),
    "w_sem": pltpu.SemaphoreType.DMA((3,)),
    "d_send": pltpu.SemaphoreType.DMA((8,)),
    "d_recv": pltpu.SemaphoreType.DMA((8,)),
    "u_send": pltpu.SemaphoreType.DMA((2, 5, 4)),
    "u_recv": pltpu.SemaphoreType.DMA((2, 5, 4)),
    "s_send": pltpu.SemaphoreType.DMA((2, 2, 6)),
    "s_recv": pltpu.SemaphoreType.DMA((2, 2, 6)),
    "r_send": pltpu.SemaphoreType.DMA((8,)),
    "r_recv": pltpu.SemaphoreType.DMA((8,)),
}


def mixer(r, ctx, exp, mx, my):
    mixer_in = r["mixer_in"]
    gate_in = r["gate_in"]
    conv_weight = r["conv_weight"]
    conv_bias = r["conv_bias"]
    x_proj = r["x_proj"]
    dt_proj = r["dt_proj"]
    dt_bias = r["dt_bias"]
    decay_rate = r["decay_rate"]
    skip = r["skip"]
    out_proj = r["out_proj"]
    residual = r["residual"]
    gain = r["gain"]
    router = r["router"]
    expert_ids = r["expert_ids"]
    stream = r["stream"]
    normed = r["normed"]
    rim = r["rim"]
    padded = r["padded"]
    conv_out = r["conv_out"]
    part = r["part"]
    parts = r["parts"]
    low_rank = r["low_rank"]
    maps = r["maps"]
    bc_s = r["bc_s"]
    step_t = r["step_t"]
    drive_t = r["drive_t"]
    cum_t = r["cum_t"]
    y_t = r["y_t"]
    rate_t = r["rate_t"]
    enter_t = r["enter_t"]
    fin_own = r["fin_own"]
    fin_y = r["fin_y"]
    sum_y = r["sum_y"]
    fin_x = r["fin_x"]
    sum_x = r["sum_x"]
    opg = r["opg"]
    ga = r["ga"]
    zs = r["zs"]
    rz = r["rz"]
    ms = r["ms"]
    mo = r["mo"]
    h_sem = r["h_sem"]
    a_send = r["a_send"]
    a_recv = r["a_recv"]
    b_send = r["b_send"]
    b_recv = r["b_recv"]
    o_send = r["o_send"]
    o_recv = r["o_recv"]
    c_send = r["c_send"]
    c_recv = r["c_recv"]
    g_send = r["g_send"]
    g_recv = r["g_recv"]
    z_send = r["z_send"]
    z_recv = r["z_recv"]
    m_send = r["m_send"]
    m_recv = r["m_recv"]
    l_sem = r["l_sem"]
    every = slice(None)

    def along_x(d):
        return {"ctx": wrap(mx + d, 4) * 4 + my}

    def along_y(d):
        return {"ctx": mx * 4 + wrap(my + d, 4)}

    def peer(d):
        return {"exp": lax.rem(exp + d, 8)}

    ahead = {"ctx": lax.rem(ctx + 1, 16)}
    sent = []

    def send(src, dst, ss, rs, device):
        c = remote(src, dst, ss, rs, device)
        c.start()
        sent.append(c)
        return c

    halo = send(mixer_in.at[pl.ds(112, 16)], rim, h_sem.at[0], h_sem.at[1], ahead)
    columns = [
        send(out_proj, opg.at[my], o_send.at[0], o_recv.at[0], along_y(1)),
        send(out_proj, opg.at[my], o_send.at[1], o_recv.at[1], along_y(-1)),
    ]
    opg[pl.ds(my, 1)] = out_proj[...][None]
    padded[pl.ds(8, 128), :] = mixer_in[...].astype(F32)
    for g in range(8):
        rate_t[pl.ds(g, 16, stride=8), :] = decay_rate[:, g * 128 : (g + 1) * 128] * (-LOG2E)
    halo.wait_recv()
    keep = jnp.where(ctx > 0, 1.0, 0.0).astype(F32)
    padded[pl.ds(0, 8), :] = rim[pl.ds(0, 16), :].astype(F32)[8:] * keep
    for g in range(8):
        cols = pl.ds(g * 128, 128)
        total = conv_bias[:, cols] + conv_weight[0:1, cols] * padded[pl.ds(5, 128), cols]
        for k in range(1, 4):
            total = total + conv_weight[k : k + 1, cols] * padded[pl.ds(5 + k, 128), cols]
        conv_out[:, cols] = (total * jax.nn.sigmoid(total)).astype(BF16)

    part[...] = dot_t(conv_out[...], x_proj[...]).reshape(8, 16, 544)
    scatter = [
        send(part.at[lax.rem(exp + d, 8)], parts.at[exp], a_send.at[d], a_recv.at[d], peer(d))
        for d in range(1, 8)
    ]
    parts[pl.ds(exp, 1)] = part[pl.ds(exp, 1)]
    for c in scatter:
        c.wait_recv()
    total = parts[0]
    for j in range(1, 8):
        total = total + parts[j]
    low_rank[pl.ds(exp, 1)] = total[:, :512].astype(BF16)[None]
    maps[pl.ds(exp, 1), :, pl.ds(0, 32)] = total[:, 512:][None]
    gather = []
    for d in range(1, 8):
        for k, ref in enumerate((low_rank, maps)):
            s = 2 * d + k
            gather.append(send(ref.at[exp], ref.at[exp], b_send.at[s], b_recv.at[s], peer(d)))
    top, low = pl.ds(0, 512), pl.ds(512, 512)
    left, right = wrap(my - 1, 4), wrap(my + 1, 4)
    columns[0].wait_recv()
    columns.append(
        send(opg.at[left, top], opg.at[left, top], o_send.at[2], o_recv.at[2], along_y(1))
    )
    columns[1].wait_recv()
    columns.append(
        send(opg.at[right, low], opg.at[right, low], o_send.at[3], o_recv.at[3], along_y(-1))
    )
    for c in gather:
        c.wait_recv()
    scalars = pltpu.make_async_copy(maps, bc_s, l_sem.at[0])
    scalars.start()
    step_low = low_rank[...].reshape(128, 512)
    for j in range(4):
        cols = pl.ds(j * 256, 256)
        raw = dot(step_low, dt_proj[:, cols]) + dt_bias[:, cols]
        step = jnp.maximum(raw, 0.0) + jnp.log1p(jnp.exp(-jnp.abs(raw)))
        drive = step * conv_out[:, cols].astype(F32)
        for i in range(2):
            rows = pl.ds(j * 2 + i, 128, stride=8)
            step_t[rows, :] = step[:, i * 128 : (i + 1) * 128]
            drive_t[rows, :] = drive[:, i * 128 : (i + 1) * 128]
    scalars.wait()

    rates = [rate_t[pl.ds(n * 8, 8), :] for n in range(16)]
    zero = jnp.zeros((8, 128), F32)

    def scan_step(t, carry):
        states, running = carry
        rows = pl.ds(pl.multiple_of(t * 8, 8), 8)
        s, d = step_t[rows, :], drive_t[rows, :]
        outs = [zero, zero]
        after = []
        for n in range(16):
            h = jnp.exp2(rates[n] * s) * states[n] + bc_s[t // 16, t % 16, n] * d
            outs[n % 2] = outs[n % 2] + bc_s[t // 16, t % 16, 16 + n] * h
            after.append(h)
        running = running + s
        y_t[rows, :] = outs[0] + outs[1]
        cum_t[rows, :] = running
        return (tuple(after), running)

    states, running = lax.fori_loop(0, 128, scan_step, ((zero,) * 16, zero), unroll=2)

    def exchange(finals, total, fin, sums, place, base, step):
        for n in range(16):
            fin_own[base // 6, pl.ds(n * 8, 8), :] = finals[n].astype(BF16)
        sums[pl.ds(place, 1)] = total[None]
        fin[pl.ds(place, 1)] = fin_own[base // 6][None]
        moves = []
        for k, d in enumerate((1, -1, 2)):
            s, r = base + 2 * k, base + 2 * k + 1
            moves.append(
                send(fin_own.at[base // 6], fin.at[place], c_send.at[s], c_recv.at[s], step(d))
            )
            moves.append(send(sums.at[place], sums.at[place], c_send.at[r], c_recv.at[r], step(d)))
        for c in moves:
            c.wait_recv()

    exchange(states, running, fin_y, sum_y, my, 0, along_y)
    before, row_total = zero, zero
    for v in range(4):
        before = before + jnp.where(v < my, 1.0, 0.0).astype(F32) * sum_y[v]
        row_total = row_total + sum_y[v]
    row_final = []
    for n in range(16):
        entering, whole = zero, zero
        for v in range(4):
            own = fin_y[v, pl.ds(n * 8, 8), :].astype(F32)
            decay = jnp.exp2(rates[n] * sum_y[v])
            entering = jnp.where(v < my, decay * entering + own, entering)
            whole = decay * whole + own
        enter_t[pl.ds(n * 8, 8), :] = entering
        row_final.append(whole)
    exchange(row_final, row_total, fin_x, sum_x, mx, 6, along_x)
    for n in range(16):
        entering = zero
        for u in range(4):
            own = fin_x[u, pl.ds(n * 8, 8), :].astype(F32)
            decay = jnp.exp2(rates[n] * sum_x[u])
            entering = jnp.where(u < mx, decay * entering + own, entering)
        rows = pl.ds(n * 8, 8)
        enter_t[rows, :] = enter_t[rows, :] + jnp.exp2(rates[n] * before) * entering

    def add_entering(t, carry):
        rows = pl.ds(pl.multiple_of(t * 8, 8), 8)
        c = cum_t[rows, :]
        outs = [y_t[rows, :], zero]
        for n in range(16):
            outs[n % 2] = outs[n % 2] + bc_s[t // 16, t % 16, 16 + n] * (jnp.exp2(rates[n] * c) * entered[n])
        y_t[rows, :] = outs[0] + outs[1]
        return carry

    entered = [enter_t[pl.ds(n * 8, 8), :] for n in range(16)]
    moves = []
    for half in range(2):
        lax.fori_loop(half * 64, half * 64 + 64, add_entering, 0, unroll=2)
        rows = pl.ds(half * 64, 64)
        for g in range(8):
            cols = pl.ds(g * 128, 128)
            y = y_t[pl.ds(half * 512 + g, 64, stride=8), :]
            y = y + skip[:, cols] * conv_out[rows, cols].astype(F32)
            z = gate_in[rows, cols].astype(F32)
            ga[pl.ds(mx, 1), rows, cols] = (y * (z * jax.nn.sigmoid(z))).astype(BF16)[None]
        place = ga.at[mx, rows]
        for k, d in enumerate((1, -1)):
            s = half * 2 + k
            moves.append(send(place, place, g_send.at[s], g_recv.at[s], along_x(d)))

    def project(u):
        for v in range(4):
            cols = pl.ds(v * 256, 256)
            out = dot(ga[u], opg[v])
            zs[pl.ds(u, 1), :, :, cols] = out.astype(BF16).reshape(1, 8, 16, 256)
        rz[pl.ds(u, 1), pl.ds(exp, 1)] = zs[pl.ds(u, 1), pl.ds(exp, 1)]

    def scatter_group(k, u):
        return [
            send(zs.at[u, lax.rem(exp + d, 8)], rz.at[u, exp], z_send.at[k, d], z_recv.at[k, d], peer(d))
            for d in range(1, 8)
        ]

    for c in columns[2:]:
        c.wait_recv()
    left, right, far = wrap(mx - 1, 4), wrap(mx + 1, 4), wrap(mx + 2, 4)
    top, low = pl.ds(0, 64), pl.ds(64, 64)
    project(mx)
    groups = [scatter_group(0, mx)]
    moves[0].wait_recv()
    moves.append(send(ga.at[left, top], ga.at[left, top], g_send.at[4], g_recv.at[4], along_x(1)))
    moves[1].wait_recv()
    moves[3].wait_recv()
    moves.append(send(ga.at[right, low], ga.at[right, low], g_send.at[5], g_recv.at[5], along_x(-1)))
    moves[2].wait_recv()
    for k, u in ((1, left), (2, right)):
        project(u)
        groups.append(scatter_group(k, u))
    moves[4].wait_recv()
    moves[5].wait_recv()
    project(far)
    groups.append(scatter_group(3, far))
    backs = []
    for k, (u, d) in enumerate(((mx, 0), (left, -1), (right, 1), (far, 2))):
        for c in groups[k]:
            c.wait_recv()
        total = rz[u, 0].astype(F32)
        for j in range(1, 8):
            total = total + rz[u, j].astype(F32)
        if d == 0:
            mo[pl.ds(mx, 1)] = total[None]
        else:
            ms[k - 1] = total
            backs.append(send(ms.at[k - 1], mo.at[mx], m_send.at[k], m_recv.at[k], along_x(d)))
    for c in backs:
        c.wait_recv()

    squares = jnp.zeros((16, 1), F32)
    for u in range(4):
        cols = pl.ds(u * 1024, 1024)
        rows = residual[:, cols].astype(F32) + mo[u]
        stream[:, cols] = rows
        squares = squares + jnp.sum(rows * rows, axis=1, keepdims=True)
    scale = lax.rsqrt(squares * (1.0 / 4096.0) + 1e-06)
    logits = jnp.zeros((8, 16), F32)
    for u in range(4):
        cols = pl.ds(u * 1024, 1024)
        rows = (stream[:, cols] * scale * gain[:, cols]).astype(BF16)
        normed[:, cols] = rows
        logits = logits + dot_t(router[:, cols], rows)
    ids = expert_ids[...]
    lanes = lax.broadcasted_iota(jnp.int32, (8, 16), 0)
    signs = jnp.where(ids[0:1] == lanes, 1.0, 0.0) - jnp.where(ids[1:2] == lanes, 1.0, 0.0)
    first = jax.nn.sigmoid(jnp.sum(logits * signs, axis=0, keepdims=True))
    return first, sent


def experts(r, gate_row, sent, out, exp, mx, my, halves, loads):
    pick_a = r["pick_a"]
    pick_b = r["pick_b"]
    stream = r["stream"]
    normed = r["normed"]
    spread = r["spread"]
    fetch = r["fetch"]
    go = r["go"]
    rcv = r["rcv"]
    rback = r["rback"]
    xa = r["xa"]
    xb = r["xb"]
    wgu = r["wgu"]
    wd = r["wd"]
    lhs = r["lhs"]
    acc = r["acc"]
    hid = r["hid"]
    oa = r["oa"]
    ob = r["ob"]
    far = r["far"]
    near = r["near"]
    tot = r["tot"]
    far2 = r["far2"]
    near2 = r["near2"]
    d_send = r["d_send"]
    d_recv = r["d_recv"]
    u_send = r["u_send"]
    u_recv = r["u_recv"]
    s_send = r["s_send"]
    s_recv = r["s_recv"]
    r_send = r["r_send"]
    r_recv = r["r_recv"]
    xs, os = (xa, xb), (oa, ob)
    lo, hi = pl.ds(0, 1024), pl.ds(1024, 1024)
    every = slice(None)

    rows = normed[...]
    packed = dot(spread[0], rows[:, :2048]) + dot(spread[1], rows[:, 2048:])
    go[...] = packed.astype(BF16).reshape(8, 16, 2048)
    sends = []
    for d in range(1, 8):
        peer = lax.rem(exp + d, 8)
        c = remote(go.at[peer], rcv.at[exp], d_send.at[d], d_recv.at[d], {"exp": peer})
        c.start()
        sends.append(c)
    rcv[pl.ds(exp, 1)] = go[pl.ds(exp, 1)]
    acc[...] = jnp.zeros_like(acc)
    for c in sends:
        c.wait_recv()
    flat = rcv[...].reshape(128, 2048)
    xa[pl.ds(mx, 1), pl.ds(my, 1)] = dot(pick_a[...], flat).astype(BF16)[None, None]
    xb[pl.ds(mx, 1), pl.ds(my, 1)] = dot(pick_b[...], flat).astype(BF16)[None, None]
    for c in sends:
        c.wait_send()

    def push(h, x, at, cols, g, k, device):
        place = x.at[at + (every, cols)] if cols is not None else x.at[at]
        c = remote(place, place, u_send.at[h, g, k], u_recv.at[h, g, k], device)
        c.start()
        sent.append(c)
        return c

    first, second = [], [[None] * 4, [None] * 4]

    def second_start(i, g, u):
        h, x = halves[i], xs[i]
        at = h.unit(u, h.q)
        second[i][g] = [
            push(i, x, at, None, g + 1, 0, h.two(1)),
            push(i, x, at, None, g + 1, 1, h.two(-1)),
        ]

    def second_pass(i, g, u):
        h, x = halves[i], xs[i]
        second[i][g][0].wait_recv()
        a = push(i, x, h.unit(u, wrap(h.q - 1, 4)), lo, g + 1, 2, h.two(1))
        second[i][g][1].wait_recv()
        b = push(i, x, h.unit(u, wrap(h.q + 1, 4)), hi, g + 1, 3, h.two(-1))
        second[i][g] += [a, b]

    for i, (h, x) in enumerate(zip(halves, xs)):
        at = h.unit(h.p, h.q)
        first.append(
            [push(i, x, at, None, 0, 0, h.one(1)), push(i, x, at, None, 0, 1, h.one(-1))]
        )
    for i, h in enumerate(halves):
        second_start(i, 0, h.p)
    for i, (h, x) in enumerate(zip(halves, xs)):
        left, right = wrap(h.p - 1, 4), wrap(h.p + 1, 4)
        first[i][0].wait_recv()
        first[i].append(push(i, x, h.unit(left, h.q), lo, 0, 2, h.one(1)))
        first[i][1].wait_recv()
        first[i].append(push(i, x, h.unit(right, h.q), hi, 0, 3, h.one(-1)))
        second_start(i, 1, left)
        second_start(i, 2, right)
    for i, h in enumerate(halves):
        first[i][2].wait_recv()
        first[i][3].wait_recv()
        second_start(i, 3, wrap(h.p + 2, 4))

    def gate_up(i, v):
        h = halves[i]
        at = h.group(v)
        lhs[...] = xs[i][at].reshape(160, 2048)

        @pl.loop(0, 6)
        def _(j):
            cols = pl.ds(pl.multiple_of(j * 256, 256), 256)
            part = dot(lhs[...], wgu[pl.ds(i * 2048, 2048), cols])
            place = at + (every, cols)
            acc[place] = acc[place] + part.reshape(4, 40, 256)

    loads[0].wait()
    loads[1].wait()
    for i, h in enumerate(halves):
        gate_up(i, h.q)
    for g in range(4):
        for i, h in enumerate(halves):
            u = (h.p, wrap(h.p - 1, 4), wrap(h.p + 1, 4), wrap(h.p + 2, 4))[g]
            second_pass(i, g, u)
    for i, h in enumerate(halves):
        gate_up(i, wrap(h.q - 1, 4))
        gate_up(i, wrap(h.q + 1, 4))
    for i, h in enumerate(halves):
        for g in range(4):
            second[i][g][2].wait_recv()
            second[i][g][3].wait_recv()
        gate_up(i, wrap(h.q + 2, 4))

    @pl.loop(0, 16)
    def _(n):
        at = (n // 4, n % 4)
        gate = acc[at + (every, pl.ds(0, 768))]
        up = acc[at + (every, pl.ds(768, 768))]
        hid[at] = (gate * jax.nn.sigmoid(gate) * up).astype(BF16)

    loads[2].wait()

    def down(i, v):
        at = halves[i].group(v)
        lhs[:, pl.ds(0, 768)] = hid[at].reshape(160, 768)

        @pl.loop(0, 8)
        def _(j):
            start = pl.multiple_of(j * 256, 256)
            part = dot(lhs[:, pl.ds(0, 768)], wd[:, pl.ds(i * 2048 + start, 256)])
            os[i][at + (every, pl.ds(start, 256))] = part.reshape(4, 40, 256).astype(BF16)

    def send(src, dst, i, stage, k, device):
        c = remote(src, dst, s_send.at[i, stage, k], s_recv.at[i, stage, k], device)
        c.start()
        sent.append(c)
        return c

    def ring_far(i, stage, chunk, ahead, behind, step):
        return [
            send(chunk(2, lo), ahead, i, stage, 0, step(1)),
            send(chunk(2, hi), behind, i, stage, 1, step(-1)),
        ]

    def add_into(ref, at, other, other_at):
        ref[at] = (ref[at].astype(F32) + other[other_at].astype(F32)).astype(BF16)

    stage_one = [None, None]
    for i, h in enumerate(halves):
        down(i, wrap(h.q + 2, 4))
        o, at = os[i], h.group(wrap(h.q + 2, 4))
        stage_one[i] = [
            send(o.at[at + (every, lo)], far.at[i, 0], i, 0, 0, h.two(1)),
            send(o.at[at + (every, hi)], far.at[i, 1], i, 0, 1, h.two(-1)),
        ]
    for i, h in enumerate(halves):
        o = os[i]
        down(i, wrap(h.q + 1, 4))
        at = h.group(wrap(h.q + 1, 4))
        stage_one[i].append(
            send(o.at[at + (every, hi)], near.at[i, 0, :, :, hi], i, 0, 2, h.two(1))
        )
        down(i, wrap(h.q - 1, 4))
        at = h.group(wrap(h.q - 1, 4))
        stage_one[i].append(
            send(o.at[at + (every, lo)], near.at[i, 1, :, :, lo], i, 0, 3, h.two(-1))
        )
    for i, h in enumerate(halves):
        down(i, h.q)
    for i, h in enumerate(halves):
        o = os[i]
        stage_one[i][0].wait_recv()
        at = h.group(wrap(h.q + 1, 4)) + (every, lo)
        add_into(o, at, far, (i, 0))
        stage_one[i].append(send(o.at[at], near.at[i, 0, :, :, lo], i, 0, 4, h.two(1)))
        stage_one[i][1].wait_recv()
        at = h.group(wrap(h.q - 1, 4)) + (every, hi)
        add_into(o, at, far, (i, 1))
        stage_one[i].append(send(o.at[at], near.at[i, 1, :, :, hi], i, 0, 5, h.two(-1)))

    stage_two = [None, None]
    for i, h in enumerate(halves):
        for c in stage_one[i][2:]:
            c.wait_recv()

        def total(u):
            mine = os[i][h.unit(u, h.q)].astype(F32)
            tot[i, u] = (mine + near[i, 0, u].astype(F32) + near[i, 1, u].astype(F32)).astype(BF16)

        opposite, ahead, behind = wrap(h.p + 2, 4), wrap(h.p + 1, 4), wrap(h.p - 1, 4)
        total(opposite)
        stage_two[i] = [
            send(tot.at[i, opposite, :, lo], far2.at[i, 0], i, 1, 0, h.one(1)),
            send(tot.at[i, opposite, :, hi], far2.at[i, 1], i, 1, 1, h.one(-1)),
        ]
        total(ahead)
        total(behind)
        stage_two[i].append(send(tot.at[i, ahead, :, hi], near2.at[i, 0, :, hi], i, 1, 2, h.one(1)))
        stage_two[i].append(
            send(tot.at[i, behind, :, lo], near2.at[i, 1, :, lo], i, 1, 3, h.one(-1))
        )
        total(h.p)
    for i, h in enumerate(halves):
        ahead, behind = wrap(h.p + 1, 4), wrap(h.p - 1, 4)
        stage_two[i][0].wait_recv()
        add_into(tot, (i, ahead, every, lo), far2, (i, 0))
        stage_two[i].append(send(tot.at[i, ahead, :, lo], near2.at[i, 0, :, lo], i, 1, 4, h.one(1)))
        stage_two[i][1].wait_recv()
        add_into(tot, (i, behind, every, hi), far2, (i, 1))
        stage_two[i].append(
            send(tot.at[i, behind, :, hi], near2.at[i, 1, :, hi], i, 1, 5, h.one(-1))
        )
    ends = []
    for i, h in enumerate(halves):
        for c in stage_two[i][2:]:
            c.wait_recv()
        final = (
            tot[i, h.p].astype(F32) + near2[i, 0].astype(F32) + near2[i, 1].astype(F32)
        ).astype(BF16)
        ends.append(final)

    across = (((0,), (0,)), ((), ()))
    back = lax.dot_general(pick_a[...], ends[0], across, preferred_element_type=F32)
    back = back + lax.dot_general(pick_b[...], ends[1], across, preferred_element_type=F32)
    go[...] = back.astype(BF16).reshape(8, 16, 2048)
    sends = []
    for d in range(1, 8):
        peer = lax.rem(exp + d, 8)
        c = remote(go.at[peer], rback.at[exp], r_send.at[d], r_recv.at[d], {"exp": peer})
        c.start()
        sends.append(c)
    rback[pl.ds(exp, 1)] = go[pl.ds(exp, 1)]
    for c in sends:
        c.wait_recv()
    flat = rback[...].reshape(128, 2048)
    eye = lax.broadcasted_iota(jnp.int32, (16, 16), 0) == lax.broadcasted_iota(
        jnp.int32, (16, 16), 1
    )
    gate = jnp.sum(jnp.where(eye, jnp.broadcast_to(gate_row, (16, 16)), 0.0), axis=1, keepdims=True)
    for i in range(2):
        cols = pl.ds(i * 2048, 2048)
        pair = [
            lax.dot_general(fetch[i, k], flat, across, preferred_element_type=F32)
            for k in range(2)
        ]
        mix = gate * pair[0] + (1.0 - gate) * pair[1]
        out[:, cols] = (stream[:, cols] + mix).astype(BF16)
    for c in sends + sent:
        c.wait_send()


def token_places(ids, spread, fetch):
    experts_of = lax.broadcasted_iota(jnp.int32, (8, 16), 0)
    hits = [ids[k : k + 1] == experts_of for k in range(2)]
    either = jnp.where(hits[0] | hits[1], 1.0, 0.0).astype(BF16)
    before = lax.broadcasted_iota(jnp.int32, (16, 16), 0) < lax.broadcasted_iota(
        jnp.int32, (16, 16), 1
    )
    earlier = dot(either, jnp.where(before, 1.0, 0.0).astype(BF16))
    rows = lax.broadcasted_iota(jnp.int32, (128, 16), 0).astype(F32)
    for half in range(2):
        found = []
        for k in range(2):
            slot = jnp.sum(jnp.where(hits[k], earlier, 0.0), axis=0, keepdims=True)
            place = ids[k : k + 1].astype(F32) * 16.0 + slot + half * 8.0
            found.append(jnp.where(rows == place, 1.0, 0.0))
            fetch[half, k] = found[k].astype(BF16)
        spread[half] = (found[0] + found[1]).astype(BF16)


def block_kernel(*refs):
    names = INPUTS + ("out",) + tuple(SCRATCH)
    r = dict(zip(names, refs, strict=True))
    ctx, exp = lax.axis_index("ctx"), lax.axis_index("exp")
    mx, my = ctx // 4, ctx % 4
    halves = (Half(0, mx, my), Half(1, mx, my))
    wgu, wd, w_sem = r["wgu"], r["wd"], r["w_sem"]
    loads = [
        pltpu.make_async_copy(r["w_gate"].at[0], wgu.at[:, pl.ds(0, 768)], w_sem.at[0]),
        pltpu.make_async_copy(r["w_up"].at[0], wgu.at[:, pl.ds(768, 768)], w_sem.at[1]),
        pltpu.make_async_copy(r["w_down"].at[0], wd, w_sem.at[2]),
    ]
    for load in loads:
        load.start()
    greet(
        [{"ctx": lax.rem(ctx + 15, 16)}, {"ctx": lax.rem(ctx + 1, 16)}]
        + [h.one(d) for h in halves for d in (1, 2, -1)]
        + [{"exp": lax.rem(exp + d, 8)} for d in range(1, 8)]
    )
    token_places(r["expert_ids"][...], r["spread"], r["fetch"])
    first, sent = mixer(r, ctx, exp, mx, my)
    experts(r, first, sent, r["out"], exp, mx, my, halves, loads)


def shards(
    mixer_in,
    gate_in,
    conv_weight,
    conv_bias,
    x_proj,
    dt_proj,
    dt_bias,
    decay_rate,
    skip,
    out_proj,
    residual,
    gain,
    router,
    w_gate,
    w_up,
    w_down,
    expert_ids,
):
    pick = np.zeros((2, 40, 128), np.float32)
    for j in range(8):
        for s in range(5):
            pick[0, j * 5 + s, j * 16 + s] = 1.0
            pick[1, j * 5 + s, j * 16 + 8 + s] = 1.0
    vmem = pl.BlockSpec(memory_space=pltpu.VMEM)
    anywhere = pl.BlockSpec(memory_space=pl.ANY)
    return pl.pallas_call(
        block_kernel,
        out_shape=jax.ShapeDtypeStruct((16, 4096), BF16),
        in_specs=[anywhere if name.startswith("w_") else vmem for name in INPUTS],
        out_specs=vmem,
        scratch_shapes=list(SCRATCH.values()),
        compiler_params=pltpu.CompilerParams(
            collective_id=0, has_side_effects=True, vmem_limit_bytes=VMEM_LIMIT
        ),
        cost_estimate=pl.CostEstimate(
            flops=13_500_000_000, bytes_accessed=24_000_000, transcendentals=0
        ),
    )(
        mixer_in,
        gate_in,
        conv_weight,
        conv_bias[None],
        x_proj.T,
        dt_proj,
        dt_bias[None],
        decay_rate,
        skip[None],
        out_proj,
        residual,
        gain[None],
        router.T,
        expert_ids.T,
        w_gate,
        w_up,
        w_down,
        jnp.asarray(pick[0], BF16),
        jnp.asarray(pick[1], BF16),
    )


def solution(mesh):
    in_specs = (
        P("ctx", "exp"),
        P("ctx", "exp"),
        P(None, "exp"),
        P("exp"),
        P("exp", None),
        P(None, "exp"),
        P("exp"),
        P(None, "exp"),
        P("exp"),
        P("exp", "ctx"),
        P(("ctx", "exp"), None),
        P(),
        P(),
        P("exp", None, "ctx"),
        P("exp", None, "ctx"),
        P("exp", "ctx", None),
        P(("ctx", "exp"), None),
    )
    out_specs = P(("ctx", "exp"), None)
    return jax.shard_map(shards, mesh=mesh, in_specs=in_specs, out_specs=out_specs, check_vma=False)
```

time: 438 us -> 155 us (0.35)
  waiting for transfers between devices: 246 us -> 0 us
  Pallas kernels: 99 us -> 153 us
  other arithmetic: 37.2 us -> 0 us
  local copies, waits for them, and re-layouts: 26.7 us -> 1.57 us
  between operations: 13.5 us -> 0.01 us
  matrix products: 8.99 us -> 0 us
    all_gather x3 -> x0, waiting for transfers between devices: 156 us -> none  [the longest x2 82.8 us: entering_2(): gathered = jax.tree.map(lambda a: lax.all_gather(a, axis), part)]
    psum x1 -> x0, waiting for transfers between devices: 61.2 us -> none  [shards(): lax.psum(jnp.dot(conv_out, x_proj, preferred_element_type=jnp.float32), '...]
    pallas_call x1, Pallas kernels: 99 us -> 153 us  [shards(): pl.pallas_call(block_kernel, out_shape=jax.ShapeDtypeStruct((16, 4096), B...]
    reduce_scatter x1 -> x0, waiting for transfers between devices: 27.8 us -> none  [shards(): lax.psum_scatter(jnp.dot(gated, full_out, preferred_element_type=jnp.floa...]
    reduce_sum x10 -> x0, other arithmetic: 10.5 us -> none  [the longest x4 6.44 us: local_scan(): jnp.sum(c_groups[:, :, :, None] * states, axis=2)]
    dynamic_update_slice x16 -> x0, other arithmetic: 9.64 us -> none  [shards(): lax.map(local_scan, (to_blocks(step_size), to_blocks(drive), to_blocks(de...]
    dot_general x4 -> x0, matrix products: 8.99 us -> none  [the longest x1 6.1 us: shards(): jnp.dot(gated, full_out, preferred_element_type=jnp.float32)]
    another operation x19 -> x0, other arithmetic: 8.22 us -> none  [the longest x4 6.07 us: local_scan(): inner = decay_in * jnp.cumsum(jnp.exp(exponent) * inputs, axis=1)]
  transfers between devices with their start and end apart: 6 -> 0, of which waited for: 5 -> 0; matrix products, arithmetic and copies ran while one was open for 3% -> 0% of each run, Pallas kernels for 0% -> 0%
where the time goes in v3:
time: 155 us
  Pallas kernels  153 us (99%)
  local copies, waits for them, and re-layouts  1.57 us (1%)
    pallas_call x1, Pallas kernels, shards(): pl.pallas_call(block_kernel, out_shape=jax.ShapeDtypeStruct((16, 4096), B...  153 us

profile of v3, /device:TPU:1, one launch (start us, length us, event | category | flops | bytes accessed | tf_op | source)
XLA Modules:
  0.0 154.9 jit_solution(5676836702817119968)
XLA Ops:
  0.0 153.3 %shard_map.181 = bf16[16,4096]{1,0:T(8,128)(2,1)} custom-call(bf16[128,1024]{1,0:T(8,128)(2,1)} %refs_0_.1, bf16[128,1024]{1,0:T(8,128)(2,1)} %refs_1_.1, f32[4,1024]{1,0:T(4,128)} %refs_2_.1, f32[1,1024]{1,0:T(1,128)} %bitcast.10, bf16[544,1024]{1,0:T(8,128)(2,1)} %bitcast.7, bf16[512,1024]{1,0:T(8,128)(2,1)} %refs_5_.1, f32[1,1024]{1,0:T(1,128)} %bitcast.11, ...), custom_call_target="tpu_custom_call" | custom-call | flops 13500000256 | bytes 24000000 | tf_op jit(solution)/shard_map/pallas_call | solution.py:793
  153.3 1.6 %copy.21 = bf16[16,4096]{1,0:T(8,128)(2,1)} copy(bf16[16,4096]{1,0:T(8,128)(2,1)} %shard_map.181) | data formatting | bytes 262144

commit v4 on v3

--- a/solution.py
+++ b/solution.py
@@ -82,20 +82,19 @@
     "w_gate",
     "w_up",
     "w_down",
-    "pick_a",
-    "pick_b",
+    "pick",
 )
 
 SCRATCH = {
     "stream": pltpu.VMEM((16, 4096), F32),
     "normed": pltpu.VMEM((16, 4096), BF16),
-    "spread": pltpu.VMEM((2, 128, 16), BF16),
-    "fetch": pltpu.VMEM((2, 2, 128, 16), BF16),
+    "spread": pltpu.VMEM((3, 128, 16), BF16),
+    "fetch": pltpu.VMEM((3, 2, 128, 16), BF16),
     "rim": pltpu.VMEM((16, 1024), BF16),
     "padded": pltpu.VMEM((136, 1024), F32),
     "conv_out": pltpu.VMEM((128, 1024), BF16),
-    "part": pltpu.VMEM((8, 16, 544), F32),
-    "parts": pltpu.VMEM((8, 16, 544), F32),
+    "part": pltpu.VMEM((8, 16, 544), BF16),
+    "parts": pltpu.VMEM((8, 16, 544), BF16),
     "low_rank": pltpu.VMEM((8, 16, 512), BF16),
     "maps": pltpu.VMEM((8, 16, 128), F32),
     "bc_s": pltpu.SMEM((8, 16, 128), F32),
@@ -114,8 +113,8 @@
     "ga": pltpu.VMEM((4, 128, 1024), BF16),
     "zs": pltpu.VMEM((4, 8, 16, 1024), BF16),
     "rz": pltpu.VMEM((4, 8, 16, 1024), BF16),
-    "ms": pltpu.VMEM((3, 16, 1024), F32),
-    "mo": pltpu.VMEM((4, 16, 1024), F32),
+    "ms": pltpu.VMEM((3, 16, 1024), BF16),
+    "mo": pltpu.VMEM((4, 16, 1024), BF16),
     "h_sem": pltpu.SemaphoreType.DMA((2,)),
     "a_send": pltpu.SemaphoreType.DMA((8,)),
     "a_recv": pltpu.SemaphoreType.DMA((8,)),
@@ -132,9 +131,9 @@
     "m_send": pltpu.SemaphoreType.DMA((4,)),
     "m_recv": pltpu.SemaphoreType.DMA((4,)),
     "l_sem": pltpu.SemaphoreType.DMA((1,)),
-    "go": pltpu.VMEM((8, 16, 2048), BF16),
-    "rcv": pltpu.VMEM((8, 16, 2048), BF16),
-    "rback": pltpu.VMEM((8, 16, 2048), BF16),
+    "go": pltpu.VMEM((2, 8, 16, 768), BF16),
+    "rcv": pltpu.VMEM((2, 8, 16, 768), BF16),
+    "rback": pltpu.VMEM((2, 8, 16, 768), BF16),
     "xa": pltpu.VMEM((4, 4, 40, 2048), BF16),
     "xb": pltpu.VMEM((4, 4, 40, 2048), BF16),
     "wgu": pltpu.VMEM((4096, 1536), BF16),
@@ -150,14 +149,14 @@
     "far2": pltpu.VMEM((2, 2, 40, 1024), BF16),
     "near2": pltpu.VMEM((2, 2, 40, 2048), BF16),
     "w_sem": pltpu.SemaphoreType.DMA((3,)),
-    "d_send": pltpu.SemaphoreType.DMA((8,)),
-    "d_recv": pltpu.SemaphoreType.DMA((8,)),
+    "d_send": pltpu.SemaphoreType.DMA((2, 8)),
+    "d_recv": pltpu.SemaphoreType.DMA((2, 8)),
     "u_send": pltpu.SemaphoreType.DMA((2, 5, 4)),
     "u_recv": pltpu.SemaphoreType.DMA((2, 5, 4)),
-    "s_send": pltpu.SemaphoreType.DMA((2, 2, 6)),
-    "s_recv": pltpu.SemaphoreType.DMA((2, 2, 6)),
-    "r_send": pltpu.SemaphoreType.DMA((8,)),
-    "r_recv": pltpu.SemaphoreType.DMA((8,)),
+    "s_send": pltpu.SemaphoreType.DMA((2, 24)),
+    "s_recv": pltpu.SemaphoreType.DMA((2, 24)),
+    "r_send": pltpu.SemaphoreType.DMA((2, 8)),
+    "r_recv": pltpu.SemaphoreType.DMA((2, 8)),
 }
 
 
@@ -248,17 +247,23 @@
     padded[pl.ds(8, 128), :] = mixer_in[...].astype(F32)
     for g in range(8):
         rate_t[pl.ds(g, 16, stride=8), :] = decay_rate[:, g * 128 : (g + 1) * 128] * (-LOG2E)
+
+    def convolve(start, rows):
+        for g in range(8):
+            cols = pl.ds(g * 128, 128)
+            total = conv_bias[:, cols]
+            for k in range(4):
+                taps = conv_weight[k : k + 1, cols]
+                total = total + taps * padded[pl.ds(start + 5 + k, rows), cols]
+            conv_out[pl.ds(start, rows), cols] = (total * jax.nn.sigmoid(total)).astype(BF16)
+
+    convolve(16, 112)
     halo.wait_recv()
     keep = jnp.where(ctx > 0, 1.0, 0.0).astype(F32)
     padded[pl.ds(0, 8), :] = rim[pl.ds(0, 16), :].astype(F32)[8:] * keep
-    for g in range(8):
-        cols = pl.ds(g * 128, 128)
-        total = conv_bias[:, cols] + conv_weight[0:1, cols] * padded[pl.ds(5, 128), cols]
-        for k in range(1, 4):
-            total = total + conv_weight[k : k + 1, cols] * padded[pl.ds(5 + k, 128), cols]
-        conv_out[:, cols] = (total * jax.nn.sigmoid(total)).astype(BF16)
-
-    part[...] = dot_t(conv_out[...], x_proj[...]).reshape(8, 16, 544)
+    convolve(0, 16)
+
+    part[...] = dot_t(conv_out[...], x_proj[...]).astype(BF16).reshape(8, 16, 544)
     scatter = [
         send(part.at[lax.rem(exp + d, 8)], parts.at[exp], a_send.at[d], a_recv.at[d], peer(d))
         for d in range(1, 8)
@@ -266,9 +271,9 @@
     parts[pl.ds(exp, 1)] = part[pl.ds(exp, 1)]
     for c in scatter:
         c.wait_recv()
-    total = parts[0]
+    total = parts[0].astype(F32)
     for j in range(1, 8):
-        total = total + parts[j]
+        total = total + parts[j].astype(F32)
     low_rank[pl.ds(exp, 1)] = total[:, :512].astype(BF16)[None]
     maps[pl.ds(exp, 1), :, pl.ds(0, 32)] = total[:, 512:][None]
     gather = []
@@ -276,6 +281,8 @@
         for k, ref in enumerate((low_rank, maps)):
             s = 2 * d + k
             gather.append(send(ref.at[exp], ref.at[exp], b_send.at[s], b_recv.at[s], peer(d)))
+    for c in gather:
+        c.wait_recv()
     top, low = pl.ds(0, 512), pl.ds(512, 512)
     left, right = wrap(my - 1, 4), wrap(my + 1, 4)
     columns[0].wait_recv()
@@ -286,8 +293,6 @@
     columns.append(
         send(opg.at[right, low], opg.at[right, low], o_send.at[3], o_recv.at[3], along_y(-1))
     )
-    for c in gather:
-        c.wait_recv()
     scalars = pltpu.make_async_copy(maps, bc_s, l_sem.at[0])
     scalars.start()
     step_low = low_rank[...].reshape(128, 512)
@@ -427,9 +432,9 @@
         for j in range(1, 8):
             total = total + rz[u, j].astype(F32)
         if d == 0:
-            mo[pl.ds(mx, 1)] = total[None]
+            mo[pl.ds(mx, 1)] = total.astype(BF16)[None]
         else:
-            ms[k - 1] = total
+            ms[k - 1] = total.astype(BF16)
             backs.append(send(ms.at[k - 1], mo.at[mx], m_send.at[k], m_recv.at[k], along_x(d)))
     for c in backs:
         c.wait_recv()
@@ -437,7 +442,7 @@
     squares = jnp.zeros((16, 1), F32)
     for u in range(4):
         cols = pl.ds(u * 1024, 1024)
-        rows = residual[:, cols].astype(F32) + mo[u]
+        rows = residual[:, cols].astype(F32) + mo[u].astype(F32)
         stream[:, cols] = rows
         squares = squares + jnp.sum(rows * rows, axis=1, keepdims=True)
     scale = lax.rsqrt(squares * (1.0 / 4096.0) + 1e-06)
@@ -455,8 +460,7 @@
 
 
 def experts(r, gate_row, sent, out, exp, mx, my, halves, loads):
-    pick_a = r["pick_a"]
-    pick_b = r["pick_b"]
+    pick = r["pick"]
     stream = r["stream"]
     normed = r["normed"]
     spread = r["spread"]
@@ -490,24 +494,28 @@
     lo, hi = pl.ds(0, 1024), pl.ds(1024, 1024)
     every = slice(None)
 
-    rows = normed[...]
-    packed = dot(spread[0], rows[:, :2048]) + dot(spread[1], rows[:, 2048:])
-    go[...] = packed.astype(BF16).reshape(8, 16, 2048)
-    sends = []
-    for d in range(1, 8):
-        peer = lax.rem(exp + d, 8)
-        c = remote(go.at[peer], rcv.at[exp], d_send.at[d], d_recv.at[d], {"exp": peer})
-        c.start()
-        sends.append(c)
-    rcv[pl.ds(exp, 1)] = go[pl.ds(exp, 1)]
+    windows = (0, 768, 1280)
+
+    def all_to_all(half, into, ss, rs):
+        moves = []
+        for d in range(1, 8):
+            peer = lax.rem(exp + d, 8)
+            src, dst = go.at[half, peer], into.at[half, exp]
+            c = remote(src, dst, ss.at[half, d], rs.at[half, d], {"exp": peer})
+            c.start()
+            moves.append(c)
+        into[half, pl.ds(exp, 1)] = go[half, pl.ds(exp, 1)]
+        sent.extend(moves)
+        return moves
+
+    dispatch = []
+    for i in range(2):
+        packed = jnp.zeros((128, 768), F32)
+        for k, w in enumerate(windows):
+            packed = packed + dot(spread[k], normed[:, pl.ds(i * 2048 + w, 768)])
+        go[i] = packed.astype(BF16).reshape(8, 16, 768)
+        dispatch.append(all_to_all(i, rcv, d_send, d_recv))
     acc[...] = jnp.zeros_like(acc)
-    for c in sends:
-        c.wait_recv()
-    flat = rcv[...].reshape(128, 2048)
-    xa[pl.ds(mx, 1), pl.ds(my, 1)] = dot(pick_a[...], flat).astype(BF16)[None, None]
-    xb[pl.ds(mx, 1), pl.ds(my, 1)] = dot(pick_b[...], flat).astype(BF16)[None, None]
-    for c in sends:
-        c.wait_send()
 
     def push(h, x, at, cols, g, k, device):
         place = x.at[at + (every, cols)] if cols is not None else x.at[at]
@@ -517,17 +525,18 @@
         return c
 
     first, second = [], [[None] * 4, [None] * 4]
-
-    def second_start(i, g, u):
+    steps = [[wrap(h.p + d, 4) for d in (0, -1, 1, 2)] for h in halves]
+
+    def second_start(i, g):
         h, x = halves[i], xs[i]
-        at = h.unit(u, h.q)
+        at = h.unit(steps[i][g], h.q)
         second[i][g] = [
             push(i, x, at, None, g + 1, 0, h.two(1)),
             push(i, x, at, None, g + 1, 1, h.two(-1)),
         ]
 
-    def second_pass(i, g, u):
-        h, x = halves[i], xs[i]
+    def second_pass(i, g):
+        h, x, u = halves[i], xs[i], steps[i][g]
         second[i][g][0].wait_recv()
         a = push(i, x, h.unit(u, wrap(h.q - 1, 4)), lo, g + 1, 2, h.two(1))
         second[i][g][1].wait_recv()
@@ -535,45 +544,48 @@
         second[i][g] += [a, b]
 
     for i, (h, x) in enumerate(zip(halves, xs)):
+        for c in dispatch[i]:
+            c.wait_recv()
+        flat = rcv[i].reshape(128, 768)
+        for k, w in enumerate(windows):
+            block = dot(pick[k], flat).astype(BF16)[None, None]
+            x[pl.ds(mx, 1), pl.ds(my, 1), :, pl.ds(w, 768)] = block
         at = h.unit(h.p, h.q)
         first.append(
             [push(i, x, at, None, 0, 0, h.one(1)), push(i, x, at, None, 0, 1, h.one(-1))]
         )
-    for i, h in enumerate(halves):
-        second_start(i, 0, h.p)
+        second_start(i, 0)
     for i, (h, x) in enumerate(zip(halves, xs)):
-        left, right = wrap(h.p - 1, 4), wrap(h.p + 1, 4)
         first[i][0].wait_recv()
-        first[i].append(push(i, x, h.unit(left, h.q), lo, 0, 2, h.one(1)))
+        first[i].append(push(i, x, h.unit(steps[i][1], h.q), lo, 0, 2, h.one(1)))
         first[i][1].wait_recv()
-        first[i].append(push(i, x, h.unit(right, h.q), hi, 0, 3, h.one(-1)))
-        second_start(i, 1, left)
-        second_start(i, 2, right)
-    for i, h in enumerate(halves):
+        first[i].append(push(i, x, h.unit(steps[i][2], h.q), hi, 0, 3, h.one(-1)))
+    second_start(0, 1)
+    second_start(1, 1)
+    for i in range(2):
         first[i][2].wait_recv()
         first[i][3].wait_recv()
-        second_start(i, 3, wrap(h.p + 2, 4))
+        second_start(i, 2)
+        second_start(i, 3)
 
     def gate_up(i, v):
-        h = halves[i]
-        at = h.group(v)
+        at = halves[i].group(v)
         lhs[...] = xs[i][at].reshape(160, 2048)
-
-        @pl.loop(0, 6)
-        def _(j):
-            cols = pl.ds(pl.multiple_of(j * 256, 256), 256)
+        for j in range(6):
+            cols = pl.ds(j * 256, 256)
             part = dot(lhs[...], wgu[pl.ds(i * 2048, 2048), cols])
             place = at + (every, cols)
             acc[place] = acc[place] + part.reshape(4, 40, 256)
 
     loads[0].wait()
     loads[1].wait()
-    for i, h in enumerate(halves):
-        gate_up(i, h.q)
-    for g in range(4):
-        for i, h in enumerate(halves):
-            u = (h.p, wrap(h.p - 1, 4), wrap(h.p + 1, 4), wrap(h.p + 2, 4))[g]
-            second_pass(i, g, u)
+    gate_up(0, halves[0].q)
+    second_pass(0, 0)
+    second_pass(1, 0)
+    gate_up(1, halves[1].q)
+    for g in range(1, 4):
+        second_pass(0, g)
+        second_pass(1, g)
     for i, h in enumerate(halves):
         gate_up(i, wrap(h.q - 1, 4))
         gate_up(i, wrap(h.q + 1, 4))
@@ -595,130 +607,110 @@
     def down(i, v):
         at = halves[i].group(v)
         lhs[:, pl.ds(0, 768)] = hid[at].reshape(160, 768)
-
-        @pl.loop(0, 8)
-        def _(j):
-            start = pl.multiple_of(j * 256, 256)
-            part = dot(lhs[:, pl.ds(0, 768)], wd[:, pl.ds(i * 2048 + start, 256)])
-            os[i][at + (every, pl.ds(start, 256))] = part.reshape(4, 40, 256).astype(BF16)
-
-    def send(src, dst, i, stage, k, device):
-        c = remote(src, dst, s_send.at[i, stage, k], s_recv.at[i, stage, k], device)
+        for j in range(8):
+            part = dot(lhs[:, pl.ds(0, 768)], wd[:, pl.ds(i * 2048 + j * 256, 256)])
+            os[i][at + (every, pl.ds(j * 256, 256))] = part.reshape(4, 40, 256).astype(BF16)
+
+    def send(src, dst, i, k, device):
+        c = remote(src, dst, s_send.at[i, k], s_recv.at[i, k], device)
         c.start()
         sent.append(c)
         return c
 
-    def ring_far(i, stage, chunk, ahead, behind, step):
-        return [
-            send(chunk(2, lo), ahead, i, stage, 0, step(1)),
-            send(chunk(2, hi), behind, i, stage, 1, step(-1)),
-        ]
-
     def add_into(ref, at, other, other_at):
         ref[at] = (ref[at].astype(F32) + other[other_at].astype(F32)).astype(BF16)
 
-    stage_one = [None, None]
+    order = [[wrap(h.p + d, 4) for d in (2, 1, -1, 0)] for h in halves]
+    fars, nears, adds, lasts = [[], []], [[], []], [[], []], [[], []]
     for i, h in enumerate(halves):
-        down(i, wrap(h.q + 2, 4))
-        o, at = os[i], h.group(wrap(h.q + 2, 4))
-        stage_one[i] = [
-            send(o.at[at + (every, lo)], far.at[i, 0], i, 0, 0, h.two(1)),
-            send(o.at[at + (every, hi)], far.at[i, 1], i, 0, 1, h.two(-1)),
-        ]
+        v = wrap(h.q + 2, 4)
+        down(i, v)
+        for k, u in enumerate(order[i]):
+            at = h.unit(u, v)
+            fars[i].append(
+                [
+                    send(os[i].at[at + (every, lo)], far.at[i, 0, u], i, k, h.two(1)),
+                    send(os[i].at[at + (every, hi)], far.at[i, 1, u], i, 4 + k, h.two(-1)),
+                ]
+            )
     for i, h in enumerate(halves):
-        o = os[i]
-        down(i, wrap(h.q + 1, 4))
-        at = h.group(wrap(h.q + 1, 4))
-        stage_one[i].append(
-            send(o.at[at + (every, hi)], near.at[i, 0, :, :, hi], i, 0, 2, h.two(1))
-        )
-        down(i, wrap(h.q - 1, 4))
-        at = h.group(wrap(h.q - 1, 4))
-        stage_one[i].append(
-            send(o.at[at + (every, lo)], near.at[i, 1, :, :, lo], i, 0, 3, h.two(-1))
-        )
+        for v, d, cols, b in ((wrap(h.q + 1, 4), 1, hi, 0), (wrap(h.q - 1, 4), -1, lo, 1)):
+            down(i, v)
+            src = os[i].at[h.group(v) + (every, cols)]
+            nears[i].append(send(src, near.at[i, b, :, :, cols], i, 8 + b, h.two(d)))
+    down(0, halves[0].q)
+    for k in range(4):
+        for i, h in enumerate(halves):
+            u, moves = order[i][k], []
+            for b, d, cols in ((0, 1, lo), (1, -1, hi)):
+                fars[i][k][b].wait_recv()
+                at = h.unit(u, wrap(h.q + d, 4)) + (every, cols)
+                add_into(os[i], at, far, (i, b, u))
+                dst = near.at[i, b, u, :, cols]
+                moves.append(send(os[i].at[at], dst, i, 10 + 4 * b + k, h.two(d)))
+            adds[i].append(moves)
+    down(1, halves[1].q)
+    for i in range(2):
+        for c in nears[i]:
+            c.wait_recv()
+    for k in range(4):
+        for i, h in enumerate(halves):
+            u = order[i][k]
+            for c in adds[i][k]:
+                c.wait_recv()
+            mine = os[i][h.unit(u, h.q)].astype(F32)
+            mine = mine + near[i, 0, u].astype(F32) + near[i, 1, u].astype(F32)
+            tot[i, u] = mine.astype(BF16)
+            if k == 0:
+                lasts[i].append(send(tot.at[i, u, :, lo], far2.at[i, 0], i, 18, h.one(1)))
+                lasts[i].append(send(tot.at[i, u, :, hi], far2.at[i, 1], i, 19, h.one(-1)))
+            if k == 1:
+                lasts[i].append(send(tot.at[i, u, :, hi], near2.at[i, 0, :, hi], i, 20, h.one(1)))
+            if k == 2:
+                lasts[i].append(send(tot.at[i, u, :, lo], near2.at[i, 1, :, lo], i, 21, h.one(-1)))
     for i, h in enumerate(halves):
-        down(i, h.q)
+        for b, d, cols in ((0, 1, lo), (1, -1, hi)):
+            u = order[i][1 + b]
+            lasts[i][b].wait_recv()
+            add_into(tot, (i, u, every, cols), far2, (i, b))
+            dst = near2.at[i, b, :, cols]
+            lasts[i].append(send(tot.at[i, u, :, cols], dst, i, 22 + b, h.one(d)))
+
+    across = (((0,), (0,)), ((), ()))
+    returns = []
     for i, h in enumerate(halves):
-        o = os[i]
-        stage_one[i][0].wait_recv()
-        at = h.group(wrap(h.q + 1, 4)) + (every, lo)
-        add_into(o, at, far, (i, 0))
-        stage_one[i].append(send(o.at[at], near.at[i, 0, :, :, lo], i, 0, 4, h.two(1)))
-        stage_one[i][1].wait_recv()
-        at = h.group(wrap(h.q - 1, 4)) + (every, hi)
-        add_into(o, at, far, (i, 1))
-        stage_one[i].append(send(o.at[at], near.at[i, 1, :, :, hi], i, 0, 5, h.two(-1)))
-
-    stage_two = [None, None]
-    for i, h in enumerate(halves):
-        for c in stage_one[i][2:]:
+        for c in lasts[i][2:]:
             c.wait_recv()
-
-        def total(u):
-            mine = os[i][h.unit(u, h.q)].astype(F32)
-            tot[i, u] = (mine + near[i, 0, u].astype(F32) + near[i, 1, u].astype(F32)).astype(BF16)
-
-        opposite, ahead, behind = wrap(h.p + 2, 4), wrap(h.p + 1, 4), wrap(h.p - 1, 4)
-        total(opposite)
-        stage_two[i] = [
-            send(tot.at[i, opposite, :, lo], far2.at[i, 0], i, 1, 0, h.one(1)),
-            send(tot.at[i, opposite, :, hi], far2.at[i, 1], i, 1, 1, h.one(-1)),
-        ]
-        total(ahead)
-        total(behind)
-        stage_two[i].append(send(tot.at[i, ahead, :, hi], near2.at[i, 0, :, hi], i, 1, 2, h.one(1)))
-        stage_two[i].append(
-            send(tot.at[i, behind, :, lo], near2.at[i, 1, :, lo], i, 1, 3, h.one(-1))
-        )
-        total(h.p)
-    for i, h in enumerate(halves):
-        ahead, behind = wrap(h.p + 1, 4), wrap(h.p - 1, 4)
-        stage_two[i][0].wait_recv()
-        add_into(tot, (i, ahead, every, lo), far2, (i, 0))
-        stage_two[i].append(send(tot.at[i, ahead, :, lo], near2.at[i, 0, :, lo], i, 1, 4, h.one(1)))
-        stage_two[i][1].wait_recv()
-        add_into(tot, (i, behind, every, hi), far2, (i, 1))
-        stage_two[i].append(
-            send(tot.at[i, behind, :, hi], near2.at[i, 1, :, hi], i, 1, 5, h.one(-1))
-        )
-    ends = []
-    for i, h in enumerate(halves):
-        for c in stage_two[i][2:]:
-            c.wait_recv()
-        final = (
-            tot[i, h.p].astype(F32) + near2[i, 0].astype(F32) + near2[i, 1].astype(F32)
-        ).astype(BF16)
-        ends.append(final)
-
-    across = (((0,), (0,)), ((), ()))
-    back = lax.dot_general(pick_a[...], ends[0], across, preferred_element_type=F32)
-    back = back + lax.dot_general(pick_b[...], ends[1], across, preferred_element_type=F32)
-    go[...] = back.astype(BF16).reshape(8, 16, 2048)
-    sends = []
-    for d in range(1, 8):
-        peer = lax.rem(exp + d, 8)
-        c = remote(go.at[peer], rback.at[exp], r_send.at[d], r_recv.at[d], {"exp": peer})
-        c.start()
-        sends.append(c)
-    rback[pl.ds(exp, 1)] = go[pl.ds(exp, 1)]
-    for c in sends:
-        c.wait_recv()
-    flat = rback[...].reshape(128, 2048)
+        final = tot[i, h.p].astype(F32) + near2[i, 0].astype(F32) + near2[i, 1].astype(F32)
+        final = final.astype(BF16)
+        back = jnp.zeros((128, 768), F32)
+        for k, w in enumerate(windows):
+            block = final[:, w : w + 768]
+            back = back + lax.dot_general(pick[k], block, across, preferred_element_type=F32)
+        for c in dispatch[i]:
+            c.wait_send()
+        go[i] = back.astype(BF16).reshape(8, 16, 768)
+        returns.append(all_to_all(i, rback, r_send, r_recv))
     eye = lax.broadcasted_iota(jnp.int32, (16, 16), 0) == lax.broadcasted_iota(
         jnp.int32, (16, 16), 1
     )
     gate = jnp.sum(jnp.where(eye, jnp.broadcast_to(gate_row, (16, 16)), 0.0), axis=1, keepdims=True)
     for i in range(2):
-        cols = pl.ds(i * 2048, 2048)
-        pair = [
-            lax.dot_general(fetch[i, k], flat, across, preferred_element_type=F32)
-            for k in range(2)
-        ]
-        mix = gate * pair[0] + (1.0 - gate) * pair[1]
-        out[:, cols] = (stream[:, cols] + mix).astype(BF16)
-    for c in sends + sent:
-        c.wait_send()
+        for c in returns[i]:
+            c.wait_recv()
+        flat = rback[i].reshape(128, 768)
+        for j, w in enumerate(windows):
+            cols = pl.ds(i * 2048 + w, 768)
+            pair = [
+                lax.dot_general(fetch[j, k], flat, across, preferred_element_type=F32)
+                for k in range(2)
+            ]
+            mix = gate * pair[0] + (1.0 - gate) * pair[1]
+            out[:, cols] = (stream[:, cols] + mix).astype(BF16)
+    early = dispatch[0] + dispatch[1]
+    for c in sent:
+        if not any(c is other for other in early):
+            c.wait_send()
 
 
 def token_places(ids, spread, fetch):
@@ -730,14 +722,14 @@
     )
     earlier = dot(either, jnp.where(before, 1.0, 0.0).astype(BF16))
     rows = lax.broadcasted_iota(jnp.int32, (128, 16), 0).astype(F32)
-    for half in range(2):
+    for j in range(3):
         found = []
         for k in range(2):
             slot = jnp.sum(jnp.where(hits[k], earlier, 0.0), axis=0, keepdims=True)
-            place = ids[k : k + 1].astype(F32) * 16.0 + slot + half * 8.0
+            place = ids[k : k + 1].astype(F32) * 16.0 + slot + j * 5.0
             found.append(jnp.where(rows == place, 1.0, 0.0))
-            fetch[half, k] = found[k].astype(BF16)
-        spread[half] = (found[0] + found[1]).astype(BF16)
+            fetch[j, k] = found[k].astype(BF16)
+        spread[j] = (found[0] + found[1]).astype(BF16)
 
 
 def block_kernel(*refs):
@@ -783,11 +775,11 @@
     w_down,
     expert_ids,
 ):
-    pick = np.zeros((2, 40, 128), np.float32)
-    for j in range(8):
-        for s in range(5):
-            pick[0, j * 5 + s, j * 16 + s] = 1.0
-            pick[1, j * 5 + s, j * 16 + 8 + s] = 1.0
+    pick = np.zeros((3, 40, 128), np.float32)
+    for w in range(3):
+        for j in range(8):
+            for s in range(5):
+                pick[w, j * 5 + s, j * 16 + w * 5 + s] = 1.0
     vmem = pl.BlockSpec(memory_space=pltpu.VMEM)
     anywhere = pl.BlockSpec(memory_space=pl.ANY)
     return pl.pallas_call(
@@ -820,8 +812,7 @@
         w_gate,
         w_up,
         w_down,
-        jnp.asarray(pick[0], BF16),
-        jnp.asarray(pick[1], BF16),
+        jnp.asarray(pick, BF16),
     )
 
 

time: 155 us -> 142 us (0.916)
  Pallas kernels: 153 us -> 141 us
    pallas_call x1, Pallas kernels: 153 us -> 141 us  [shards(): pl.pallas_call(block_kernel, out_shape=jax.ShapeDtypeStruct((16, 4096), B...]
where the time goes in v4:
time: 142 us
  Pallas kernels  141 us (99%)
  local copies, waits for them, and re-layouts  1.57 us (1%)
    pallas_call x1, Pallas kernels, shards(): pl.pallas_call(block_kernel, out_shape=jax.ShapeDtypeStruct((16, 4096), B...  141 us

profile of v4, /device:TPU:1, one launch (start us, length us, event | category | flops | bytes accessed | tf_op | source)
XLA Modules:
  0.0 142.2 jit_solution(4996957093918709652)
XLA Ops:
  0.0 140.7 %shard_map.172 = bf16[16,4096]{1,0:T(8,128)(2,1)} custom-call(bf16[128,1024]{1,0:T(8,128)(2,1)} %refs_0_.1, bf16[128,1024]{1,0:T(8,128)(2,1)} %refs_1_.1, f32[4,1024]{1,0:T(4,128)} %refs_2_.1, f32[1,1024]{1,0:T(1,128)} %bitcast.10, bf16[544,1024]{1,0:T(8,128)(2,1)} %bitcast.7, bf16[512,1024]{1,0:T(8,128)(2,1)} %refs_5_.1, f32[1,1024]{1,0:T(1,128)} %bitcast.11, ...), custom_call_target="tpu_custom_call" | custom-call | flops 13500000256 | bytes 24000000 | tf_op jit(solution)/shard_map/pallas_call | solution.py:785
  140.7 1.6 %copy.20 = bf16[16,4096]{1,0:T(8,128)(2,1)} copy(bf16[16,4096]{1,0:T(8,128)(2,1)} %shard_map.172) | data formatting | bytes 262144

commit v5 on v4

--- a/solution.py
+++ b/solution.py
@@ -26,7 +26,11 @@
     barrier = pltpu.get_barrier_semaphore()
     for device in devices:
         pl.semaphore_signal(barrier, inc=1, device_id=device, device_id_type=pl.DeviceIdType.MESH)
-    pl.semaphore_wait(barrier, len(devices))
+    return lambda: pl.semaphore_wait(barrier, len(devices))
+
+
+def settle(view, sem):
+    pltpu.make_async_copy(view, view, sem).wait()
 
 
 def wrap(index, count):
@@ -87,6 +91,8 @@
 
 SCRATCH = {
     "stream": pltpu.VMEM((16, 4096), F32),
+    "result": pltpu.VMEM((16, 4096), BF16),
+    "e_sem": pltpu.SemaphoreType.DMA((2,)),
     "normed": pltpu.VMEM((16, 4096), BF16),
     "spread": pltpu.VMEM((3, 128, 16), BF16),
     "fetch": pltpu.VMEM((3, 2, 128, 16), BF16),
@@ -116,20 +122,17 @@
     "ms": pltpu.VMEM((3, 16, 1024), BF16),
     "mo": pltpu.VMEM((4, 16, 1024), BF16),
     "h_sem": pltpu.SemaphoreType.DMA((2,)),
-    "a_send": pltpu.SemaphoreType.DMA((8,)),
-    "a_recv": pltpu.SemaphoreType.DMA((8,)),
-    "b_send": pltpu.SemaphoreType.DMA((16,)),
-    "b_recv": pltpu.SemaphoreType.DMA((16,)),
-    "o_send": pltpu.SemaphoreType.DMA((4,)),
-    "o_recv": pltpu.SemaphoreType.DMA((4,)),
-    "c_send": pltpu.SemaphoreType.DMA((12,)),
-    "c_recv": pltpu.SemaphoreType.DMA((12,)),
-    "g_send": pltpu.SemaphoreType.DMA((6,)),
-    "g_recv": pltpu.SemaphoreType.DMA((6,)),
-    "z_send": pltpu.SemaphoreType.DMA((4, 8)),
-    "z_recv": pltpu.SemaphoreType.DMA((4, 8)),
-    "m_send": pltpu.SemaphoreType.DMA((4,)),
-    "m_recv": pltpu.SemaphoreType.DMA((4,)),
+    "a_sem": pltpu.SemaphoreType.DMA((2,)),
+    "b_sem": pltpu.SemaphoreType.DMA((4,)),
+    "o_send": pltpu.SemaphoreType.DMA((1,)),
+    "o_recv": pltpu.SemaphoreType.DMA((3,)),
+    "c_send": pltpu.SemaphoreType.DMA((2, 2)),
+    "c_recv": pltpu.SemaphoreType.DMA((2, 2)),
+    "g_send": pltpu.SemaphoreType.DMA((1,)),
+    "g_recv": pltpu.SemaphoreType.DMA((5,)),
+    "z_send": pltpu.SemaphoreType.DMA((1,)),
+    "z_recv": pltpu.SemaphoreType.DMA((4,)),
+    "m_sem": pltpu.SemaphoreType.DMA((2,)),
     "l_sem": pltpu.SemaphoreType.DMA((1,)),
     "go": pltpu.VMEM((2, 8, 16, 768), BF16),
     "rcv": pltpu.VMEM((2, 8, 16, 768), BF16),
@@ -138,7 +141,8 @@
     "xb": pltpu.VMEM((4, 4, 40, 2048), BF16),
     "wgu": pltpu.VMEM((4096, 1536), BF16),
     "wd": pltpu.VMEM((768, 4096), BF16),
-    "lhs": pltpu.VMEM((160, 2048), BF16),
+    "lhs": pltpu.VMEM((4, 40, 2048), BF16),
+    "lhs_down": pltpu.VMEM((6, 40, 768), BF16),
     "acc": pltpu.VMEM((4, 4, 40, 1536), F32),
     "hid": pltpu.VMEM((4, 4, 40, 768), BF16),
     "oa": pltpu.VMEM((4, 4, 40, 2048), BF16),
@@ -149,18 +153,18 @@
     "far2": pltpu.VMEM((2, 2, 40, 1024), BF16),
     "near2": pltpu.VMEM((2, 2, 40, 2048), BF16),
     "w_sem": pltpu.SemaphoreType.DMA((3,)),
-    "d_send": pltpu.SemaphoreType.DMA((2, 8)),
-    "d_recv": pltpu.SemaphoreType.DMA((2, 8)),
-    "u_send": pltpu.SemaphoreType.DMA((2, 5, 4)),
-    "u_recv": pltpu.SemaphoreType.DMA((2, 5, 4)),
-    "s_send": pltpu.SemaphoreType.DMA((2, 24)),
-    "s_recv": pltpu.SemaphoreType.DMA((2, 24)),
-    "r_send": pltpu.SemaphoreType.DMA((2, 8)),
-    "r_recv": pltpu.SemaphoreType.DMA((2, 8)),
+    "d_send": pltpu.SemaphoreType.DMA((2,)),
+    "d_recv": pltpu.SemaphoreType.DMA((2,)),
+    "u_send": pltpu.SemaphoreType.DMA((2, 3)),
+    "u_recv": pltpu.SemaphoreType.DMA((2, 8)),
+    "s_send": pltpu.SemaphoreType.DMA((2, 2)),
+    "s_recv": pltpu.SemaphoreType.DMA((2, 11)),
+    "r_send": pltpu.SemaphoreType.DMA((2,)),
+    "r_recv": pltpu.SemaphoreType.DMA((2,)),
 }
 
 
-def mixer(r, ctx, exp, mx, my):
+def mixer(r, ctx, exp, mx, my, arrive):
     mixer_in = r["mixer_in"]
     gate_in = r["gate_in"]
     conv_weight = r["conv_weight"]
@@ -203,10 +207,8 @@
     ms = r["ms"]
     mo = r["mo"]
     h_sem = r["h_sem"]
-    a_send = r["a_send"]
-    a_recv = r["a_recv"]
-    b_send = r["b_send"]
-    b_recv = r["b_recv"]
+    a_sem = r["a_sem"]
+    b_sem = r["b_sem"]
     o_send = r["o_send"]
     o_recv = r["o_recv"]
     c_send = r["c_send"]
@@ -215,8 +217,7 @@
     g_recv = r["g_recv"]
     z_send = r["z_send"]
     z_recv = r["z_recv"]
-    m_send = r["m_send"]
-    m_recv = r["m_recv"]
+    m_sem = r["m_sem"]
     l_sem = r["l_sem"]
     every = slice(None)
 
@@ -230,20 +231,10 @@
         return {"exp": lax.rem(exp + d, 8)}
 
     ahead = {"ctx": lax.rem(ctx + 1, 16)}
-    sent = []
 
     def send(src, dst, ss, rs, device):
-        c = remote(src, dst, ss, rs, device)
-        c.start()
-        sent.append(c)
-        return c
-
-    halo = send(mixer_in.at[pl.ds(112, 16)], rim, h_sem.at[0], h_sem.at[1], ahead)
-    columns = [
-        send(out_proj, opg.at[my], o_send.at[0], o_recv.at[0], along_y(1)),
-        send(out_proj, opg.at[my], o_send.at[1], o_recv.at[1], along_y(-1)),
-    ]
-    opg[pl.ds(my, 1)] = out_proj[...][None]
+        remote(src, dst, ss, rs, device).start()
+
     padded[pl.ds(8, 128), :] = mixer_in[...].astype(F32)
     for g in range(8):
         rate_t[pl.ds(g, 16, stride=8), :] = decay_rate[:, g * 128 : (g + 1) * 128] * (-LOG2E)
@@ -257,42 +248,45 @@
                 total = total + taps * padded[pl.ds(start + 5 + k, rows), cols]
             conv_out[pl.ds(start, rows), cols] = (total * jax.nn.sigmoid(total)).astype(BF16)
 
+    def channel_sums(start, rows):
+        sums = dot_t(conv_out[pl.ds(start, rows), :], x_proj[...]).astype(BF16)
+        part[pl.ds(start // 16, rows // 16)] = sums.reshape(rows // 16, 16, 544)
+
     convolve(16, 112)
-    halo.wait_recv()
+
+    arrive()
+    send(mixer_in.at[pl.ds(112, 16)], rim, h_sem.at[0], h_sem.at[1], ahead)
+    send(out_proj, opg.at[my], o_send.at[0], o_recv.at[0], along_y(1))
+    send(out_proj, opg.at[my], o_send.at[0], o_recv.at[1], along_y(-1))
+    opg[pl.ds(my, 1)] = out_proj[...][None]
+    channel_sums(16, 112)
+    settle(rim, h_sem.at[1])
     keep = jnp.where(ctx > 0, 1.0, 0.0).astype(F32)
     padded[pl.ds(0, 8), :] = rim[pl.ds(0, 16), :].astype(F32)[8:] * keep
     convolve(0, 16)
-
-    part[...] = dot_t(conv_out[...], x_proj[...]).astype(BF16).reshape(8, 16, 544)
-    scatter = [
-        send(part.at[lax.rem(exp + d, 8)], parts.at[exp], a_send.at[d], a_recv.at[d], peer(d))
-        for d in range(1, 8)
-    ]
+    channel_sums(0, 16)
+
+    for d in range(1, 8):
+        src = part.at[lax.rem(exp + d, 8)]
+        send(src, parts.at[exp], a_sem.at[0], a_sem.at[1], peer(d))
     parts[pl.ds(exp, 1)] = part[pl.ds(exp, 1)]
-    for c in scatter:
-        c.wait_recv()
+    settle(parts.at[pl.ds(0, 7)], a_sem.at[1])
     total = parts[0].astype(F32)
     for j in range(1, 8):
         total = total + parts[j].astype(F32)
     low_rank[pl.ds(exp, 1)] = total[:, :512].astype(BF16)[None]
     maps[pl.ds(exp, 1), :, pl.ds(0, 32)] = total[:, 512:][None]
-    gather = []
     for d in range(1, 8):
         for k, ref in enumerate((low_rank, maps)):
-            s = 2 * d + k
-            gather.append(send(ref.at[exp], ref.at[exp], b_send.at[s], b_recv.at[s], peer(d)))
-    for c in gather:
-        c.wait_recv()
+            send(ref.at[exp], ref.at[exp], b_sem.at[k], b_sem.at[2 + k], peer(d))
+    settle(low_rank.at[pl.ds(0, 7)], b_sem.at[2])
+    settle(maps.at[pl.ds(0, 7)], b_sem.at[3])
     top, low = pl.ds(0, 512), pl.ds(512, 512)
     left, right = wrap(my - 1, 4), wrap(my + 1, 4)
-    columns[0].wait_recv()
-    columns.append(
-        send(opg.at[left, top], opg.at[left, top], o_send.at[2], o_recv.at[2], along_y(1))
-    )
-    columns[1].wait_recv()
-    columns.append(
-        send(opg.at[right, low], opg.at[right, low], o_send.at[3], o_recv.at[3], along_y(-1))
-    )
+    settle(opg.at[0], o_recv.at[0])
+    send(opg.at[left, top], opg.at[left, top], o_send.at[0], o_recv.at[2], along_y(1))
+    settle(opg.at[0], o_recv.at[1])
+    send(opg.at[right, low], opg.at[right, low], o_send.at[0], o_recv.at[2], along_y(-1))
     scalars = pltpu.make_async_copy(maps, bc_s, l_sem.at[0])
     scalars.start()
     step_low = low_rank[...].reshape(128, 512)
@@ -329,18 +323,14 @@
 
     def exchange(finals, total, fin, sums, place, base, step):
         for n in range(16):
-            fin_own[base // 6, pl.ds(n * 8, 8), :] = finals[n].astype(BF16)
+            fin_own[base, pl.ds(n * 8, 8), :] = finals[n].astype(BF16)
         sums[pl.ds(place, 1)] = total[None]
-        fin[pl.ds(place, 1)] = fin_own[base // 6][None]
-        moves = []
-        for k, d in enumerate((1, -1, 2)):
-            s, r = base + 2 * k, base + 2 * k + 1
-            moves.append(
-                send(fin_own.at[base // 6], fin.at[place], c_send.at[s], c_recv.at[s], step(d))
-            )
-            moves.append(send(sums.at[place], sums.at[place], c_send.at[r], c_recv.at[r], step(d)))
-        for c in moves:
-            c.wait_recv()
+        fin[pl.ds(place, 1)] = fin_own[base][None]
+        for d in (1, -1, 2):
+            send(fin_own.at[base], fin.at[place], c_send.at[0, base], c_recv.at[0, base], step(d))
+            send(sums.at[place], sums.at[place], c_send.at[1, base], c_recv.at[1, base], step(d))
+        settle(fin.at[pl.ds(0, 3)], c_recv.at[0, base])
+        settle(sums.at[pl.ds(0, 3)], c_recv.at[1, base])
 
     exchange(states, running, fin_y, sum_y, my, 0, along_y)
     before, row_total = zero, zero
@@ -357,7 +347,7 @@
             whole = decay * whole + own
         enter_t[pl.ds(n * 8, 8), :] = entering
         row_final.append(whole)
-    exchange(row_final, row_total, fin_x, sum_x, mx, 6, along_x)
+    exchange(row_final, row_total, fin_x, sum_x, mx, 1, along_x)
     for n in range(16):
         entering = zero
         for u in range(4):
@@ -377,7 +367,6 @@
         return carry
 
     entered = [enter_t[pl.ds(n * 8, 8), :] for n in range(16)]
-    moves = []
     for half in range(2):
         lax.fori_loop(half * 64, half * 64 + 64, add_entering, 0, unroll=2)
         rows = pl.ds(half * 64, 64)
@@ -390,7 +379,7 @@
         place = ga.at[mx, rows]
         for k, d in enumerate((1, -1)):
             s = half * 2 + k
-            moves.append(send(place, place, g_send.at[s], g_recv.at[s], along_x(d)))
+            send(place, place, g_send.at[0], g_recv.at[s], along_x(d))
 
     def project(u):
         for v in range(4):
@@ -400,34 +389,29 @@
         rz[pl.ds(u, 1), pl.ds(exp, 1)] = zs[pl.ds(u, 1), pl.ds(exp, 1)]
 
     def scatter_group(k, u):
-        return [
-            send(zs.at[u, lax.rem(exp + d, 8)], rz.at[u, exp], z_send.at[k, d], z_recv.at[k, d], peer(d))
-            for d in range(1, 8)
-        ]
-
-    for c in columns[2:]:
-        c.wait_recv()
+        for d in range(1, 8):
+            src = zs.at[u, lax.rem(exp + d, 8)]
+            send(src, rz.at[u, exp], z_send.at[0], z_recv.at[k], peer(d))
+
+    settle(opg.at[0], o_recv.at[2])
     left, right, far = wrap(mx - 1, 4), wrap(mx + 1, 4), wrap(mx + 2, 4)
     top, low = pl.ds(0, 64), pl.ds(64, 64)
     project(mx)
-    groups = [scatter_group(0, mx)]
-    moves[0].wait_recv()
-    moves.append(send(ga.at[left, top], ga.at[left, top], g_send.at[4], g_recv.at[4], along_x(1)))
-    moves[1].wait_recv()
-    moves[3].wait_recv()
-    moves.append(send(ga.at[right, low], ga.at[right, low], g_send.at[5], g_recv.at[5], along_x(-1)))
-    moves[2].wait_recv()
+    scatter_group(0, mx)
+    settle(ga.at[0, top], g_recv.at[0])
+    send(ga.at[left, top], ga.at[left, top], g_send.at[0], g_recv.at[4], along_x(1))
+    settle(ga.at[0, top], g_recv.at[1])
+    settle(ga.at[0, top], g_recv.at[3])
+    send(ga.at[right, low], ga.at[right, low], g_send.at[0], g_recv.at[4], along_x(-1))
+    settle(ga.at[0, top], g_recv.at[2])
     for k, u in ((1, left), (2, right)):
         project(u)
-        groups.append(scatter_group(k, u))
-    moves[4].wait_recv()
-    moves[5].wait_recv()
+        scatter_group(k, u)
+    settle(ga.at[0], g_recv.at[4])
     project(far)
-    groups.append(scatter_group(3, far))
-    backs = []
+    scatter_group(3, far)
     for k, (u, d) in enumerate(((mx, 0), (left, -1), (right, 1), (far, 2))):
-        for c in groups[k]:
-            c.wait_recv()
+        settle(rz.at[0, pl.ds(0, 7)], z_recv.at[k])
         total = rz[u, 0].astype(F32)
         for j in range(1, 8):
             total = total + rz[u, j].astype(F32)
@@ -435,9 +419,8 @@
             mo[pl.ds(mx, 1)] = total.astype(BF16)[None]
         else:
             ms[k - 1] = total.astype(BF16)
-            backs.append(send(ms.at[k - 1], mo.at[mx], m_send.at[k], m_recv.at[k], along_x(d)))
-    for c in backs:
-        c.wait_recv()
+            send(ms.at[k - 1], mo.at[mx], m_sem.at[0], m_sem.at[1], along_x(d))
+    settle(mo.at[pl.ds(0, 3)], m_sem.at[1])
 
     squares = jnp.zeros((16, 1), F32)
     for u in range(4):
@@ -456,11 +439,27 @@
     lanes = lax.broadcasted_iota(jnp.int32, (8, 16), 0)
     signs = jnp.where(ids[0:1] == lanes, 1.0, 0.0) - jnp.where(ids[1:2] == lanes, 1.0, 0.0)
     first = jax.nn.sigmoid(jnp.sum(logits * signs, axis=0, keepdims=True))
-    return first, sent
-
-
-def experts(r, gate_row, sent, out, exp, mx, my, halves, loads):
+
+    def drain():
+        settle(rim, h_sem.at[0])
+        settle(opg.at[pl.ds(0, 3)], o_send.at[0])
+        settle(parts.at[pl.ds(0, 7)], a_sem.at[0])
+        settle(low_rank.at[pl.ds(0, 7)], b_sem.at[0])
+        settle(maps.at[pl.ds(0, 7)], b_sem.at[1])
+        for base, (fin, sums) in enumerate(((fin_y, sum_y), (fin_x, sum_x))):
+            settle(fin.at[pl.ds(0, 3)], c_send.at[0, base])
+            settle(sums.at[pl.ds(0, 3)], c_send.at[1, base])
+        settle(ga.at[pl.ds(0, 3)], g_send.at[0])
+        settle(rz.at[:, pl.ds(0, 7)], z_send.at[0])
+        settle(mo.at[pl.ds(0, 3)], m_sem.at[0])
+
+    return first, drain
+
+
+def experts(r, gate_row, drain, out, exp, mx, my, halves, loads):
     pick = r["pick"]
+    result = r["result"]
+    e_sem = r["e_sem"]
     stream = r["stream"]
     normed = r["normed"]
     spread = r["spread"]
@@ -473,6 +472,7 @@
     wgu = r["wgu"]
     wd = r["wd"]
     lhs = r["lhs"]
+    lhs_down = r["lhs_down"]
     acc = r["acc"]
     hid = r["hid"]
     oa = r["oa"]
@@ -497,207 +497,203 @@
     windows = (0, 768, 1280)
 
     def all_to_all(half, into, ss, rs):
-        moves = []
         for d in range(1, 8):
             peer = lax.rem(exp + d, 8)
             src, dst = go.at[half, peer], into.at[half, exp]
-            c = remote(src, dst, ss.at[half, d], rs.at[half, d], {"exp": peer})
-            c.start()
-            moves.append(c)
+            remote(src, dst, ss.at[half], rs.at[half], {"exp": peer}).start()
         into[half, pl.ds(exp, 1)] = go[half, pl.ds(exp, 1)]
-        sent.extend(moves)
-        return moves
-
-    dispatch = []
+
     for i in range(2):
         packed = jnp.zeros((128, 768), F32)
         for k, w in enumerate(windows):
             packed = packed + dot(spread[k], normed[:, pl.ds(i * 2048 + w, 768)])
         go[i] = packed.astype(BF16).reshape(8, 16, 768)
-        dispatch.append(all_to_all(i, rcv, d_send, d_recv))
+        all_to_all(i, rcv, d_send, d_recv)
     acc[...] = jnp.zeros_like(acc)
 
-    def push(h, x, at, cols, g, k, device):
-        place = x.at[at + (every, cols)] if cols is not None else x.at[at]
-        c = remote(place, place, u_send.at[h, g, k], u_recv.at[h, g, k], device)
-        c.start()
-        sent.append(c)
-        return c
-
-    first, second = [], [[None] * 4, [None] * 4]
+    def push(i, at, cols, ss, rs, device):
+        place = xs[i].at[at + (every, cols)] if cols is not None else xs[i].at[at]
+        remote(place, place, u_send.at[i, ss], u_recv.at[i, rs], device).start()
+
     steps = [[wrap(h.p + d, 4) for d in (0, -1, 1, 2)] for h in halves]
 
     def second_start(i, g):
-        h, x = halves[i], xs[i]
+        h = halves[i]
         at = h.unit(steps[i][g], h.q)
-        second[i][g] = [
-            push(i, x, at, None, g + 1, 0, h.two(1)),
-            push(i, x, at, None, g + 1, 1, h.two(-1)),
-        ]
+        push(i, at, None, 1, 3 + g, h.two(1))
+        push(i, at, None, 1, 3 + g, h.two(-1))
 
     def second_pass(i, g):
-        h, x, u = halves[i], xs[i], steps[i][g]
-        second[i][g][0].wait_recv()
-        a = push(i, x, h.unit(u, wrap(h.q - 1, 4)), lo, g + 1, 2, h.two(1))
-        second[i][g][1].wait_recv()
-        b = push(i, x, h.unit(u, wrap(h.q + 1, 4)), hi, g + 1, 3, h.two(-1))
-        second[i][g] += [a, b]
+        h, u = halves[i], steps[i][g]
+        settle(xs[i].at[0, pl.ds(0, 2)], u_recv.at[i, 3 + g])
+        push(i, h.unit(u, wrap(h.q - 1, 4)), lo, 2, 7, h.two(1))
+        push(i, h.unit(u, wrap(h.q + 1, 4)), hi, 2, 7, h.two(-1))
 
     for i, (h, x) in enumerate(zip(halves, xs)):
-        for c in dispatch[i]:
-            c.wait_recv()
+        settle(rcv.at[i, pl.ds(0, 7)], d_recv.at[i])
         flat = rcv[i].reshape(128, 768)
         for k, w in enumerate(windows):
             block = dot(pick[k], flat).astype(BF16)[None, None]
             x[pl.ds(mx, 1), pl.ds(my, 1), :, pl.ds(w, 768)] = block
         at = h.unit(h.p, h.q)
-        first.append(
-            [push(i, x, at, None, 0, 0, h.one(1)), push(i, x, at, None, 0, 1, h.one(-1))]
-        )
-        second_start(i, 0)
+        push(i, at, None, 0, 0, h.one(1))
+        push(i, at, None, 0, 1, h.one(-1))
+        if i == 0:
+            second_start(0, 0)
     for i, (h, x) in enumerate(zip(halves, xs)):
-        first[i][0].wait_recv()
-        first[i].append(push(i, x, h.unit(steps[i][1], h.q), lo, 0, 2, h.one(1)))
-        first[i][1].wait_recv()
-        first[i].append(push(i, x, h.unit(steps[i][2], h.q), hi, 0, 3, h.one(-1)))
+        settle(x.at[0, 0], u_recv.at[i, 0])
+        push(i, h.unit(steps[i][1], h.q), lo, 0, 2, h.one(1))
+        settle(x.at[0, 0], u_recv.at[i, 1])
+        push(i, h.unit(steps[i][2], h.q), hi, 0, 2, h.one(-1))
+        if i == 0:
+            second_start(1, 0)
     second_start(0, 1)
     second_start(1, 1)
     for i in range(2):
-        first[i][2].wait_recv()
-        first[i][3].wait_recv()
+        settle(xs[i].at[0, 0], u_recv.at[i, 2])
         second_start(i, 2)
         second_start(i, 3)
 
-    def gate_up(i, v):
-        at = halves[i].group(v)
-        lhs[...] = xs[i][at].reshape(160, 2048)
+    def gate_up(i, units):
+        for n, at in enumerate(units):
+            lhs[n] = xs[i][at]
         for j in range(6):
             cols = pl.ds(j * 256, 256)
-            part = dot(lhs[...], wgu[pl.ds(i * 2048, 2048), cols])
-            place = at + (every, cols)
-            acc[place] = acc[place] + part.reshape(4, 40, 256)
+            part = dot(lhs[...].reshape(160, 2048), wgu[pl.ds(i * 2048, 2048), cols])
+            for n, at in enumerate(units):
+                place = at + (every, cols)
+                acc[place] = acc[place] + part[n * 40 : (n + 1) * 40]
+
+    def line(i, v):
+        return [halves[i].unit(u, v) for u in steps[i]]
+
+    def beside(i, gs):
+        h = halves[i]
+        return [h.unit(steps[i][g], wrap(h.q + d, 4)) for g in gs for d in (-1, 1)]
 
     loads[0].wait()
     loads[1].wait()
-    gate_up(0, halves[0].q)
+    gate_up(0, line(0, halves[0].q))
     second_pass(0, 0)
     second_pass(1, 0)
-    gate_up(1, halves[1].q)
-    for g in range(1, 4):
-        second_pass(0, g)
-        second_pass(1, g)
-    for i, h in enumerate(halves):
-        gate_up(i, wrap(h.q - 1, 4))
-        gate_up(i, wrap(h.q + 1, 4))
-    for i, h in enumerate(halves):
-        for g in range(4):
-            second[i][g][2].wait_recv()
-            second[i][g][3].wait_recv()
-        gate_up(i, wrap(h.q + 2, 4))
-
-    @pl.loop(0, 16)
-    def _(n):
-        at = (n // 4, n % 4)
-        gate = acc[at + (every, pl.ds(0, 768))]
-        up = acc[at + (every, pl.ds(768, 768))]
-        hid[at] = (gate * jax.nn.sigmoid(gate) * up).astype(BF16)
-
-    loads[2].wait()
-
-    def down(i, v):
-        at = halves[i].group(v)
-        lhs[:, pl.ds(0, 768)] = hid[at].reshape(160, 768)
+    gate_up(1, line(1, halves[1].q))
+    second_pass(0, 1)
+    second_pass(1, 1)
+    gate_up(0, beside(0, (0, 1)))
+    second_pass(0, 2)
+    second_pass(1, 2)
+    gate_up(1, beside(1, (0, 1)))
+    second_pass(0, 3)
+    second_pass(1, 3)
+    gate_up(0, beside(0, (2, 3)))
+    gate_up(1, beside(1, (2, 3)))
+
+    def activate(units):
+        for at in units:
+            gate = acc[at + (every, pl.ds(0, 768))]
+            up = acc[at + (every, pl.ds(768, 768))]
+            hid[at] = (gate * jax.nn.sigmoid(gate) * up).astype(BF16)
+
+    def down(i, units):
+        count = len(units)
+        for n, at in enumerate(units):
+            lhs_down[n] = hid[at]
         for j in range(8):
-            part = dot(lhs[:, pl.ds(0, 768)], wd[:, pl.ds(i * 2048 + j * 256, 256)])
-            os[i][at + (every, pl.ds(j * 256, 256))] = part.reshape(4, 40, 256).astype(BF16)
-
-    def send(src, dst, i, k, device):
-        c = remote(src, dst, s_send.at[i, k], s_recv.at[i, k], device)
-        c.start()
-        sent.append(c)
-        return c
+            cols = pl.ds(j * 256, 256)
+            rows = lhs_down[pl.ds(0, count)].reshape(count * 40, 768)
+            part = dot(rows, wd[:, pl.ds(i * 2048 + j * 256, 256)]).astype(BF16)
+            for n, at in enumerate(units):
+                os[i][at + (every, cols)] = part[n * 40 : (n + 1) * 40]
+
+    def send(src, dst, i, ss, rs, device):
+        remote(src, dst, s_send.at[i, ss], s_recv.at[i, rs], device).start()
 
     def add_into(ref, at, other, other_at):
         ref[at] = (ref[at].astype(F32) + other[other_at].astype(F32)).astype(BF16)
 
     order = [[wrap(h.p + d, 4) for d in (2, 1, -1, 0)] for h in halves]
-    fars, nears, adds, lasts = [[], []], [[], []], [[], []], [[], []]
+
+    def send_near(i, ks):
+        h = halves[i]
+        sides = ((wrap(h.q + 1, 4), 1, hi, 0), (wrap(h.q - 1, 4), -1, lo, 1))
+        down(i, [h.unit(order[i][k], v) for v, _, _, _ in sides for k in ks])
+        for v, d, cols, b in sides:
+            for k in ks:
+                u = order[i][k]
+                src, dst = os[i].at[h.unit(u, v) + (every, cols)], near.at[i, b, u, :, cols]
+                send(src, dst, i, 0, 4, h.two(d))
+
+    xx, yy = [wrap(mx + d, 4) for d in (0, 1, -1)], [wrap(my + d, 4) for d in (0, 1, -1)]
+    activate([(u, v) for u in xx for v in yy])
+    loads[2].wait()
+    for i in range(2):
+        send_near(i, (1, 2, 3))
+    for i, h in enumerate(halves):
+        settle(xs[i].at[0], u_recv.at[i, 7])
+        gate_up(i, line(i, wrap(h.q + 2, 4)))
+    fx, fy = wrap(mx + 2, 4), wrap(my + 2, 4)
+    activate([(fx, v) for v in yy] + [(u, fy) for u in xx] + [(fx, fy)])
     for i, h in enumerate(halves):
         v = wrap(h.q + 2, 4)
-        down(i, v)
+        down(i, [h.unit(u, v) for u in order[i]])
         for k, u in enumerate(order[i]):
             at = h.unit(u, v)
-            fars[i].append(
-                [
-                    send(os[i].at[at + (every, lo)], far.at[i, 0, u], i, k, h.two(1)),
-                    send(os[i].at[at + (every, hi)], far.at[i, 1, u], i, 4 + k, h.two(-1)),
-                ]
-            )
-    for i, h in enumerate(halves):
-        for v, d, cols, b in ((wrap(h.q + 1, 4), 1, hi, 0), (wrap(h.q - 1, 4), -1, lo, 1)):
-            down(i, v)
-            src = os[i].at[h.group(v) + (every, cols)]
-            nears[i].append(send(src, near.at[i, b, :, :, cols], i, 8 + b, h.two(d)))
-    down(0, halves[0].q)
-    for k in range(4):
-        for i, h in enumerate(halves):
-            u, moves = order[i][k], []
-            for b, d, cols in ((0, 1, lo), (1, -1, hi)):
-                fars[i][k][b].wait_recv()
-                at = h.unit(u, wrap(h.q + d, 4)) + (every, cols)
-                add_into(os[i], at, far, (i, b, u))
-                dst = near.at[i, b, u, :, cols]
-                moves.append(send(os[i].at[at], dst, i, 10 + 4 * b + k, h.two(d)))
-            adds[i].append(moves)
-    down(1, halves[1].q)
+            send(os[i].at[at + (every, lo)], far.at[i, 0, u], i, 0, k, h.two(1))
+            send(os[i].at[at + (every, hi)], far.at[i, 1, u], i, 0, k, h.two(-1))
     for i in range(2):
-        for c in nears[i]:
-            c.wait_recv()
+        send_near(i, (0,))
+    down(0, line(0, halves[0].q))
     for k in range(4):
         for i, h in enumerate(halves):
             u = order[i][k]
-            for c in adds[i][k]:
-                c.wait_recv()
+            settle(xs[i].at[0, 0], s_recv.at[i, k])
+            for b, d, cols in ((0, 1, lo), (1, -1, hi)):
+                at = h.unit(u, wrap(h.q + d, 4)) + (every, cols)
+                add_into(os[i], at, far, (i, b, u))
+                send(os[i].at[at], near.at[i, b, u, :, cols], i, 0, 5 + k, h.two(d))
+    down(1, line(1, halves[1].q))
+    for i in range(2):
+        settle(xs[i].at[0], s_recv.at[i, 4])
+    for k in range(4):
+        for i, h in enumerate(halves):
+            u = order[i][k]
+            settle(xs[i].at[0, 0], s_recv.at[i, 5 + k])
             mine = os[i][h.unit(u, h.q)].astype(F32)
             mine = mine + near[i, 0, u].astype(F32) + near[i, 1, u].astype(F32)
             tot[i, u] = mine.astype(BF16)
             if k == 0:
-                lasts[i].append(send(tot.at[i, u, :, lo], far2.at[i, 0], i, 18, h.one(1)))
-                lasts[i].append(send(tot.at[i, u, :, hi], far2.at[i, 1], i, 19, h.one(-1)))
+                send(tot.at[i, u, :, lo], far2.at[i, 0], i, 1, 9, h.one(1))
+                send(tot.at[i, u, :, hi], far2.at[i, 1], i, 1, 9, h.one(-1))
             if k == 1:
-                lasts[i].append(send(tot.at[i, u, :, hi], near2.at[i, 0, :, hi], i, 20, h.one(1)))
+                send(tot.at[i, u, :, hi], near2.at[i, 0, :, hi], i, 1, 10, h.one(1))
             if k == 2:
-                lasts[i].append(send(tot.at[i, u, :, lo], near2.at[i, 1, :, lo], i, 21, h.one(-1)))
+                send(tot.at[i, u, :, lo], near2.at[i, 1, :, lo], i, 1, 10, h.one(-1))
     for i, h in enumerate(halves):
+        settle(xs[i].at[0, 0], s_recv.at[i, 9])
         for b, d, cols in ((0, 1, lo), (1, -1, hi)):
             u = order[i][1 + b]
-            lasts[i][b].wait_recv()
             add_into(tot, (i, u, every, cols), far2, (i, b))
-            dst = near2.at[i, b, :, cols]
-            lasts[i].append(send(tot.at[i, u, :, cols], dst, i, 22 + b, h.one(d)))
+            send(tot.at[i, u, :, cols], near2.at[i, b, :, cols], i, 1, 10, h.one(d))
 
     across = (((0,), (0,)), ((), ()))
-    returns = []
     for i, h in enumerate(halves):
-        for c in lasts[i][2:]:
-            c.wait_recv()
+        settle(xs[i].at[0, pl.ds(0, 2)], s_recv.at[i, 10])
         final = tot[i, h.p].astype(F32) + near2[i, 0].astype(F32) + near2[i, 1].astype(F32)
         final = final.astype(BF16)
         back = jnp.zeros((128, 768), F32)
         for k, w in enumerate(windows):
             block = final[:, w : w + 768]
             back = back + lax.dot_general(pick[k], block, across, preferred_element_type=F32)
-        for c in dispatch[i]:
-            c.wait_send()
+        settle(rcv.at[i, pl.ds(0, 7)], d_send.at[i])
         go[i] = back.astype(BF16).reshape(8, 16, 768)
-        returns.append(all_to_all(i, rback, r_send, r_recv))
+        all_to_all(i, rback, r_send, r_recv)
     eye = lax.broadcasted_iota(jnp.int32, (16, 16), 0) == lax.broadcasted_iota(
         jnp.int32, (16, 16), 1
     )
     gate = jnp.sum(jnp.where(eye, jnp.broadcast_to(gate_row, (16, 16)), 0.0), axis=1, keepdims=True)
+    stores = []
     for i in range(2):
-        for c in returns[i]:
-            c.wait_recv()
+        settle(rback.at[i, pl.ds(0, 7)], r_recv.at[i])
         flat = rback[i].reshape(128, 768)
         for j, w in enumerate(windows):
             cols = pl.ds(i * 2048 + w, 768)
@@ -706,11 +702,20 @@
                 for k in range(2)
             ]
             mix = gate * pair[0] + (1.0 - gate) * pair[1]
-            out[:, cols] = (stream[:, cols] + mix).astype(BF16)
-    early = dispatch[0] + dispatch[1]
-    for c in sent:
-        if not any(c is other for other in early):
-            c.wait_send()
+            result[:, cols] = (stream[:, cols] + mix).astype(BF16)
+        cols = pl.ds(i * 2048, 2048)
+        stores.append(pltpu.make_async_copy(result.at[:, cols], out.at[:, cols], e_sem.at[i]))
+        stores[i].start()
+    drain()
+    for i in range(2):
+        settle(rback.at[i, pl.ds(0, 7)], r_send.at[i])
+        settle(xs[i].at[0, pl.ds(0, 3)], u_send.at[i, 0])
+        settle(xs[i].at[pl.ds(0, 2)], u_send.at[i, 1])
+        settle(xs[i].at[0], u_send.at[i, 2])
+        settle(xs[i].at[pl.ds(0, 3)], s_send.at[i, 0])
+        settle(xs[i].at[0, pl.ds(0, 3)], s_send.at[i, 1])
+    for c in stores:
+        c.wait()
 
 
 def token_places(ids, spread, fetch):
@@ -746,14 +751,14 @@
     ]
     for load in loads:
         load.start()
-    greet(
+    arrive = greet(
         [{"ctx": lax.rem(ctx + 15, 16)}, {"ctx": lax.rem(ctx + 1, 16)}]
         + [h.one(d) for h in halves for d in (1, 2, -1)]
         + [{"exp": lax.rem(exp + d, 8)} for d in range(1, 8)]
     )
     token_places(r["expert_ids"][...], r["spread"], r["fetch"])
-    first, sent = mixer(r, ctx, exp, mx, my)
-    experts(r, first, sent, r["out"], exp, mx, my, halves, loads)
+    gate_row, drain = mixer(r, ctx, exp, mx, my, arrive)
+    experts(r, gate_row, drain, r["out"], exp, mx, my, halves, loads)
 
 
 def shards(
@@ -786,7 +791,7 @@
         block_kernel,
         out_shape=jax.ShapeDtypeStruct((16, 4096), BF16),
         in_specs=[anywhere if name.startswith("w_") else vmem for name in INPUTS],
-        out_specs=vmem,
+        out_specs=anywhere,
         scratch_shapes=list(SCRATCH.values()),
         compiler_params=pltpu.CompilerParams(
             collective_id=0, has_side_effects=True, vmem_limit_bytes=VMEM_LIMIT

time: 142 us -> 135 us (0.951)
  Pallas kernels: 141 us -> 133 us
    pallas_call x1, Pallas kernels: 141 us -> 133 us  [shards(): pl.pallas_call(block_kernel, out_shape=jax.ShapeDtypeStruct((16, 4096), B...]
where the time goes in v5:
time: 135 us
  Pallas kernels  133 us (99%)
  local copies, waits for them, and re-layouts  1.57 us (1%)
    pallas_call x1, Pallas kernels, shards(): pl.pallas_call(block_kernel, out_shape=jax.ShapeDtypeStruct((16, 4096), B...  133 us

profile of v5, /device:TPU:1, one launch (start us, length us, event | category | flops | bytes accessed | tf_op | source)
XLA Modules:
  0.0 134.9 jit_solution(4369557236497649262)
XLA Ops:
  0.0 133.4 %shard_map.172 = bf16[16,4096]{1,0:T(8,128)(2,1)} custom-call(bf16[128,1024]{1,0:T(8,128)(2,1)} %refs_0_.1, bf16[128,1024]{1,0:T(8,128)(2,1)} %refs_1_.1, f32[4,1024]{1,0:T(4,128)} %refs_2_.1, f32[1,1024]{1,0:T(1,128)} %bitcast.10, bf16[544,1024]{1,0:T(8,128)(2,1)} %bitcast.7, bf16[512,1024]{1,0:T(8,128)(2,1)} %refs_5_.1, f32[1,1024]{1,0:T(1,128)} %bitcast.11, ...), custom_call_target="tpu_custom_call" | custom-call | flops 13500000256 | bytes 24000000 | tf_op jit(solution)/shard_map/pallas_call | solution.py:790
  133.4 1.6 %copy.20 = bf16[16,4096]{1,0:T(8,128)(2,1)} copy(bf16[16,4096]{1,0:T(8,128)(2,1)} %shard_map.172) | data formatting | bytes 262144

commit v6 on v5

--- a/solution.py
+++ b/solution.py
@@ -1,3 +1,5 @@
+import types
+
 import jax
 import jax.numpy as jnp
 import numpy as np
@@ -89,136 +91,144 @@
     "pick",
 )
 
-SCRATCH = {
-    "stream": pltpu.VMEM((16, 4096), F32),
-    "result": pltpu.VMEM((16, 4096), BF16),
-    "e_sem": pltpu.SemaphoreType.DMA((2,)),
-    "normed": pltpu.VMEM((16, 4096), BF16),
-    "spread": pltpu.VMEM((3, 128, 16), BF16),
-    "fetch": pltpu.VMEM((3, 2, 128, 16), BF16),
-    "rim": pltpu.VMEM((16, 1024), BF16),
-    "padded": pltpu.VMEM((136, 1024), F32),
-    "conv_out": pltpu.VMEM((128, 1024), BF16),
-    "part": pltpu.VMEM((8, 16, 544), BF16),
-    "parts": pltpu.VMEM((8, 16, 544), BF16),
-    "low_rank": pltpu.VMEM((8, 16, 512), BF16),
-    "maps": pltpu.VMEM((8, 16, 128), F32),
-    "bc_s": pltpu.SMEM((8, 16, 128), F32),
-    "step_t": pltpu.VMEM((1024, 128), F32),
-    "drive_t": pltpu.VMEM((1024, 128), F32),
-    "cum_t": pltpu.VMEM((1024, 128), F32),
-    "y_t": pltpu.VMEM((1024, 128), F32),
-    "rate_t": pltpu.VMEM((128, 128), F32),
-    "enter_t": pltpu.VMEM((128, 128), F32),
-    "fin_own": pltpu.VMEM((2, 128, 128), BF16),
-    "fin_y": pltpu.VMEM((4, 128, 128), BF16),
-    "sum_y": pltpu.VMEM((4, 8, 128), F32),
-    "fin_x": pltpu.VMEM((4, 128, 128), BF16),
-    "sum_x": pltpu.VMEM((4, 8, 128), F32),
-    "opg": pltpu.VMEM((4, 1024, 256), BF16),
-    "ga": pltpu.VMEM((4, 128, 1024), BF16),
-    "zs": pltpu.VMEM((4, 8, 16, 1024), BF16),
-    "rz": pltpu.VMEM((4, 8, 16, 1024), BF16),
-    "ms": pltpu.VMEM((3, 16, 1024), BF16),
-    "mo": pltpu.VMEM((4, 16, 1024), BF16),
-    "h_sem": pltpu.SemaphoreType.DMA((2,)),
-    "a_sem": pltpu.SemaphoreType.DMA((2,)),
-    "b_sem": pltpu.SemaphoreType.DMA((4,)),
-    "o_send": pltpu.SemaphoreType.DMA((1,)),
-    "o_recv": pltpu.SemaphoreType.DMA((3,)),
-    "c_send": pltpu.SemaphoreType.DMA((2, 2)),
-    "c_recv": pltpu.SemaphoreType.DMA((2, 2)),
-    "g_send": pltpu.SemaphoreType.DMA((1,)),
-    "g_recv": pltpu.SemaphoreType.DMA((5,)),
-    "z_send": pltpu.SemaphoreType.DMA((1,)),
-    "z_recv": pltpu.SemaphoreType.DMA((4,)),
-    "m_sem": pltpu.SemaphoreType.DMA((2,)),
-    "l_sem": pltpu.SemaphoreType.DMA((1,)),
-    "go": pltpu.VMEM((2, 8, 16, 768), BF16),
-    "rcv": pltpu.VMEM((2, 8, 16, 768), BF16),
-    "rback": pltpu.VMEM((2, 8, 16, 768), BF16),
-    "xa": pltpu.VMEM((4, 4, 40, 2048), BF16),
-    "xb": pltpu.VMEM((4, 4, 40, 2048), BF16),
-    "wgu": pltpu.VMEM((4096, 1536), BF16),
-    "wd": pltpu.VMEM((768, 4096), BF16),
-    "lhs": pltpu.VMEM((4, 40, 2048), BF16),
-    "lhs_down": pltpu.VMEM((6, 40, 768), BF16),
-    "acc": pltpu.VMEM((4, 4, 40, 1536), F32),
-    "hid": pltpu.VMEM((4, 4, 40, 768), BF16),
-    "oa": pltpu.VMEM((4, 4, 40, 2048), BF16),
-    "ob": pltpu.VMEM((4, 4, 40, 2048), BF16),
-    "far": pltpu.VMEM((2, 2, 4, 40, 1024), BF16),
-    "near": pltpu.VMEM((2, 2, 4, 40, 2048), BF16),
-    "tot": pltpu.VMEM((2, 4, 40, 2048), BF16),
-    "far2": pltpu.VMEM((2, 2, 40, 1024), BF16),
-    "near2": pltpu.VMEM((2, 2, 40, 2048), BF16),
-    "w_sem": pltpu.SemaphoreType.DMA((3,)),
-    "d_send": pltpu.SemaphoreType.DMA((2,)),
-    "d_recv": pltpu.SemaphoreType.DMA((2,)),
-    "u_send": pltpu.SemaphoreType.DMA((2, 3)),
-    "u_recv": pltpu.SemaphoreType.DMA((2, 8)),
-    "s_send": pltpu.SemaphoreType.DMA((2, 2)),
-    "s_recv": pltpu.SemaphoreType.DMA((2, 11)),
-    "r_send": pltpu.SemaphoreType.DMA((2,)),
-    "r_recv": pltpu.SemaphoreType.DMA((2,)),
-}
-
-
-def mixer(r, ctx, exp, mx, my, arrive):
-    mixer_in = r["mixer_in"]
-    gate_in = r["gate_in"]
-    conv_weight = r["conv_weight"]
-    conv_bias = r["conv_bias"]
-    x_proj = r["x_proj"]
-    dt_proj = r["dt_proj"]
-    dt_bias = r["dt_bias"]
-    decay_rate = r["decay_rate"]
-    skip = r["skip"]
-    out_proj = r["out_proj"]
-    residual = r["residual"]
-    gain = r["gain"]
-    router = r["router"]
-    expert_ids = r["expert_ids"]
-    stream = r["stream"]
-    normed = r["normed"]
-    rim = r["rim"]
-    padded = r["padded"]
-    conv_out = r["conv_out"]
-    part = r["part"]
-    parts = r["parts"]
-    low_rank = r["low_rank"]
-    maps = r["maps"]
-    bc_s = r["bc_s"]
-    step_t = r["step_t"]
-    drive_t = r["drive_t"]
-    cum_t = r["cum_t"]
-    y_t = r["y_t"]
-    rate_t = r["rate_t"]
-    enter_t = r["enter_t"]
-    fin_own = r["fin_own"]
-    fin_y = r["fin_y"]
-    sum_y = r["sum_y"]
-    fin_x = r["fin_x"]
-    sum_x = r["sum_x"]
-    opg = r["opg"]
-    ga = r["ga"]
-    zs = r["zs"]
-    rz = r["rz"]
-    ms = r["ms"]
-    mo = r["mo"]
-    h_sem = r["h_sem"]
-    a_sem = r["a_sem"]
-    b_sem = r["b_sem"]
-    o_send = r["o_send"]
-    o_recv = r["o_recv"]
-    c_send = r["c_send"]
-    c_recv = r["c_recv"]
-    g_send = r["g_send"]
-    g_recv = r["g_recv"]
-    z_send = r["z_send"]
-    z_recv = r["z_recv"]
-    m_sem = r["m_sem"]
-    l_sem = r["l_sem"]
+SCRATCH = dict(
+    stream=pltpu.VMEM((16, 4096), F32),
+    result=pltpu.VMEM((16, 4096), BF16),
+    e_sem=pltpu.SemaphoreType.DMA((2,)),
+    normed=pltpu.VMEM((16, 4096), BF16),
+    spread=pltpu.VMEM((3, 128, 16), BF16),
+    fetch=pltpu.VMEM((3, 2, 128, 16), BF16),
+    rim=pltpu.VMEM((16, 1024), BF16),
+    padded=pltpu.VMEM((136, 1024), F32),
+    conv_out=pltpu.VMEM((128, 1024), BF16),
+    part=pltpu.VMEM((8, 16, 544), BF16),
+    parts=pltpu.VMEM((8, 16, 544), BF16),
+    low_rank=pltpu.VMEM((8, 16, 512), BF16),
+    maps=pltpu.VMEM((8, 16, 128), F32),
+    bc_s=pltpu.SMEM((8, 16, 128), F32),
+    step_t=pltpu.VMEM((1024, 128), F32),
+    drive_t=pltpu.VMEM((1024, 128), F32),
+    cum_t=pltpu.VMEM((1024, 128), F32),
+    y_t=pltpu.VMEM((1024, 128), F32),
+    rate_t=pltpu.VMEM((128, 128), F32),
+    enter_t=pltpu.VMEM((128, 128), F32),
+    fin_own=pltpu.VMEM((2, 128, 128), BF16),
+    fin_y=pltpu.VMEM((4, 128, 128), BF16),
+    sum_y=pltpu.VMEM((4, 8, 128), F32),
+    fin_x=pltpu.VMEM((4, 128, 128), BF16),
+    sum_x=pltpu.VMEM((4, 8, 128), F32),
+    opg=pltpu.VMEM((2, 4, 1024, 256), BF16),
+    ga=pltpu.VMEM((2, 4, 64, 1024), BF16),
+    zs=pltpu.VMEM((4, 4, 2, 16, 1024), BF16),
+    pair=pltpu.VMEM((4, 4, 16, 1024), BF16),
+    both=pltpu.VMEM((4, 4, 16, 1024), BF16),
+    p_send=pltpu.SemaphoreType.DMA((1,)),
+    p_recv=pltpu.SemaphoreType.DMA((4,)),
+    rz=pltpu.VMEM((4, 4, 16, 1024), BF16),
+    ms=pltpu.VMEM((3, 16, 1024), BF16),
+    mo=pltpu.VMEM((4, 16, 1024), BF16),
+    h_sem=pltpu.SemaphoreType.DMA((2,)),
+    a_sem=pltpu.SemaphoreType.DMA((2,)),
+    b_sem=pltpu.SemaphoreType.DMA((4,)),
+    o_send=pltpu.SemaphoreType.DMA((2,)),
+    o_recv=pltpu.SemaphoreType.DMA((2, 3)),
+    c_send=pltpu.SemaphoreType.DMA((2, 2)),
+    c_recv=pltpu.SemaphoreType.DMA((2, 2)),
+    g_send=pltpu.SemaphoreType.DMA((2,)),
+    g_recv=pltpu.SemaphoreType.DMA((2, 3)),
+    z_send=pltpu.SemaphoreType.DMA((1,)),
+    z_recv=pltpu.SemaphoreType.DMA((4,)),
+    m_sem=pltpu.SemaphoreType.DMA((2,)),
+    l_sem=pltpu.SemaphoreType.DMA((1,)),
+    go=pltpu.VMEM((2, 8, 16, 768), BF16),
+    rcv=pltpu.VMEM((2, 8, 16, 768), BF16),
+    rback=pltpu.VMEM((2, 8, 16, 768), BF16),
+    xa=pltpu.VMEM((4, 4, 40, 2048), BF16),
+    xb=pltpu.VMEM((4, 4, 40, 2048), BF16),
+    wgu=pltpu.VMEM((4096, 1536), BF16),
+    wd=pltpu.VMEM((768, 4096), BF16),
+    lhs=pltpu.VMEM((4, 40, 2048), BF16),
+    lhs_down=pltpu.VMEM((6, 40, 768), BF16),
+    acc=pltpu.VMEM((4, 4, 40, 1536), F32),
+    hid=pltpu.VMEM((4, 4, 40, 768), BF16),
+    oa=pltpu.VMEM((4, 4, 40, 2048), BF16),
+    ob=pltpu.VMEM((4, 4, 40, 2048), BF16),
+    far=pltpu.VMEM((2, 2, 4, 40, 1024), BF16),
+    near=pltpu.VMEM((2, 2, 4, 40, 2048), BF16),
+    tot=pltpu.VMEM((2, 4, 40, 2048), BF16),
+    far2=pltpu.VMEM((2, 2, 40, 1024), BF16),
+    near2=pltpu.VMEM((2, 2, 40, 2048), BF16),
+    w_sem=pltpu.SemaphoreType.DMA((3,)),
+    d_send=pltpu.SemaphoreType.DMA((2,)),
+    d_recv=pltpu.SemaphoreType.DMA((2,)),
+    u_send=pltpu.SemaphoreType.DMA((2, 3)),
+    u_recv=pltpu.SemaphoreType.DMA((2, 8)),
+    s_send=pltpu.SemaphoreType.DMA((2, 2)),
+    s_recv=pltpu.SemaphoreType.DMA((2, 11)),
+    r_send=pltpu.SemaphoreType.DMA((2,)),
+    r_recv=pltpu.SemaphoreType.DMA((2,)),
+)
+
+
+def mixer(r, ctx, exp, mx, my, halves, arrive):
+    mixer_in = r.mixer_in
+    gate_in = r.gate_in
+    conv_weight = r.conv_weight
+    conv_bias = r.conv_bias
+    x_proj = r.x_proj
+    dt_proj = r.dt_proj
+    dt_bias = r.dt_bias
+    decay_rate = r.decay_rate
+    skip = r.skip
+    out_proj = r.out_proj
+    residual = r.residual
+    gain = r.gain
+    router = r.router
+    expert_ids = r.expert_ids
+    stream = r.stream
+    normed = r.normed
+    rim = r.rim
+    padded = r.padded
+    conv_out = r.conv_out
+    part = r.part
+    parts = r.parts
+    low_rank = r.low_rank
+    maps = r.maps
+    bc_s = r.bc_s
+    step_t = r.step_t
+    drive_t = r.drive_t
+    cum_t = r.cum_t
+    y_t = r.y_t
+    rate_t = r.rate_t
+    enter_t = r.enter_t
+    fin_own = r.fin_own
+    fin_y = r.fin_y
+    sum_y = r.sum_y
+    fin_x = r.fin_x
+    sum_x = r.sum_x
+    opg = r.opg
+    ga = r.ga
+    zs = r.zs
+    pair = r.pair
+    both = r.both
+    p_send = r.p_send
+    p_recv = r.p_recv
+    rz = r.rz
+    ms = r.ms
+    mo = r.mo
+    h_sem = r.h_sem
+    a_sem = r.a_sem
+    b_sem = r.b_sem
+    o_send = r.o_send
+    o_recv = r.o_recv
+    c_send = r.c_send
+    c_recv = r.c_recv
+    g_send = r.g_send
+    g_recv = r.g_recv
+    z_send = r.z_send
+    z_recv = r.z_recv
+    m_sem = r.m_sem
+    l_sem = r.l_sem
     every = slice(None)
 
     def along_x(d):
@@ -256,9 +266,10 @@
 
     arrive()
     send(mixer_in.at[pl.ds(112, 16)], rim, h_sem.at[0], h_sem.at[1], ahead)
-    send(out_proj, opg.at[my], o_send.at[0], o_recv.at[0], along_y(1))
-    send(out_proj, opg.at[my], o_send.at[0], o_recv.at[1], along_y(-1))
-    opg[pl.ds(my, 1)] = out_proj[...][None]
+    for i, h in enumerate(halves):
+        send(out_proj, opg.at[i, h.q], o_send.at[i], o_recv.at[i, 0], h.two(1))
+        send(out_proj, opg.at[i, h.q], o_send.at[i], o_recv.at[i, 1], h.two(-1))
+        opg[i, pl.ds(h.q, 1)] = out_proj[...][None]
     channel_sums(16, 112)
     settle(rim, h_sem.at[1])
     keep = jnp.where(ctx > 0, 1.0, 0.0).astype(F32)
@@ -282,11 +293,11 @@
     settle(low_rank.at[pl.ds(0, 7)], b_sem.at[2])
     settle(maps.at[pl.ds(0, 7)], b_sem.at[3])
     top, low = pl.ds(0, 512), pl.ds(512, 512)
-    left, right = wrap(my - 1, 4), wrap(my + 1, 4)
-    settle(opg.at[0], o_recv.at[0])
-    send(opg.at[left, top], opg.at[left, top], o_send.at[0], o_recv.at[2], along_y(1))
-    settle(opg.at[0], o_recv.at[1])
-    send(opg.at[right, low], opg.at[right, low], o_send.at[0], o_recv.at[2], along_y(-1))
+    for i, h in enumerate(halves):
+        for k, d, rows in ((0, 1, top), (1, -1, low)):
+            settle(opg.at[0, 0], o_recv.at[i, k])
+            place = opg.at[i, wrap(h.q - d, 4), rows]
+            send(place, place, o_send.at[i], o_recv.at[i, 2], h.two(d))
     scalars = pltpu.make_async_copy(maps, bc_s, l_sem.at[0])
     scalars.start()
     step_low = low_rank[...].reshape(128, 512)
@@ -375,57 +386,79 @@
             y = y_t[pl.ds(half * 512 + g, 64, stride=8), :]
             y = y + skip[:, cols] * conv_out[rows, cols].astype(F32)
             z = gate_in[rows, cols].astype(F32)
-            ga[pl.ds(mx, 1), rows, cols] = (y * (z * jax.nn.sigmoid(z))).astype(BF16)[None]
-        place = ga.at[mx, rows]
+            block = (y * (z * jax.nn.sigmoid(z))).astype(BF16)
+            ga[half, pl.ds(halves[half].p, 1), :, cols] = block[None]
+        place = ga.at[half, halves[half].p]
         for k, d in enumerate((1, -1)):
-            s = half * 2 + k
-            send(place, place, g_send.at[0], g_recv.at[s], along_x(d))
-
-    def project(u):
+            send(place, place, g_send.at[half], g_recv.at[half, k], halves[half].one(d))
+
+    hops = (0, -1, 1, 2)
+
+    def project(i, k):
+        rows = ga[i, wrap(halves[i].p + hops[k], 4)]
         for v in range(4):
-            cols = pl.ds(v * 256, 256)
-            out = dot(ga[u], opg[v])
-            zs[pl.ds(u, 1), :, :, cols] = out.astype(BF16).reshape(1, 8, 16, 256)
-        rz[pl.ds(u, 1), pl.ds(exp, 1)] = zs[pl.ds(u, 1), pl.ds(exp, 1)]
-
-    def scatter_group(k, u):
-        for d in range(1, 8):
-            src = zs.at[u, lax.rem(exp + d, 8)]
-            send(src, rz.at[u, exp], z_send.at[0], z_recv.at[k], peer(d))
-
-    settle(opg.at[0], o_recv.at[2])
-    left, right, far = wrap(mx - 1, 4), wrap(mx + 1, 4), wrap(mx + 2, 4)
-    top, low = pl.ds(0, 64), pl.ds(64, 64)
-    project(mx)
-    scatter_group(0, mx)
-    settle(ga.at[0, top], g_recv.at[0])
-    send(ga.at[left, top], ga.at[left, top], g_send.at[0], g_recv.at[4], along_x(1))
-    settle(ga.at[0, top], g_recv.at[1])
-    settle(ga.at[0, top], g_recv.at[3])
-    send(ga.at[right, low], ga.at[right, low], g_send.at[0], g_recv.at[4], along_x(-1))
-    settle(ga.at[0, top], g_recv.at[2])
-    for k, u in ((1, left), (2, right)):
-        project(u)
-        scatter_group(k, u)
-    settle(ga.at[0], g_recv.at[4])
-    project(far)
-    scatter_group(3, far)
-    for k, (u, d) in enumerate(((mx, 0), (left, -1), (right, 1), (far, 2))):
-        settle(rz.at[0, pl.ds(0, 7)], z_recv.at[k])
-        total = rz[u, 0].astype(F32)
-        for j in range(1, 8):
-            total = total + rz[u, j].astype(F32)
+            block = dot(rows, opg[i, v]).astype(BF16).reshape(2, 2, 16, 256)
+            zs[k, pl.ds(2 * i, 2), :, :, pl.ds(v * 256, 256)] = block
+
+    mz, core = exp // 2, exp % 2
+
+    def pair_group(k):
+        sibling = {"exp": 2 * mz + 1 - core}
+        send(zs.at[k, :, 1 - core], pair.at[k], p_send.at[0], p_recv.at[k], sibling)
+
+    def scatter_group(k):
+        settle(pair.at[0], p_recv.at[k])
+        own = zs[k, :, pl.ds(core, 1)].reshape(4, 16, 1024).astype(F32)
+        both[k] = (own + pair[k].astype(F32)).astype(BF16)
+        for d in (1, 3, 2):
+            z = wrap(mz + d, 4)
+            send(both.at[k, z], rz.at[k, mz], z_send.at[0], z_recv.at[k], {"exp": 2 * z + core})
+        rz[k, pl.ds(mz, 1)] = both[k, pl.ds(mz, 1)]
+
+    top, low = pl.ds(0, 32), pl.ds(32, 32)
+    for i in range(2):
+        settle(opg.at[0, 0], o_recv.at[i, 2])
+        project(i, 0)
+    pair_group(0)
+    for i, h in enumerate(halves):
+        for k, d, rows in ((0, 1, top), (1, -1, low)):
+            settle(ga.at[0, 0], g_recv.at[i, k])
+            place = ga.at[i, wrap(h.p - d, 4), rows]
+            send(place, place, g_send.at[i], g_recv.at[i, 2], h.one(d))
+    scatter_group(0)
+    for k in (1, 2):
+        project(0, k)
+        project(1, k)
+        pair_group(k)
+    scatter_group(1)
+    scatter_group(2)
+    for i in range(2):
+        settle(ga.at[0, 0], g_recv.at[i, 2])
+        project(i, 3)
+    pair_group(3)
+    scatter_group(3)
+    second = exp // 4
+    place = mx + second * (my - mx)
+    for k, d in enumerate(hops):
+        settle(rz.at[0, pl.ds(0, 3)], z_recv.at[k])
+        total = rz[k, 0].astype(F32)
+        for j in range(1, 4):
+            total = total + rz[k, j].astype(F32)
         if d == 0:
-            mo[pl.ds(mx, 1)] = total.astype(BF16)[None]
+            mo[pl.ds(place, 1)] = total.astype(BF16)[None]
         else:
             ms[k - 1] = total.astype(BF16)
-            send(ms.at[k - 1], mo.at[mx], m_sem.at[0], m_sem.at[1], along_x(d))
+            near_x, near_y = along_x(d)["ctx"], along_y(d)["ctx"]
+            device = {"ctx": near_x + second * (near_y - near_x)}
+            send(ms.at[k - 1], mo.at[place], m_sem.at[0], m_sem.at[1], device)
     settle(mo.at[pl.ds(0, 3)], m_sem.at[1])
 
     squares = jnp.zeros((16, 1), F32)
     for u in range(4):
         cols = pl.ds(u * 1024, 1024)
-        rows = residual[:, cols].astype(F32) + mo[u].astype(F32)
+        across = [mo[v, :, pl.ds(u * 256, 256)] for v in range(4)]
+        mixed = jnp.where(second == 0, mo[u].astype(F32), jnp.concatenate(across, 1).astype(F32))
+        rows = residual[:, cols].astype(F32) + mixed
         stream[:, cols] = rows
         squares = squares + jnp.sum(rows * rows, axis=1, keepdims=True)
     scale = lax.rsqrt(squares * (1.0 / 4096.0) + 1e-06)
@@ -442,54 +475,56 @@
 
     def drain():
         settle(rim, h_sem.at[0])
-        settle(opg.at[pl.ds(0, 3)], o_send.at[0])
+        for i in range(2):
+            settle(opg.at[0, pl.ds(0, 3)], o_send.at[i])
+            settle(ga.at[0, pl.ds(0, 3)], g_send.at[i])
         settle(parts.at[pl.ds(0, 7)], a_sem.at[0])
         settle(low_rank.at[pl.ds(0, 7)], b_sem.at[0])
         settle(maps.at[pl.ds(0, 7)], b_sem.at[1])
         for base, (fin, sums) in enumerate(((fin_y, sum_y), (fin_x, sum_x))):
             settle(fin.at[pl.ds(0, 3)], c_send.at[0, base])
             settle(sums.at[pl.ds(0, 3)], c_send.at[1, base])
-        settle(ga.at[pl.ds(0, 3)], g_send.at[0])
-        settle(rz.at[:, pl.ds(0, 7)], z_send.at[0])
+        settle(pair, p_send.at[0])
+        settle(rz.at[:, pl.ds(0, 3)], z_send.at[0])
         settle(mo.at[pl.ds(0, 3)], m_sem.at[0])
 
     return first, drain
 
 
 def experts(r, gate_row, drain, out, exp, mx, my, halves, loads):
-    pick = r["pick"]
-    result = r["result"]
-    e_sem = r["e_sem"]
-    stream = r["stream"]
-    normed = r["normed"]
-    spread = r["spread"]
-    fetch = r["fetch"]
-    go = r["go"]
-    rcv = r["rcv"]
-    rback = r["rback"]
-    xa = r["xa"]
-    xb = r["xb"]
-    wgu = r["wgu"]
-    wd = r["wd"]
-    lhs = r["lhs"]
-    lhs_down = r["lhs_down"]
-    acc = r["acc"]
-    hid = r["hid"]
-    oa = r["oa"]
-    ob = r["ob"]
-    far = r["far"]
-    near = r["near"]
-    tot = r["tot"]
-    far2 = r["far2"]
-    near2 = r["near2"]
-    d_send = r["d_send"]
-    d_recv = r["d_recv"]
-    u_send = r["u_send"]
-    u_recv = r["u_recv"]
-    s_send = r["s_send"]
-    s_recv = r["s_recv"]
-    r_send = r["r_send"]
-    r_recv = r["r_recv"]
+    pick = r.pick
+    result = r.result
+    e_sem = r.e_sem
+    stream = r.stream
+    normed = r.normed
+    spread = r.spread
+    fetch = r.fetch
+    go = r.go
+    rcv = r.rcv
+    rback = r.rback
+    xa = r.xa
+    xb = r.xb
+    wgu = r.wgu
+    wd = r.wd
+    lhs = r.lhs
+    lhs_down = r.lhs_down
+    acc = r.acc
+    hid = r.hid
+    oa = r.oa
+    ob = r.ob
+    far = r.far
+    near = r.near
+    tot = r.tot
+    far2 = r.far2
+    near2 = r.near2
+    d_send = r.d_send
+    d_recv = r.d_recv
+    u_send = r.u_send
+    u_recv = r.u_recv
+    s_send = r.s_send
+    s_recv = r.s_recv
+    r_send = r.r_send
+    r_recv = r.r_recv
     xs, os = (xa, xb), (oa, ob)
     lo, hi = pl.ds(0, 1024), pl.ds(1024, 1024)
     every = slice(None)
@@ -739,15 +774,15 @@
 
 def block_kernel(*refs):
     names = INPUTS + ("out",) + tuple(SCRATCH)
-    r = dict(zip(names, refs, strict=True))
+    r = types.SimpleNamespace(**dict(zip(names, refs, strict=True)))
     ctx, exp = lax.axis_index("ctx"), lax.axis_index("exp")
     mx, my = ctx // 4, ctx % 4
     halves = (Half(0, mx, my), Half(1, mx, my))
-    wgu, wd, w_sem = r["wgu"], r["wd"], r["w_sem"]
+    wgu, wd, w_sem = r.wgu, r.wd, r.w_sem
     loads = [
-        pltpu.make_async_copy(r["w_gate"].at[0], wgu.at[:, pl.ds(0, 768)], w_sem.at[0]),
-        pltpu.make_async_copy(r["w_up"].at[0], wgu.at[:, pl.ds(768, 768)], w_sem.at[1]),
-        pltpu.make_async_copy(r["w_down"].at[0], wd, w_sem.at[2]),
+        pltpu.make_async_copy(r.w_gate.at[0], wgu.at[:, pl.ds(0, 768)], w_sem.at[0]),
+        pltpu.make_async_copy(r.w_up.at[0], wgu.at[:, pl.ds(768, 768)], w_sem.at[1]),
+        pltpu.make_async_copy(r.w_down.at[0], wd, w_sem.at[2]),
     ]
     for load in loads:
         load.start()
@@ -756,9 +791,9 @@
         + [h.one(d) for h in halves for d in (1, 2, -1)]
         + [{"exp": lax.rem(exp + d, 8)} for d in range(1, 8)]
     )
-    token_places(r["expert_ids"][...], r["spread"], r["fetch"])
-    gate_row, drain = mixer(r, ctx, exp, mx, my, arrive)
-    experts(r, gate_row, drain, r["out"], exp, mx, my, halves, loads)
+    token_places(r.expert_ids[...], r.spread, r.fetch)
+    gate_row, drain = mixer(r, ctx, exp, mx, my, halves, arrive)
+    experts(r, gate_row, drain, r.out, exp, mx, my, halves, loads)
 
 
 def shards(

time: 135 us -> 133 us (0.985)
  Pallas kernels: 133 us -> 131 us
    pallas_call x1, Pallas kernels: 133 us -> 131 us  [shards(): pl.pallas_call(block_kernel, out_shape=jax.ShapeDtypeStruct((16, 4096), B...]
where the time goes in v6:
time: 133 us
  Pallas kernels  131 us (98%)
  local copies, waits for them, and re-layouts  1.57 us (1%)
    pallas_call x1, Pallas kernels, shards(): pl.pallas_call(block_kernel, out_shape=jax.ShapeDtypeStruct((16, 4096), B...  131 us

profile of v6, /device:TPU:1, one launch (start us, length us, event | category | flops | bytes accessed | tf_op | source)
XLA Modules:
  0.0 133.0 jit_solution(3626339077948837975)
XLA Ops:
  0.0 131.4 %shard_map.172 = bf16[16,4096]{1,0:T(8,128)(2,1)} custom-call(bf16[128,1024]{1,0:T(8,128)(2,1)} %refs_0_.1, bf16[128,1024]{1,0:T(8,128)(2,1)} %refs_1_.1, f32[4,1024]{1,0:T(4,128)} %refs_2_.1, f32[1,1024]{1,0:T(1,128)} %bitcast.10, bf16[544,1024]{1,0:T(8,128)(2,1)} %bitcast.7, bf16[512,1024]{1,0:T(8,128)(2,1)} %refs_5_.1, f32[1,1024]{1,0:T(1,128)} %bitcast.11, ...), custom_call_target="tpu_custom_call" | custom-call | flops 13500000256 | bytes 24000000 | tf_op jit(solution)/shard_map/pallas_call | solution.py:825
  131.4 1.6 %copy.20 = bf16[16,4096]{1,0:T(8,128)(2,1)} copy(bf16[16,4096]{1,0:T(8,128)(2,1)} %shard_map.172) | data formatting | bytes 262144

commit v7 on v6

--- a/solution.py
+++ b/solution.py
@@ -101,8 +101,10 @@
     rim=pltpu.VMEM((16, 1024), BF16),
     padded=pltpu.VMEM((136, 1024), F32),
     conv_out=pltpu.VMEM((128, 1024), BF16),
-    part=pltpu.VMEM((8, 16, 544), BF16),
-    parts=pltpu.VMEM((8, 16, 544), BF16),
+    part=pltpu.VMEM((8, 16, 512), BF16),
+    own_maps=pltpu.VMEM((8, 16, 128), F32),
+    part_maps=pltpu.VMEM((8, 16, 128), F32),
+    parts=pltpu.VMEM((8, 16, 512), BF16),
     low_rank=pltpu.VMEM((8, 16, 512), BF16),
     maps=pltpu.VMEM((8, 16, 128), F32),
     bc_s=pltpu.SMEM((8, 16, 128), F32),
@@ -128,7 +130,7 @@
     ms=pltpu.VMEM((3, 16, 1024), BF16),
     mo=pltpu.VMEM((4, 16, 1024), BF16),
     h_sem=pltpu.SemaphoreType.DMA((2,)),
-    a_sem=pltpu.SemaphoreType.DMA((2,)),
+    a_sem=pltpu.SemaphoreType.DMA((4,)),
     b_sem=pltpu.SemaphoreType.DMA((4,)),
     o_send=pltpu.SemaphoreType.DMA((2,)),
     o_recv=pltpu.SemaphoreType.DMA((2, 3)),
@@ -191,6 +193,8 @@
     padded = r.padded
     conv_out = r.conv_out
     part = r.part
+    own_maps = r.own_maps
+    part_maps = r.part_maps
     parts = r.parts
     low_rank = r.low_rank
     maps = r.maps
@@ -245,6 +249,7 @@
     def send(src, dst, ss, rs, device):
         remote(src, dst, ss, rs, device).start()
 
+    own_maps[...] = jnp.zeros_like(own_maps)
     padded[pl.ds(8, 128), :] = mixer_in[...].astype(F32)
     for g in range(8):
         rate_t[pl.ds(g, 16, stride=8), :] = decay_rate[:, g * 128 : (g + 1) * 128] * (-LOG2E)
@@ -259,17 +264,15 @@
             conv_out[pl.ds(start, rows), cols] = (total * jax.nn.sigmoid(total)).astype(BF16)
 
     def channel_sums(start, rows):
-        sums = dot_t(conv_out[pl.ds(start, rows), :], x_proj[...]).astype(BF16)
-        part[pl.ds(start // 16, rows // 16)] = sums.reshape(rows // 16, 16, 544)
+        sums = dot_t(conv_out[pl.ds(start, rows), :], x_proj[...])
+        blocks = pl.ds(start // 16, rows // 16)
+        part[blocks] = sums[:, :512].astype(BF16).reshape(rows // 16, 16, 512)
+        own_maps[blocks, :, pl.ds(0, 32)] = sums[:, 512:].reshape(rows // 16, 16, 32)
 
     convolve(16, 112)
 
     arrive()
     send(mixer_in.at[pl.ds(112, 16)], rim, h_sem.at[0], h_sem.at[1], ahead)
-    for i, h in enumerate(halves):
-        send(out_proj, opg.at[i, h.q], o_send.at[i], o_recv.at[i, 0], h.two(1))
-        send(out_proj, opg.at[i, h.q], o_send.at[i], o_recv.at[i, 1], h.two(-1))
-        opg[i, pl.ds(h.q, 1)] = out_proj[...][None]
     channel_sums(16, 112)
     settle(rim, h_sem.at[1])
     keep = jnp.where(ctx > 0, 1.0, 0.0).astype(F32)
@@ -278,26 +281,28 @@
     channel_sums(0, 16)
 
     for d in range(1, 8):
-        src = part.at[lax.rem(exp + d, 8)]
-        send(src, parts.at[exp], a_sem.at[0], a_sem.at[1], peer(d))
+        to = lax.rem(exp + d, 8)
+        send(part.at[to], parts.at[exp], a_sem.at[0], a_sem.at[1], peer(d))
+        send(own_maps.at[to], part_maps.at[exp], a_sem.at[2], a_sem.at[3], peer(d))
     parts[pl.ds(exp, 1)] = part[pl.ds(exp, 1)]
+    part_maps[pl.ds(exp, 1)] = own_maps[pl.ds(exp, 1)]
+    for i, h in enumerate(halves):
+        send(out_proj, opg.at[i, h.q], o_send.at[i], o_recv.at[i, 0], h.two(1))
+        send(out_proj, opg.at[i, h.q], o_send.at[i], o_recv.at[i, 1], h.two(-1))
+        opg[i, pl.ds(h.q, 1)] = out_proj[...][None]
     settle(parts.at[pl.ds(0, 7)], a_sem.at[1])
-    total = parts[0].astype(F32)
+    settle(part_maps.at[pl.ds(0, 7)], a_sem.at[3])
+    total, total_maps = parts[0].astype(F32), part_maps[0]
     for j in range(1, 8):
         total = total + parts[j].astype(F32)
-    low_rank[pl.ds(exp, 1)] = total[:, :512].astype(BF16)[None]
-    maps[pl.ds(exp, 1), :, pl.ds(0, 32)] = total[:, 512:][None]
+        total_maps = total_maps + part_maps[j]
+    low_rank[pl.ds(exp, 1)] = total.astype(BF16)[None]
+    maps[pl.ds(exp, 1)] = total_maps[None]
     for d in range(1, 8):
         for k, ref in enumerate((low_rank, maps)):
             send(ref.at[exp], ref.at[exp], b_sem.at[k], b_sem.at[2 + k], peer(d))
     settle(low_rank.at[pl.ds(0, 7)], b_sem.at[2])
     settle(maps.at[pl.ds(0, 7)], b_sem.at[3])
-    top, low = pl.ds(0, 512), pl.ds(512, 512)
-    for i, h in enumerate(halves):
-        for k, d, rows in ((0, 1, top), (1, -1, low)):
-            settle(opg.at[0, 0], o_recv.at[i, k])
-            place = opg.at[i, wrap(h.q - d, 4), rows]
-            send(place, place, o_send.at[i], o_recv.at[i, 2], h.two(d))
     scalars = pltpu.make_async_copy(maps, bc_s, l_sem.at[0])
     scalars.start()
     step_low = low_rank[...].reshape(128, 512)
@@ -311,6 +316,12 @@
             step_t[rows, :] = step[:, i * 128 : (i + 1) * 128]
             drive_t[rows, :] = drive[:, i * 128 : (i + 1) * 128]
     scalars.wait()
+    top, low = pl.ds(0, 512), pl.ds(512, 512)
+    for i, h in enumerate(halves):
+        for k, d, rows in ((0, 1, top), (1, -1, low)):
+            settle(opg.at[0, 0], o_recv.at[i, k])
+            place = opg.at[i, wrap(h.q - d, 4), rows]
+            send(place, place, o_send.at[i], o_recv.at[i, 2], h.two(d))
 
     rates = [rate_t[pl.ds(n * 8, 8), :] for n in range(16)]
     zero = jnp.zeros((8, 128), F32)
@@ -415,6 +426,23 @@
             send(both.at[k, z], rz.at[k, mz], z_send.at[0], z_recv.at[k], {"exp": 2 * z + core})
         rz[k, pl.ds(mz, 1)] = both[k, pl.ds(mz, 1)]
 
+    second = exp // 4
+    place = mx + second * (my - mx)
+
+    def finish_group(k):
+        settle(rz.at[0, pl.ds(0, 3)], z_recv.at[k])
+        total = rz[k, 0].astype(F32)
+        for j in range(1, 4):
+            total = total + rz[k, j].astype(F32)
+        d = hops[k]
+        if d == 0:
+            mo[pl.ds(place, 1)] = total.astype(BF16)[None]
+        else:
+            ms[k - 1] = total.astype(BF16)
+            near_x, near_y = along_x(d)["ctx"], along_y(d)["ctx"]
+            device = {"ctx": near_x + second * (near_y - near_x)}
+            send(ms.at[k - 1], mo.at[place], m_sem.at[0], m_sem.at[1], device)
+
     top, low = pl.ds(0, 32), pl.ds(32, 32)
     for i in range(2):
         settle(opg.at[0, 0], o_recv.at[i, 2])
@@ -423,8 +451,8 @@
     for i, h in enumerate(halves):
         for k, d, rows in ((0, 1, top), (1, -1, low)):
             settle(ga.at[0, 0], g_recv.at[i, k])
-            place = ga.at[i, wrap(h.p - d, 4), rows]
-            send(place, place, g_send.at[i], g_recv.at[i, 2], h.one(d))
+            block = ga.at[i, wrap(h.p - d, 4), rows]
+            send(block, block, g_send.at[i], g_recv.at[i, 2], h.one(d))
     scatter_group(0)
     for k in (1, 2):
         project(0, k)
@@ -436,21 +464,10 @@
         settle(ga.at[0, 0], g_recv.at[i, 2])
         project(i, 3)
     pair_group(3)
+    finish_group(0)
     scatter_group(3)
-    second = exp // 4
-    place = mx + second * (my - mx)
-    for k, d in enumerate(hops):
-        settle(rz.at[0, pl.ds(0, 3)], z_recv.at[k])
-        total = rz[k, 0].astype(F32)
-        for j in range(1, 4):
-            total = total + rz[k, j].astype(F32)
-        if d == 0:
-            mo[pl.ds(place, 1)] = total.astype(BF16)[None]
-        else:
-            ms[k - 1] = total.astype(BF16)
-            near_x, near_y = along_x(d)["ctx"], along_y(d)["ctx"]
-            device = {"ctx": near_x + second * (near_y - near_x)}
-            send(ms.at[k - 1], mo.at[place], m_sem.at[0], m_sem.at[1], device)
+    for k in (1, 2, 3):
+        finish_group(k)
     settle(mo.at[pl.ds(0, 3)], m_sem.at[1])
 
     squares = jnp.zeros((16, 1), F32)
@@ -479,6 +496,7 @@
             settle(opg.at[0, pl.ds(0, 3)], o_send.at[i])
             settle(ga.at[0, pl.ds(0, 3)], g_send.at[i])
         settle(parts.at[pl.ds(0, 7)], a_sem.at[0])
+        settle(part_maps.at[pl.ds(0, 7)], a_sem.at[2])
         settle(low_rank.at[pl.ds(0, 7)], b_sem.at[0])
         settle(maps.at[pl.ds(0, 7)], b_sem.at[1])
         for base, (fin, sums) in enumerate(((fin_y, sum_y), (fin_x, sum_x))):

time: 133 us -> 134 us (level)
  Pallas kernels: 131 us -> 133 us
where the time goes in v7:
time: 134 us
  Pallas kernels  133 us (99%)
  local copies, waits for them, and re-layouts  1.57 us (1%)
    pallas_call x1, Pallas kernels, shards(): pl.pallas_call(block_kernel, out_shape=jax.ShapeDtypeStruct((16, 4096), B...  133 us

profile of v7, /device:TPU:1, one launch (start us, length us, event | category | flops | bytes accessed | tf_op | source)
XLA Modules:
  0.0 134.2 jit_solution(17099609317931604907)
XLA Ops:
  0.0 132.6 %shard_map.172 = bf16[16,4096]{1,0:T(8,128)(2,1)} custom-call(bf16[128,1024]{1,0:T(8,128)(2,1)} %refs_0_.1, bf16[128,1024]{1,0:T(8,128)(2,1)} %refs_1_.1, f32[4,1024]{1,0:T(4,128)} %refs_2_.1, f32[1,1024]{1,0:T(1,128)} %bitcast.10, bf16[544,1024]{1,0:T(8,128)(2,1)} %bitcast.7, bf16[512,1024]{1,0:T(8,128)(2,1)} %refs_5_.1, f32[1,1024]{1,0:T(1,128)} %bitcast.11, ...), custom_call_target="tpu_custom_call" | custom-call | flops 13500000256 | bytes 24000000 | tf_op jit(solution)/shard_map/pallas_call | solution.py:843
  132.6 1.6 %copy.20 = bf16[16,4096]{1,0:T(8,128)(2,1)} copy(bf16[16,4096]{1,0:T(8,128)(2,1)} %shard_map.172) | data formatting | bytes 262144

commit v8 on v7

--- a/solution.py
+++ b/solution.py
@@ -69,6 +69,7 @@
 
 
 LOG2E = 1.4426950408889634
+FAR_FIRST = (4, 3, 5, 2, 6, 1, 7)
 
 INPUTS = (
     "mixer_in",
@@ -93,7 +94,7 @@
 
 SCRATCH = dict(
     stream=pltpu.VMEM((16, 4096), F32),
-    result=pltpu.VMEM((16, 4096), BF16),
+    result=pltpu.VMEM((16, 4096), F32),
     e_sem=pltpu.SemaphoreType.DMA((2,)),
     normed=pltpu.VMEM((16, 4096), BF16),
     spread=pltpu.VMEM((3, 128, 16), BF16),
@@ -273,6 +274,10 @@
 
     arrive()
     send(mixer_in.at[pl.ds(112, 16)], rim, h_sem.at[0], h_sem.at[1], ahead)
+    for i, h in enumerate(halves):
+        send(out_proj, opg.at[i, h.q], o_send.at[i], o_recv.at[i, 0], h.two(1))
+        send(out_proj, opg.at[i, h.q], o_send.at[i], o_recv.at[i, 1], h.two(-1))
+        opg[i, pl.ds(h.q, 1)] = out_proj[...][None]
     channel_sums(16, 112)
     settle(rim, h_sem.at[1])
     keep = jnp.where(ctx > 0, 1.0, 0.0).astype(F32)
@@ -280,16 +285,12 @@
     convolve(0, 16)
     channel_sums(0, 16)
 
-    for d in range(1, 8):
+    for d in FAR_FIRST:
         to = lax.rem(exp + d, 8)
         send(part.at[to], parts.at[exp], a_sem.at[0], a_sem.at[1], peer(d))
         send(own_maps.at[to], part_maps.at[exp], a_sem.at[2], a_sem.at[3], peer(d))
     parts[pl.ds(exp, 1)] = part[pl.ds(exp, 1)]
     part_maps[pl.ds(exp, 1)] = own_maps[pl.ds(exp, 1)]
-    for i, h in enumerate(halves):
-        send(out_proj, opg.at[i, h.q], o_send.at[i], o_recv.at[i, 0], h.two(1))
-        send(out_proj, opg.at[i, h.q], o_send.at[i], o_recv.at[i, 1], h.two(-1))
-        opg[i, pl.ds(h.q, 1)] = out_proj[...][None]
     settle(parts.at[pl.ds(0, 7)], a_sem.at[1])
     settle(part_maps.at[pl.ds(0, 7)], a_sem.at[3])
     total, total_maps = parts[0].astype(F32), part_maps[0]
@@ -298,11 +299,17 @@
         total_maps = total_maps + part_maps[j]
     low_rank[pl.ds(exp, 1)] = total.astype(BF16)[None]
     maps[pl.ds(exp, 1)] = total_maps[None]
-    for d in range(1, 8):
+    for d in FAR_FIRST:
         for k, ref in enumerate((low_rank, maps)):
             send(ref.at[exp], ref.at[exp], b_sem.at[k], b_sem.at[2 + k], peer(d))
     settle(low_rank.at[pl.ds(0, 7)], b_sem.at[2])
     settle(maps.at[pl.ds(0, 7)], b_sem.at[3])
+    top, low = pl.ds(0, 512), pl.ds(512, 512)
+    for i, h in enumerate(halves):
+        for k, d, rows in ((0, 1, top), (1, -1, low)):
+            settle(opg.at[0, 0], o_recv.at[i, k])
+            place = opg.at[i, wrap(h.q - d, 4), rows]
+            send(place, place, o_send.at[i], o_recv.at[i, 2], h.two(d))
     scalars = pltpu.make_async_copy(maps, bc_s, l_sem.at[0])
     scalars.start()
     step_low = low_rank[...].reshape(128, 512)
@@ -316,12 +323,6 @@
             step_t[rows, :] = step[:, i * 128 : (i + 1) * 128]
             drive_t[rows, :] = drive[:, i * 128 : (i + 1) * 128]
     scalars.wait()
-    top, low = pl.ds(0, 512), pl.ds(512, 512)
-    for i, h in enumerate(halves):
-        for k, d, rows in ((0, 1, top), (1, -1, low)):
-            settle(opg.at[0, 0], o_recv.at[i, k])
-            place = opg.at[i, wrap(h.q - d, 4), rows]
-            send(place, place, o_send.at[i], o_recv.at[i, 2], h.two(d))
 
     rates = [rate_t[pl.ds(n * 8, 8), :] for n in range(16)]
     zero = jnp.zeros((8, 128), F32)
@@ -550,7 +551,7 @@
     windows = (0, 768, 1280)
 
     def all_to_all(half, into, ss, rs):
-        for d in range(1, 8):
+        for d in FAR_FIRST:
             peer = lax.rem(exp + d, 8)
             src, dst = go.at[half, peer], into.at[half, exp]
             remote(src, dst, ss.at[half], rs.at[half], {"exp": peer}).start()
@@ -755,7 +756,7 @@
                 for k in range(2)
             ]
             mix = gate * pair[0] + (1.0 - gate) * pair[1]
-            result[:, cols] = (stream[:, cols] + mix).astype(BF16)
+            result[:, cols] = stream[:, cols] + mix
         cols = pl.ds(i * 2048, 2048)
         stores.append(pltpu.make_async_copy(result.at[:, cols], out.at[:, cols], e_sem.at[i]))
         stores[i].start()
@@ -840,9 +841,9 @@
                 pick[w, j * 5 + s, j * 16 + w * 5 + s] = 1.0
     vmem = pl.BlockSpec(memory_space=pltpu.VMEM)
     anywhere = pl.BlockSpec(memory_space=pl.ANY)
-    return pl.pallas_call(
+    block = pl.pallas_call(
         block_kernel,
-        out_shape=jax.ShapeDtypeStruct((16, 4096), BF16),
+        out_shape=jax.ShapeDtypeStruct((16, 4096), F32),
         in_specs=[anywhere if name.startswith("w_") else vmem for name in INPUTS],
         out_specs=anywhere,
         scratch_shapes=list(SCRATCH.values()),
@@ -872,6 +873,7 @@
         w_down,
         jnp.asarray(pick, BF16),
     )
+    return block.astype(BF16)
 
 
 def solution(mesh):

time: 134 us -> 133 us (level)
  Pallas kernels: 133 us -> 131 us
  other arithmetic: 0 us -> 1.62 us
  local copies, waits for them, and re-layouts: 1.57 us -> 0 us
    pallas_call x1, Pallas kernels: 133 us -> 131 us  [shards(): pl.pallas_call(block_kernel, out_shape=jax.ShapeDtypeStruct((16, 4096), F...]
    convert_element_type x0 -> x1, other arithmetic: none -> 1.62 us  [shards(): return block.astype(BF16)]
    unnamed x1 -> x0, local copies, waits for them, and re-layouts: 1.57 us -> none
where the time goes in v8:
time: 133 us; the launch traced here: 132 us
  Pallas kernels  131 us (98%)
  other arithmetic  1.62 us (1%)
    pallas_call x1, Pallas kernels, shards(): pl.pallas_call(block_kernel, out_shape=jax.ShapeDtypeStruct((16, 4096), F...  131 us

profile of v8, /device:TPU:1, one launch (start us, length us, event | category | flops | bytes accessed | tf_op | source)
XLA Modules:
  0.0 132.4 jit_solution(17230879746489166924)
XLA Ops:
  0.0 130.8 %shard_map.172 = f32[16,4096]{1,0:T(8,128)} custom-call(bf16[128,1024]{1,0:T(8,128)(2,1)} %refs_0_.1, bf16[128,1024]{1,0:T(8,128)(2,1)} %refs_1_.1, f32[4,1024]{1,0:T(4,128)} %refs_2_.1, f32[1,1024]{1,0:T(1,128)} %bitcast.10, bf16[544,1024]{1,0:T(8,128)(2,1)} %bitcast.7, bf16[512,1024]{1,0:T(8,128)(2,1)} %refs_5_.1, f32[1,1024]{1,0:T(1,128)} %bitcast.11, ...), custom_call_target="tpu_custom_call" | custom-call | flops 13500000256 | bytes 24000000 | tf_op jit(solution)/shard_map/pallas_call | solution.py:844
  130.8 1.6 %convert_element_type.3 = bf16[16,4096]{1,0:T(8,128)(2,1)} convert(f32[16,4096]{1,0:T(8,128)} %shard_map.172) | non-fusion elementwise | flops 65536 | bytes 393216 | tf_op jit(solution)/shard_map/convert_element_type | solution.py:876
